TPU v7x, 32 devices: a whole 2x2x4 slice. The times are simulated.
32 devices in a mesh: seq: 16 (over z, y, x), head: 2 (over core).
Axes of the slice: x: 2, y: 2, z: 4, core: 2. Of those that a mesh axis runs over, the one named last changes fastest.
Arguments:
- layer_input: bfloat16 [2, 8192, 1792], P(None, 'seq', 'head'), may hold values from -6 to 6
- cotangent: bfloat16 [2, 8192, 1792], P(None, 'seq', 'head'), may hold values from -6 to 6
- lengths: int32 [2, 4], replicated, may hold values from 1 to 7808, as said below
- doc_order: int32 [2, 4], replicated, may hold values from 0 to 3, as said below
- norm_gains: bfloat16 [2, 1792], P(None, 'seq'), may hold values from 0.5 to 1.5
- conv_filter: bfloat16 [3, 1792], P(None, 'seq'), may hold values from -3 to 3
- w_query: bfloat16 [1792, 256], P('seq', 'head'), may hold values from -0.125 to 0.125
- w_key: bfloat16 [1792, 256], P('seq', 'head'), may hold values from -0.125 to 0.125
- w_value: bfloat16 [1792, 1792], P('seq', 'head'), may hold values from -0.125 to 0.125
- w_wquery: bfloat16 [1792, 1792], P('seq', 'head'), may hold values from -0.125 to 0.125
- w_wkey: bfloat16 [1792, 1792], P('seq', 'head'), may hold values from -0.125 to 0.125
- w_conv_in: bfloat16 [1792, 1792], P('seq', 'head'), may hold values from -0.125 to 0.125
- w_conv_gate: bfloat16 [1792, 1792], P('seq', 'head'), may hold values from -0.125 to 0.125
- w_out: bfloat16 [1792, 1792], P('head', 'seq'), may hold values from -0.1875 to 0.1875
- w_gate: bfloat16 [1792, 4864], P('seq', 'head'), may hold values from -0.125 to 0.125
- w_up: bfloat16 [1792, 4864], P('seq', 'head'), may hold values from -0.125 to 0.125
- w_down: bfloat16 [4864, 1792], P('head', 'seq'), may hold values from -0.078125 to 0.078125
Outputs:
- output: bfloat16 [2, 8192, 1792], P(None, 'seq', 'head')
- grad_input: bfloat16 [2, 8192, 1792], P(None, 'seq', 'head')
- grad_norm_gains: float32 [2, 1792], P(None, 'seq')
- grad_conv_filter: float32 [3, 1792], P(None, 'seq')
- grad_w_query: float32 [1792, 256], P('seq', 'head')
- grad_w_key: float32 [1792, 256], P('seq', 'head')
- grad_w_value: float32 [1792, 1792], P('seq', 'head')
- grad_w_wquery: float32 [1792, 1792], P('seq', 'head')
- grad_w_wkey: float32 [1792, 1792], P('seq', 'head')
- grad_w_conv_in: float32 [1792, 1792], P('seq', 'head')
- grad_w_conv_gate: float32 [1792, 1792], P('seq', 'head')
- grad_w_out: float32 [1792, 1792], P('head', 'seq')
- grad_w_gate: float32 [1792, 4864], P('seq', 'head')
- grad_w_up: float32 [1792, 4864], P('seq', 'head')
- grad_w_down: float32 [4864, 1792], P('head', 'seq')
Inputs may be any that keep to these rules, and one draw needn't show every extreme that they name: `lengths`: in each row one document has exactly (61) * 128 tokens and each other document 1 to 128, so that the documents fill the 64 tiles. `doc_order`: each row is a permutation of 0 to 3.
All inputs are finite; a program needn't handle non-finite values.
Results may differ from a plain program's by a relative error of at most 0.018.
Values may be sent and summed in bfloat16 or wider, within the bound.
A program may use at most 640 MiB of HBM per device.

v0:
```python
import math

import jax
import jax.numpy as jnp
from jax import lax
from jax.sharding import PartitionSpec as P

FDIM = 16
HDIM = 112
WIN = 64
KCONV = 3
TILE = 128


highest = lax.Precision.HIGHEST


def entering(x, axis, combine, identity, reverse):
    size, mine = (lax.axis_size(axis), lax.axis_index(axis))
    everything = jax.tree.map(
        lambda part, kind: lax.all_gather(part.astype(kind), axis),
        x,
        jax.tree.map(lambda a: jnp.bfloat16 if a.dtype == jnp.float32 else a.dtype, x),
    )
    start = jax.tree.map(
        lambda part, zero: jnp.broadcast_to(jnp.asarray(zero, part.dtype), part.shape), x, identity
    )

    def turn(k, before):
        at = size - 1 - k if reverse else k
        reached = at > mine if reverse else at < mine
        new = combine(
            before, jax.tree.map(lambda part, own: part[at].astype(own.dtype), everything, x)
        )
        return jax.tree.map(lambda a, b: jnp.where(reached, a, b), new, before)

    return lax.fori_loop(0, size, turn, start)


def from_behind(x, axis, by):
    size = lax.axis_size(axis)
    pairs = [(i, i + by) for i in range(size) if 0 <= i + by < size]
    return lax.ppermute(x, axis, pairs)


def shortened(x):
    return jax.tree.map(lambda a: a.astype(jnp.bfloat16) if a.dtype == jnp.float32 else a, x)


def round_value(values):
    return lax.optimization_barrier(values.astype(jnp.bfloat16)).astype(jnp.float32)


def round_keep(values):
    return (round_value(values), None)


def round_pass(kept, grad):
    return (grad,)


def make_low():
    rounding = jax.custom_vjp(round_value)
    rounding.defvjp(round_keep, round_pass)
    return rounding


def low(values):
    return make_low()(values)


def same_value(values):
    return values


def same_keep(values):
    return (values, None)


def grad_round(kept, grad):
    return (low(grad),)


def make_low_back():
    passing = jax.custom_vjp(same_value)
    passing.defvjp(same_keep, grad_round)
    return passing


def low_back(values):
    return make_low_back()(values)


def project(rows, weight):
    return jnp.dot(rows, weight, preferred_element_type=jnp.float32)


def back_prod(grad, weight):
    return lax.dot_general(
        grad, weight, (((1,), (1,)), ((), ())), preferred_element_type=jnp.float32
    )


def outer_sum(left, right):
    return lax.dot_general(
        left, right, (((0,), (0,)), ((), ())), preferred_element_type=jnp.float32
    )


def normalize(values):
    return values * lax.rsqrt(jnp.mean(values * values, axis=-1, keepdims=True) + 1e-05)


def feature_map(entries):
    halved = 0.5 * entries
    squares_map = halved[..., :, None] * halved[..., None, :]
    flattened = squares_map.reshape(entries.shape[:-1] + (entries.shape[-1] * entries.shape[-1],))
    unit_col = jnp.ones(entries.shape[:-1] + (1,), jnp.float32)
    return jnp.concatenate([unit_col, halved, flattened * (1.0 / math.sqrt(2.0))], axis=-1)


def layout(lengths, order, positions, tile_rows):
    count = lengths.shape[0]
    places = jnp.arange(count, dtype=jnp.int32)
    picked = (order[:, None] == places[None, :]).astype(jnp.int32)
    ordered = jnp.sum(picked * lengths[None, :], axis=1, dtype=jnp.int32)
    tiles = (ordered + tile_rows - 1) // tile_rows
    first_tile = jnp.cumsum(tiles, dtype=jnp.int32) - tiles
    row_tile = positions // tile_rows
    doc_slot = (
        jnp.sum(
            (row_tile[:, None] >= first_tile[None, :]).astype(jnp.int32), axis=1, dtype=jnp.int32
        )
        - 1
    )
    chosen = (doc_slot[:, None] == places[None, :]).astype(jnp.int32)
    doc_start = jnp.sum(chosen * first_tile[None, :], axis=1, dtype=jnp.int32) * tile_rows
    doc_length = jnp.sum(chosen * ordered[None, :], axis=1, dtype=jnp.int32)
    is_valid = positions - doc_start < doc_length
    return (doc_slot, doc_start, is_valid)


def linear_out(queries, key_rows, values, state, total, doc_slot, doc_start, is_valid, block_start):
    row_count = queries.shape[0]
    head_count = queries.shape[1] // FDIM
    query_heads = queries.reshape(row_count, head_count, FDIM)
    key_heads = key_rows.reshape(row_count, head_count, FDIM)
    value_heads = values.reshape(row_count, head_count, -1)
    products = 0.25 * jnp.einsum("ihf,jhf->hij", query_heads, key_heads, precision=highest)
    kernel = 1.0 + products + 0.5 * products * products
    row_index = jnp.arange(row_count, dtype=jnp.int32)
    allowed = (
        (row_index[None, :] <= row_index[:, None])
        & (doc_slot[None, :] == doc_slot[:, None])
        & (is_valid[None, :] | (row_index[None, :] == row_index[:, None]))
    )
    weights = jnp.where(allowed[None], kernel, 0.0)
    numer = jnp.einsum("hij,jhd->ihd", low(weights), value_heads, precision=highest)
    denom = jnp.sum(weights, axis=2).T
    carried = (doc_start < block_start).astype(jnp.float32)
    mapped = low(feature_map(query_heads))
    numer = numer + carried[:, None, None] * jnp.einsum(
        "ihp,hpd->ihd", mapped, state, precision=highest
    )
    denom = denom + carried[:, None] * jnp.einsum("ihp,hp->ih", mapped, total, precision=highest)
    return (numer / denom[:, :, None]).reshape(row_count, -1)


def linear_own(key_rows, values, doc_slot, is_valid):
    row_count = key_rows.shape[0]
    head_count = key_rows.shape[1] // FDIM
    key_heads = key_rows.reshape(row_count, head_count, FDIM)
    value_heads = values.reshape(row_count, head_count, -1)
    last_doc = ((doc_slot == doc_slot[row_count - 1]) & is_valid).astype(jnp.float32)
    mapped = low(feature_map(key_heads)) * last_doc[:, None, None]
    state = jnp.einsum("jhp,jhd->hpd", mapped, value_heads, precision=highest)
    total = jnp.sum(mapped, axis=0)
    return (state, total)


def window_out(queries, doc_slot, positions, key_rows, values, key_slot, key_valid, key_place):
    row_count = queries.shape[0]
    head_count = queries.shape[1] // HDIM
    query_heads = queries.reshape(row_count, head_count, HDIM)
    key_heads = key_rows.reshape(-1, head_count, HDIM)
    value_heads = values.reshape(-1, head_count, HDIM)
    scores = jnp.einsum("ihd,jhd->hij", query_heads, key_heads, precision=highest) * (
        1.0 / math.sqrt(HDIM)
    )
    distance = positions[:, None] - key_place[None, :]
    allowed = (
        (distance >= 0)
        & (distance <= WIN)
        & (doc_slot[:, None] == key_slot[None, :])
        & (key_valid[None, :] | (distance == 0))
    )
    scores = jnp.where(allowed[None], scores, -1e30)
    row_max = jnp.max(scores, axis=2, keepdims=True)
    exponent = jnp.exp(scores - row_max)
    weights_soft = low(exponent / jnp.sum(exponent, axis=2, keepdims=True))
    return jnp.einsum("hij,jhd->ihd", weights_soft, value_heads, precision=highest).reshape(
        row_count, -1
    )


def conv_mix(normed_before, normed, taps, slot_before, doc_slot):
    row_count = normed.shape[0]
    stacked = jnp.concatenate([normed_before, normed], axis=0)
    slot_stack = jnp.concatenate([slot_before, doc_slot], axis=0)
    result = taps[0] * normed
    for shift_by in range(1, KCONV):
        first_row = KCONV - 1 - shift_by
        earlier = stacked[first_row : first_row + row_count]
        same_doc = (slot_stack[first_row : first_row + row_count] == doc_slot).astype(jnp.float32)[
            :, None
        ]
        result = result + taps[shift_by] * earlier * same_doc
    return result


def chain(earlier, later):
    keep = 1.0 - later[2]
    return (
        later[0] + keep * earlier[0],
        later[1] + keep * earlier[1],
        jnp.maximum(earlier[2], later[2]),
    )


def fetch_weights(shards):
    gathered = (
        lax.all_gather(shards[0], "seq", axis=1, tiled=True),
        lax.all_gather(shards[1], "seq", axis=1, tiled=True),
        lax.all_gather(shards[2], "seq", axis=0, tiled=True),
        lax.all_gather(shards[3], "seq", axis=0, tiled=True),
        lax.all_gather(shards[4], "seq", axis=0, tiled=True),
        lax.all_gather(shards[5], "seq", axis=0, tiled=True),
        lax.all_gather(shards[6], "seq", axis=0, tiled=True),
        lax.all_gather(shards[7], "seq", axis=0, tiled=True),
        lax.all_gather(shards[8], "seq", axis=0, tiled=True),
        lax.all_gather(shards[9], "seq", axis=1, tiled=True),
        lax.all_gather(shards[10], "seq", axis=0, tiled=True),
        lax.all_gather(shards[11], "seq", axis=0, tiled=True),
        lax.all_gather(shards[12], "seq", axis=1, tiled=True),
    )
    return (gathered[0].astype(jnp.float32), gathered[1].astype(jnp.float32)) + tuple(gathered[2:])


def reduce_grads(grads):
    return (
        lax.psum_scatter(grads[0], "seq", scatter_dimension=1, tiled=True),
        lax.psum_scatter(grads[1], "seq", scatter_dimension=1, tiled=True),
        lax.psum_scatter(grads[2], "seq", scatter_dimension=0, tiled=True),
        lax.psum_scatter(grads[3], "seq", scatter_dimension=0, tiled=True),
        lax.psum_scatter(grads[4], "seq", scatter_dimension=0, tiled=True),
        lax.psum_scatter(grads[5], "seq", scatter_dimension=0, tiled=True),
        lax.psum_scatter(grads[6], "seq", scatter_dimension=0, tiled=True),
        lax.psum_scatter(grads[7], "seq", scatter_dimension=0, tiled=True),
        lax.psum_scatter(grads[8], "seq", scatter_dimension=0, tiled=True),
        lax.psum_scatter(grads[9], "seq", scatter_dimension=1, tiled=True),
        lax.psum_scatter(grads[10], "seq", scatter_dimension=0, tiled=True),
        lax.psum_scatter(grads[11], "seq", scatter_dimension=0, tiled=True),
        lax.psum_scatter(grads[12], "seq", scatter_dimension=1, tiled=True),
    )


def pad_tail(rows_part, row_count):
    return jnp.pad(rows_part, ((row_count - rows_part.shape[0], 0), (0, 0)))


def first_norm(input_rows, gain_rows):
    return low(normalize(input_rows) * gain_rows[0])


def second_norm(resid, gain_rows):
    return low(normalize(resid) * gain_rows[1])


def activate(gate, up_rows):
    return jax.nn.silu(gate) * up_rows


def per_device(
    layer_input,
    cotangent,
    lengths,
    doc_order,
    norm_gains,
    conv_filter,
    w_query,
    w_key,
    w_value,
    w_wquery,
    w_wkey,
    w_conv_in,
    w_conv_gate,
    w_out,
    w_gate,
    w_up,
    w_down,
):
    row_count = layer_input.shape[1]
    half_width = layer_input.shape[2]
    place = lax.axis_index("seq") * row_count
    head_place = lax.axis_index("head") * half_width
    positions = place + jnp.arange(row_count, dtype=jnp.int32)
    window_place = place - WIN + jnp.arange(WIN, dtype=jnp.int32)
    conv_place = place - (KCONV - 1) + jnp.arange(KCONV - 1, dtype=jnp.int32)
    shards = (
        norm_gains,
        conv_filter,
        w_query,
        w_key,
        w_value,
        w_wquery,
        w_wkey,
        w_conv_in,
        w_conv_gate,
        w_out,
        w_gate,
        w_up,
        w_down,
    )
    weights_full = None
    summed = None
    results = []
    grads_in = []
    for micro in range(layer_input.shape[0]):
        weights_full = fetch_weights(shards)
        (
            gains,
            taps,
            wq_full,
            wk_full,
            wv_full,
            wwq_full,
            wwk_full,
            wc1_full,
            wc2_full,
            wo_full,
            wg_full,
            wu_full,
            wd_full,
        ) = weights_full
        doc_slot, doc_start, is_valid = layout(lengths[micro], doc_order[micro], positions, TILE)
        window_slot, _, window_valid = layout(lengths[micro], doc_order[micro], window_place, TILE)
        conv_slot, _, _ = layout(lengths[micro], doc_order[micro], conv_place, TILE)
        reset = (doc_start[row_count - 1] >= place).astype(jnp.float32)

        def section_own(key_rows, values):
            return linear_own(key_rows, values, doc_slot, is_valid)

        def section_conv(normed, normed_prev, taps_rows):
            return low(conv_mix(normed_prev, normed, taps_rows, conv_slot, doc_slot))

        def section_mix(
            queries,
            key_rows,
            values,
            wqueries,
            wkeys,
            wkeys_prev,
            values_prev,
            conv_in,
            conv_gate,
            state,
            total,
        ):
            conv_out = low_back(conv_in) * low_back(conv_gate)
            linear = linear_out(
                queries, key_rows, values, state, total, doc_slot, doc_start, is_valid, place
            )
            window = window_out(
                wqueries,
                doc_slot,
                positions,
                jnp.concatenate([wkeys_prev, wkeys], axis=0),
                jnp.concatenate([values_prev, values], axis=0),
                jnp.concatenate([window_slot, doc_slot], axis=0),
                jnp.concatenate([window_valid, is_valid], axis=0),
                jnp.concatenate([window_place, positions], axis=0),
            )
            return low_back(low(linear + window + conv_out))

        input_full = lax.all_gather(layer_input[micro], "head", axis=1, tiled=True).astype(
            jnp.float32
        )
        normed, pull_norm1 = jax.vjp(first_norm, input_full, gains)
        normed_low = normed.astype(jnp.bfloat16)
        queries_low = project(normed_low, wq_full).astype(jnp.bfloat16)
        keys_low = project(normed_low, wk_full).astype(jnp.bfloat16)
        values_low = project(normed_low, wv_full).astype(jnp.bfloat16)
        wqueries_low = project(normed_low, wwq_full).astype(jnp.bfloat16)
        wkeys_low = project(normed_low, wwk_full).astype(jnp.bfloat16)
        conv_gate = project(normed_low, wc2_full)
        keys_f = keys_low.astype(jnp.float32)
        values_f = values_low.astype(jnp.float32)
        own_out, pull_own = jax.vjp(section_own, keys_f, values_f)
        identity = (
            jnp.zeros_like(own_out[0]),
            jnp.zeros_like(own_out[1]),
            jnp.zeros((), jnp.float32),
        )
        prefix = entering((own_out[0], own_out[1], reset), "seq", chain, identity, False)
        width = wkeys_low.shape[1]
        cut_size = WIN * width
        tail = jnp.concatenate(
            [
                wkeys_low[row_count - WIN :].reshape(-1),
                values_low[row_count - WIN :].reshape(-1),
                normed_low[row_count - (KCONV - 1) :].reshape(-1),
            ]
        )
        arrived = from_behind(tail, "seq", 1).astype(jnp.float32)
        wkeys_prev = arrived[:cut_size].reshape(WIN, width)
        values_prev = arrived[cut_size : 2 * cut_size].reshape(WIN, width)
        normed_prev = arrived[2 * cut_size :].reshape(KCONV - 1, normed.shape[1])
        conv, pull_conv = jax.vjp(section_conv, normed, normed_prev, taps)
        conv_low = conv.astype(jnp.bfloat16)
        conv_in = project(conv_low, wc1_full)
        mixed, pull_mix = jax.vjp(
            section_mix,
            queries_low.astype(jnp.float32),
            keys_f,
            values_f,
            wqueries_low.astype(jnp.float32),
            wkeys_low.astype(jnp.float32),
            wkeys_prev,
            values_prev,
            conv_in,
            conv_gate,
            prefix[0],
            prefix[1],
        )
        mixed_low = mixed.astype(jnp.bfloat16)
        mix_part = project(mixed_low, wo_full)
        mixed_sum = lax.psum(mix_part.astype(jnp.bfloat16), "head").astype(jnp.float32)
        resid_full = input_full + mixed_sum
        second, pull_norm2 = jax.vjp(second_norm, resid_full, gains)
        second_low = second.astype(jnp.bfloat16)
        gate = project(second_low, wg_full)
        up_rows = project(second_low, wu_full)
        hidden, pull_act = jax.vjp(activate, gate, up_rows)
        hidden_low = hidden.astype(jnp.bfloat16)
        ffn_part = project(hidden_low, wd_full)
        ffn_half = lax.psum_scatter(
            ffn_part.astype(jnp.bfloat16), "head", scatter_dimension=1, tiled=True
        ).astype(jnp.float32)
        resid_half = lax.dynamic_slice_in_dim(resid_full, head_place, half_width, 1)
        results.append((resid_half + ffn_half).astype(jnp.bfloat16))
        cot_low = lax.all_gather(cotangent[micro], "head", axis=1, tiled=True)
        cot_full = cot_low.astype(jnp.float32)
        d_hidden = back_prod(cot_low, wd_full)
        d_gate_f, d_up_f = pull_act(d_hidden)
        d_gate = d_gate_f.astype(jnp.bfloat16)
        d_up = d_up_f.astype(jnp.bfloat16)
        d_second = back_prod(d_gate, wg_full) + back_prod(d_up, wu_full)
        d_resid_part, d_gains_ffn = pull_norm2(d_second)
        grad_down = outer_sum(hidden_low, cot_low)
        grad_gate = outer_sum(second_low, d_gate)
        grad_up = outer_sum(second_low, d_up)
        d_resid_sum, d_gains_back = (
            lax.psum(d_resid_part.astype(jnp.bfloat16), "head").astype(jnp.float32),
            lax.psum(d_gains_ffn.astype(jnp.bfloat16), "head").astype(jnp.float32),
        )
        d_resid = cot_full + d_resid_sum
        out_f = wo_full.astype(jnp.float32)
        d_mixed = lax.dot_general(
            d_resid,
            out_f,
            (((1,), (1,)), ((), ())),
            precision=highest,
            preferred_element_type=jnp.float32,
        )
        grad_out = lax.dot_general(
            mixed,
            d_resid,
            (((0,), (0,)), ((), ())),
            precision=highest,
            preferred_element_type=jnp.float32,
        )
        (
            d_q_part,
            d_k_part,
            d_v_part,
            d_wq_part,
            d_wk_part,
            d_wk_prev,
            d_v_prev,
            d_conv_in,
            d_conv_gate,
            d_state,
            d_total,
        ) = pull_mix(d_mixed)
        own_grads = entering((d_state, d_total, reset), "seq", chain, identity, True)
        d_keys_own, d_values_own = pull_own((own_grads[0], own_grads[1]))
        d_conv_in_low = d_conv_in.astype(jnp.bfloat16)
        d_conv_gate_low = d_conv_gate.astype(jnp.bfloat16)
        d_conv = back_prod(d_conv_in_low, wc1_full)
        grad_conv_in = outer_sum(conv_low, d_conv_in_low)
        d_normed_conv, d_normed_prev, d_taps = pull_conv(d_conv)
        back_rows = jnp.concatenate(
            [d_wk_prev.reshape(-1), d_v_prev.reshape(-1), d_normed_prev.reshape(-1)]
        )
        returned = from_behind(shortened(back_rows), "seq", -1).astype(back_rows.dtype)
        d_queries = d_q_part.astype(jnp.bfloat16)
        d_keys = (d_k_part + d_keys_own).astype(jnp.bfloat16)
        d_values = (
            d_v_part
            + d_values_own
            + pad_tail(returned[cut_size : 2 * cut_size].reshape(WIN, width), row_count)
        ).astype(jnp.bfloat16)
        d_wqueries = d_wq_part.astype(jnp.bfloat16)
        d_wkeys = (d_wk_part + pad_tail(returned[:cut_size].reshape(WIN, width), row_count)).astype(
            jnp.bfloat16
        )
        d_normed = d_normed_conv + pad_tail(
            returned[2 * cut_size :].reshape(KCONV - 1, normed.shape[1]), row_count
        )
        d_normed = (
            d_normed
            + back_prod(d_queries, wq_full)
            + back_prod(d_keys, wk_full)
            + back_prod(d_values, wv_full)
        )
        d_normed = (
            d_normed
            + back_prod(d_wqueries, wwq_full)
            + back_prod(d_wkeys, wwk_full)
            + back_prod(d_conv_gate_low, wc2_full)
        )
        grad_query = outer_sum(normed_low, d_queries)
        grad_key = outer_sum(normed_low, d_keys)
        grad_value = outer_sum(normed_low, d_values)
        grad_wquery = outer_sum(normed_low, d_wqueries)
        grad_wkey = outer_sum(normed_low, d_wkeys)
        grad_conv_gate = outer_sum(normed_low, d_conv_gate_low)
        d_input_part, d_gains_front = pull_norm1(d_normed)
        d_input_sum, d_gains_sum, d_taps_sum = (
            lax.psum(d_input_part.astype(jnp.bfloat16), "head").astype(jnp.float32),
            lax.psum(d_gains_front.astype(jnp.bfloat16), "head").astype(jnp.float32),
            lax.psum(d_taps.astype(jnp.bfloat16), "head").astype(jnp.float32),
        )
        d_input_full = d_resid + d_input_sum
        grads_in.append(
            lax.dynamic_slice_in_dim(d_input_full, head_place, half_width, 1).astype(jnp.bfloat16)
        )
        grads = (
            d_gains_back + d_gains_sum,
            d_taps_sum,
            grad_query,
            grad_key,
            grad_value,
            grad_wquery,
            grad_wkey,
            grad_conv_in,
            grad_conv_gate,
            grad_out,
            grad_gate,
            grad_up,
            grad_down,
        )
        reduced = reduce_grads(grads)
        summed = (
            reduced
            if summed is None
            else tuple((running + extra for running, extra in zip(summed, reduced)))
        )
    return (jnp.stack(results), jnp.stack(grads_in)) + tuple(summed)


def solution(mesh):
    in_specs = (
        P(None, "seq", "head"),
        P(None, "seq", "head"),
        P(),
        P(),
        P(None, "seq"),
        P(None, "seq"),
        P("seq", "head"),
        P("seq", "head"),
        P("seq", "head"),
        P("seq", "head"),
        P("seq", "head"),
        P("seq", "head"),
        P("seq", "head"),
        P("head", "seq"),
        P("seq", "head"),
        P("seq", "head"),
        P("head", "seq"),
    )
    out_specs = (
        P(None, "seq", "head"),
        P(None, "seq", "head"),
        P(None, "seq"),
        P(None, "seq"),
        P("seq", "head"),
        P("seq", "head"),
        P("seq", "head"),
        P("seq", "head"),
        P("seq", "head"),
        P("seq", "head"),
        P("seq", "head"),
        P("head", "seq"),
        P("seq", "head"),
        P("seq", "head"),
        P("head", "seq"),
    )
    return jax.shard_map(
        per_device, mesh=mesh, in_specs=in_specs, out_specs=out_specs, check_vma=False
    )
```

profile of v0, /device:TPU:0, one launch (start us, length us, event | category | flops | bytes accessed | tf_op | source)
XLA Modules:
  0.0 4187.1 jit_solution(11610880285939903447)
XLA Ops:
  15.9 42.2 %all-gather.12 = bf16[16,112,2]{1,2,0:T(2,128)(2,1)S(1)} all-gather(bf16[1,112,2]{1,2,0:T(2,128)(2,1)S(1)} %bitcast.663), channel_id=1, replica_groups=mesh['seq'=16,'head'=2] {'seq'}, dimensions={0}, use_global_device_ids=true | all-gather | bytes 7616 | tf_op jit(solution)/shard_map/all_gather | solution.py:232
  60.6 40.1 all_gather.127
  100.6 41.7 all_gather.128
  202.8 35.7 all-gather.13
  241.5 39.6 all-reduce.22
  297.5 39.6 all-gather.2
  337.1 41.0 all-gather.5
  521.9 55.5 %while.69 = (s32[]{:T(128)}, f32[8,273,112]{2,1,0:T(8,128)S(1)}, f32[8,273]{1,0:T(8,128)S(1)}, s32[]{:T(128)}, bf16[16,8,273,112]{3,1,0,2:T(8,128)(2,1)}, /*inde...) while((s32[]{:T(128)}, f32[8,273,112]{2,1,0:T(8,128)S(1)}, ...), condition=%wide.region_27.28_spmd.clone, body=%wide.region_26.27_spmd.clone.sunk | while | flops 1233965 | bytes 3446517 | solution.py:37
  577.4 60.9 %all-gather.52.cloned.1.call-done = bf16[128,273,112]{2,0,1:T(8,128)(2,1)} async-done(((bf16[8,273,112]{2,0,1:T(8,128)(2,1)}), bf16[128,273,112]{2,0,1:T(8,128)(2,1)}) %all-gather.52.cloned.1.call-update) | async-done | bytes 7827472 | tf_op jit(solution)/shard_map/all_gather | solution.py:21
  638.3 55.9 %while.68 = (s32[]{:T(128)}, f32[8,273,112]{2,1,0:T(8,128)S(1)}, f32[8,273]{1,0:T(8,128)S(1)}, s32[]{:T(128)}, bf16[16,8,273,112]{3,1,0,2:T(8,128)(2,1)}, /*inde...) while((s32[]{:T(128)}, f32[8,273,112]{2,1,0:T(8,128)S(1)}, ...), condition=%wide.region_8.9_spmd.clone, body=%wide.region_7.8_spmd.clone.sunk | while | flops 1233965 | bytes 3446517 | solution.py:37
  735.2 42.5 %all-gather.42.cloned.1.call-done = bf16[896,1792]{0,1:T(8,128)(2,1)} async-done(((bf16[896,112]{0,1:T(8,128)(2,1)}), bf16[896,1792]{0,1:T(8,128)(2,1)}) %all-gather.42.cloned.1.call-update) | async-done | bytes 3211280 | tf_op jit(solution)/shard_map/all_gather | solution.py:241
  814.9 114.9 %all-gather.46.cloned.1.call-done = bf16[1792,2432]{1,0:T(8,128)(2,1)} async-done(((bf16[112,2432]{1,0:T(8,128)(2,1)}), bf16[1792,2432]{1,0:T(8,128)(2,1)}) %all-gather.46.cloned.1.call-update) | async-done | bytes 8716304 | tf_op jit(solution)/shard_map/all_gather | solution.py:243
  941.0 106.0 %all-gather.44.cloned.1.call-done = bf16[1792,2432]{1,0:T(8,128)(2,1)} async-done(((bf16[112,2432]{1,0:T(8,128)(2,1)}), bf16[1792,2432]{1,0:T(8,128)(2,1)}) %all-gather.44.cloned.1.call-update) | async-done | bytes 8716304 | tf_op jit(solution)/shard_map/all_gather | solution.py:242
  1058.1 118.8 %all-gather.48.cloned.1.call-done = bf16[2432,1792]{0,1:T(8,128)(2,1)} async-done(((bf16[2432,112]{0,1:T(8,128)(2,1)}), bf16[2432,1792]{0,1:T(8,128)(2,1)}) %all-gather.48.cloned.1.call-update) | async-done | bytes 8716304 | tf_op jit(solution)/shard_map/all_gather | solution.py:244
  1271.6 22.4 all-reduce.33.cloned.1.call-done
  1471.5 44.8 %all-gather.11 = bf16[128,273]{1,0:T(8,128)(2,1)} all-gather(bf16[8,273]{1,0:T(8,128)(2,1)S(1)} %bitcast.661), channel_id=13, replica_groups=mesh['seq'=16,'head'=2] {'seq'}, dimensions={0}, use_global_device_ids=true | all-gather | bytes 74256 | tf_op jit(solution)/shard_map/all_gather | solution.py:21
  1538.8 17.5 fusion.11
  1567.0 17.7 fusion.9
  1645.1 39.6 all-gather.8
  1698.4 55.5 %while.71 = (s32[]{:T(128)}, f32[8,273,112]{2,1,0:T(8,128)S(1)}, f32[8,273]{1,0:T(8,128)S(1)}, s32[]{:T(128)}, bf16[16,8,273,112]{3,1,0,2:T(8,128)(2,1)}, /*inde...) while((s32[]{:T(128)}, f32[8,273,112]{2,1,0:T(8,128)S(1)}, ...), condition=%wide.region_61.62_spmd.clone, body=%wide.region_60.61_spmd.clone.sunk | while | flops 1233969 | bytes 3446579 | solution.py:37
  1770.4 44.9 %while.70 = (s32[]{:T(128)}, f32[8,273,112]{2,1,0:T(8,128)S(1)}, f32[8,273]{1,0:T(8,128)S(1)}, s32[]{:T(128)}, bf16[16,8,273,112]{3,1,0,2:T(8,128)(2,1)}, /*inde...) while((s32[]{:T(128)}, f32[8,273,112]{2,1,0:T(8,128)S(1)}, ...), condition=%wide.region_47.48_spmd.clone, body=%wide.region_46.47_spmd.clone.sunk | while | flops 1233969 | bytes 3446579 | solution.py:37
  2074.0 73.8 %reduce-scatter.24.cloned.1.call-done = f32[112,128]{1,0:T(8,128)} async-done(((f32[1792,128]{1,0:T(8,128)}), f32[112,128]{1,0:T(8,128)}) %reduce-scatter.24.cloned.1.call-update) | async-done | bytes 57360 | tf_op jit(solution)/shard_map/reduce_scatter | solution.py:253
  2147.8 138.2 %reduce-scatter.38.cloned.1.call-done = f32[896,112]{0,1:T(8,128)} async-done(((f32[896,1792]{0,1:T(8,128)}), f32[896,112]{0,1:T(8,128)}) %reduce-scatter.38.cloned.1.call-update) | async-done | bytes 401424 | tf_op jit(solution)/shard_map/reduce_scatter | solution.py:260
  2286.0 142.9 %reduce-scatter.34.cloned.1.call-done = f32[112,896]{1,0:T(8,128)} async-done(((f32[1792,896]{1,0:T(8,128)}), f32[112,896]{1,0:T(8,128)}) %reduce-scatter.34.cloned.1.call-update) | async-done | bytes 401424 | tf_op jit(solution)/shard_map/reduce_scatter | solution.py:258
  2428.9 143.6 %reduce-scatter.36.cloned.1.call-done = f32[112,896]{1,0:T(8,128)} async-done(((f32[1792,896]{1,0:T(8,128)}), f32[112,896]{1,0:T(8,128)}) %reduce-scatter.36.cloned.1.call-update) | async-done | bytes 401424 | tf_op jit(solution)/shard_map/reduce_scatter | solution.py:259
  2572.5 143.6 %reduce-scatter.30.cloned.1.call-done = f32[112,896]{1,0:T(8,128)} async-done(((f32[1792,896]{1,0:T(8,128)}), f32[112,896]{1,0:T(8,128)}) %reduce-scatter.30.cloned.1.call-update) | async-done | bytes 401424 | tf_op jit(solution)/shard_map/reduce_scatter | solution.py:256
  2716.1 143.4 %reduce-scatter.32.cloned.1.call-done = f32[112,896]{1,0:T(8,128)} async-done(((f32[1792,896]{1,0:T(8,128)}), f32[112,896]{1,0:T(8,128)}) %reduce-scatter.32.cloned.1.call-update) | async-done | bytes 401424 | tf_op jit(solution)/shard_map/reduce_scatter | solution.py:257
  2859.5 82.0 %reduce-scatter.26.cloned.1.call-done = f32[112,128]{1,0:T(8,128)} async-done(((f32[1792,128]{1,0:T(8,128)}), f32[112,128]{1,0:T(8,128)}) %reduce-scatter.26.cloned.1.call-update) | async-done | bytes 57360 | tf_op jit(solution)/shard_map/reduce_scatter | solution.py:254
  2941.6 138.3 %reduce-scatter.28.cloned.1.call-done = f32[112,896]{1,0:T(8,128)} async-done(((f32[1792,896]{1,0:T(8,128)}), f32[112,896]{1,0:T(8,128)}) %reduce-scatter.28.cloned.1.call-update) | async-done | bytes 401424 | tf_op jit(solution)/shard_map/reduce_scatter | solution.py:255
  3079.9 363.8 %reduce-scatter.44.cloned.1.call-done = f32[2432,112]{0,1:T(8,128)} async-done(((f32[2432,1792]{0,1:T(8,128)}), f32[2432,112]{0,1:T(8,128)}) %reduce-scatter.44.cloned.1.call-update) | async-done | bytes 1089552 | tf_op jit(solution)/shard_map/reduce_scatter | solution.py:263
  3443.7 368.3 %reduce-scatter.42.cloned.1.call-done = f32[112,2432]{1,0:T(8,128)} async-done(((f32[1792,2432]{1,0:T(8,128)}), f32[112,2432]{1,0:T(8,128)}) %reduce-scatter.42.cloned.1.call-update) | async-done | bytes 1089552 | tf_op jit(solution)/shard_map/reduce_scatter | solution.py:262
  3811.9 368.3 %reduce-scatter.40.cloned.1.call-done = f32[112,2432]{1,0:T(8,128)} async-done(((f32[1792,2432]{1,0:T(8,128)}), f32[112,2432]{1,0:T(8,128)}) %reduce-scatter.40.cloned.1.call-update) | async-done | bytes 1089552 | tf_op jit(solution)/shard_map/reduce_scatter | solution.py:261
  (1252 shorter events, 1152.0 us)
Async XLA Ops:
  10.9 155.9 %all-gather.32.cloned.1.call-start = ((), (), s32[]{:S(2)}) async-start(), calls=%async_computation.15 | async-start | bytes 3411968 | tf_op jit(solution)/shard_map/all_gather | solution.py:236
  11.6 382.6 %all-gather.36.cloned.1.call-start = ((), (), s32[]{:S(2)}) async-start(), calls=%async_computation.17 | async-start | bytes 3411968 | tf_op jit(solution)/shard_map/all_gather | solution.py:237
  12.2 396.8 %all-gather.34.cloned.1.call-start = ((), (), s32[]{:S(2)}) async-start(), calls=%async_computation.16 | async-start | bytes 3411968 | tf_op jit(solution)/shard_map/all_gather | solution.py:238
  12.8 423.7 %all-gather.40.cloned.1.call-start = ((), (), s32[]{:S(2)}) async-start(), calls=%async_computation.19 | async-start | bytes 3411968 | tf_op jit(solution)/shard_map/all_gather | solution.py:240
  13.4 508.5 %all-gather.56.cloned.1.call-start = ((), (), s32[]{:S(2)}) async-start(), calls=%async_computation.27 | async-start | bytes 9504768 | tf_op jit(solution)/shard_map/all_gather | solution.py:21
  179.1 459.2 %all-gather.52.cloned.1.call-start = ((), (), s32[]{:S(2)}) async-start(), calls=%async_computation.25 | async-start | bytes 9504768 | tf_op jit(solution)/shard_map/all_gather | solution.py:21
  194.1 514.1 %all-gather.38.cloned.1.call-start = ((), (), s32[]{:S(2)}) async-start(), calls=%async_computation.18 | async-start | bytes 3411968 | tf_op jit(solution)/shard_map/all_gather | solution.py:239
  194.9 582.9 %all-gather.42.cloned.1.call-start = ((), (), s32[]{:S(2)}) async-start(), calls=%async_computation.20 | async-start | bytes 3411968 | tf_op jit(solution)/shard_map/all_gather | solution.py:241
  195.5 614.2 %all-reduce.35.cloned.1.call-start = ((), (), s32[]{:S(2)}) async-start(), calls=%async_computation.49 | async-start | bytes 7340032 | tf_op jit(solution)/shard_map/psum | solution.py:437
  787.4 259.6 %all-gather.44.cloned.1.call-start = ((), (), s32[]{:S(2)}) async-start(), calls=%async_computation.21 | async-start | bytes 9261056 | tf_op jit(solution)/shard_map/all_gather | solution.py:242
  788.1 270.0 %all-gather.58.cloned.1.call-start = ((), (), s32[]{:S(2)}) async-start(), calls=%async_computation.28 | async-start | bytes 2752512 | tf_op jit(solution)/shard_map/all_gather | solution.py:451
  791.1 385.8 %all-gather.48.cloned.1.call-start = ((), (), s32[]{:S(2)}) async-start(), calls=%async_computation.23 | async-start | bytes 9261056 | tf_op jit(solution)/shard_map/all_gather | solution.py:244
  791.7 443.7 %all-gather.62.cloned.1.call-start = ((), (), s32[]{:S(2)}) async-start(), calls=%async_computation.30 | async-start | bytes 2752512 | tf_op jit(solution)/shard_map/all_gather | solution.py:451
  792.3 501.7 %all-reduce.33.cloned.1.call-start = ((), (), s32[]{:S(2)}) async-start(), calls=%async_computation.48 | async-start | bytes 7340032 | tf_op jit(solution)/shard_map/psum | solution.py:463
  1271.6 426.8 %all-gather.64.cloned.1.call-start = ((), (), s32[]{:S(2)}) async-start(), calls=%async_computation.31 | async-start | bytes 9504768 | tf_op jit(solution)/shard_map/all_gather | solution.py:21
  1308.9 461.5 %all-gather.60.cloned.1.call-start = ((), (), s32[]{:S(2)}) async-start(), calls=%async_computation.29 | async-start | bytes 9504768 | tf_op jit(solution)/shard_map/all_gather | solution.py:21
  1323.9 727.2 %reduce-scatter.46.cloned.1.call-start = ((), (), s32[]{:S(2)}) async-start(), calls=%async_computation.43 | async-start | bytes 2752512
  1338.6 714.0 %reduce-scatter.48.cloned.1.call-start = ((), (), s32[]{:S(2)}) async-start(), calls=%async_computation.44 | async-start | bytes 2752512
  1353.8 711.7 %reduce-scatter.50.cloned.1.call-start = ((), (), s32[]{:S(2)}) async-start(), calls=%async_computation.45 | async-start | bytes 974848
  1893.4 173.5 %reduce-scatter.52.cloned.1.call-start = ((), (), s32[]{:S(2)}) async-start(), calls=%async_computation.46 | async-start | bytes 974848
  1894.8 173.6 %all-reduce.31.cloned.1.call-start = ((), (), s32[]{:S(2)}) async-start(), calls=%async_computation.47 | async-start | bytes 7340032 | tf_op jit(solution)/shard_map/psum | solution.py:540
  1901.2 246.6 %reduce-scatter.24.cloned.1.call-start = ((), (), s32[]{:S(2)}) async-start(), calls=%async_computation.32 | async-start | bytes 974848 | tf_op jit(solution)/shard_map/reduce_scatter | solution.py:253
  1905.1 380.9 %reduce-scatter.38.cloned.1.call-start = ((), (), s32[]{:S(2)}) async-start(), calls=%async_computation.39 | async-start | bytes 6823936 | tf_op jit(solution)/shard_map/reduce_scatter | solution.py:260
  1922.4 506.5 %reduce-scatter.34.cloned.1.call-start = ((), (), s32[]{:S(2)}) async-start(), calls=%async_computation.37 | async-start | bytes 6823936 | tf_op jit(solution)/shard_map/reduce_scatter | solution.py:258
  1931.4 641.1 %reduce-scatter.36.cloned.1.call-start = ((), (), s32[]{:S(2)}) async-start(), calls=%async_computation.38 | async-start | bytes 6823936 | tf_op jit(solution)/shard_map/reduce_scatter | solution.py:259
  1940.1 776.0 %reduce-scatter.30.cloned.1.call-start = ((), (), s32[]{:S(2)}) async-start(), calls=%async_computation.35 | async-start | bytes 6823936 | tf_op jit(solution)/shard_map/reduce_scatter | solution.py:256
  1949.3 910.2 %reduce-scatter.32.cloned.1.call-start = ((), (), s32[]{:S(2)}) async-start(), calls=%async_computation.36 | async-start | bytes 6823936 | tf_op jit(solution)/shard_map/reduce_scatter | solution.py:257
  1959.6 982.0 %reduce-scatter.26.cloned.1.call-start = ((), (), s32[]{:S(2)}) async-start(), calls=%async_computation.33 | async-start | bytes 974848 | tf_op jit(solution)/shard_map/reduce_scatter | solution.py:254
  1963.6 1116.3 %reduce-scatter.28.cloned.1.call-start = ((), (), s32[]{:S(2)}) async-start(), calls=%async_computation.34 | async-start | bytes 6823936 | tf_op jit(solution)/shard_map/reduce_scatter | solution.py:255
  1973.1 1470.6 %reduce-scatter.44.cloned.1.call-start = ((), (), s32[]{:S(2)}) async-start(), calls=%async_computation.42 | async-start | bytes 18522112 | tf_op jit(solution)/shard_map/reduce_scatter | solution.py:263
  1998.6 1813.3 %reduce-scatter.42.cloned.1.call-start = ((), (), s32[]{:S(2)}) async-start(), calls=%async_computation.41 | async-start | bytes 18522112 | tf_op jit(solution)/shard_map/reduce_scatter | solution.py:262
  2024.3 2155.9 %reduce-scatter.40.cloned.1.call-start = ((), (), s32[]{:S(2)}) async-start(), calls=%async_computation.40 | async-start | bytes 18522112 | tf_op jit(solution)/shard_map/reduce_scatter | solution.py:261
  (280 other events, 5007.3 us)
Sparse Core Ops, SparseCore 0:
  10.2 12.8 all-gather.53
  25.3 11.3 all-gather.49
  39.3 77.0 all-gather.31
  119.0 66.4 all-gather.35
  187.9 67.6 all-gather.33
  258.2 68.0 all-gather.39
  329.0 158.8 all-gather.55
  490.6 147.6 all-gather.51
  641.0 67.0 all-gather.37
  710.6 67.0 all-gather.41
  786.9 22.7 all-reduce.34
  812.6 117.1 all-gather.45
  932.8 114.1 all-gather.43
  1059.7 117.1 all-gather.47
  1271.7 22.2 all-reduce.32
  1309.1 150.6 all-gather.63
  1462.4 153.3 all-gather.59
  1627.0 10.5 reduce-scatter.47
  1893.5 73.6 reduce-scatter.49
  1969.6 73.8 reduce-scatter.51
  2045.7 20.6 all-reduce.30
  2069.3 78.4 reduce-scatter.23
  2150.5 135.4 reduce-scatter.37
  2288.8 140.1 reduce-scatter.33
  2431.8 140.6 reduce-scatter.35
  2575.4 140.6 reduce-scatter.29
  2718.8 140.6 reduce-scatter.31
  2862.4 79.1 reduce-scatter.25
  2944.6 135.2 reduce-scatter.27
  3082.7 360.8 reduce-scatter.43
  3446.6 365.3 reduce-scatter.41
  3814.9 365.2 reduce-scatter.39
  (3 shorter events, 23.2 us)
where the time goes:
time: 4200 us; the launch traced here: 4190 us
  waiting for transfers between devices  2600 us (62%)
  matrix products  688 us (16%)
  blocking collectives  368 us (9%)
  local copies, waits for them, and re-layouts  253 us (6%)
  other arithmetic  209 us (5%)
  loops' own time  44.6 us (1%)
    reduce_scatter x1, waiting for transfers between devices, reduce_grads(): lax.psum_scatter(grads[10], 'seq', scatter_dimension=0, tiled=True)  368 us
    reduce_scatter x1, waiting for transfers between devices, reduce_grads(): lax.psum_scatter(grads[11], 'seq', scatter_dimension=0, tiled=True)  368 us
    reduce_scatter x1, waiting for transfers between devices, reduce_grads(): lax.psum_scatter(grads[12], 'seq', scatter_dimension=1, tiled=True)  364 us
    all_gather x4, blocking collectives, entering(): lax.all_gather(part.astype(kind), axis)  165 us
    dot_general x20, matrix products, back_prod(): lax.dot_general(grad, weight, (((1,), (1,)), ((), ())), preferred_element...  152 us
    reduce_scatter x1, waiting for transfers between devices, reduce_grads(): lax.psum_scatter(grads[5], 'seq', scatter_dimension=0, tiled=True)  144 us
    reduce_scatter x1, waiting for transfers between devices, reduce_grads(): lax.psum_scatter(grads[8], 'seq', scatter_dimension=0, tiled=True)  144 us
    reduce_scatter x1, waiting for transfers between devices, reduce_grads(): lax.psum_scatter(grads[6], 'seq', scatter_dimension=0, tiled=True)  143 us
  transfers between devices with their start and end apart: 39, of which 18 were waited for; matrix products, arithmetic and copies ran while one was open for 25% of the time, Pallas kernels for 0%

commit v1 on v0

v1 whole, which is shorter than its diff:
```python
import functools
import math

import jax
import jax.numpy as jnp
import numpy as np
from jax import lax
from jax.experimental import pallas as pl
from jax.experimental.pallas import tpu as pltpu
from jax.sharding import PartitionSpec as P

FDIM = 16
HDIM = 112
WIN = 64
KCONV = 3
TILE = 128
LANES = 128
PHI = 160

f32 = jnp.float32
bf16 = jnp.bfloat16
VMEM_BYTES = 56 * 1024 * 1024


def mul(a, b):
    return lax.dot_general(a, b, (((1,), (0,)), ((), ())), preferred_element_type=f32)


def mul_t(a, b):
    return lax.dot_general(a, b, (((1,), (1,)), ((), ())), preferred_element_type=f32)


def t_mul(a, b):
    return lax.dot_general(a, b, (((0,), (0,)), ((), ())), preferred_element_type=f32)


def feature_tables(heads):
    left = np.zeros((heads, heads * FDIM, PHI), np.float32)
    right = np.zeros((heads, heads * FDIM, PHI), np.float32)
    consts = np.zeros((8, PHI), np.float32)
    at = 0
    for a in range(FDIM):
        for b in range(a, FDIM):
            for h in range(heads):
                left[h, h * FDIM + a, at] = 0.5
                right[h, h * FDIM + b, at] = 0.5
            consts[2, at] = 1.0 / math.sqrt(2.0)
            consts[3, at] = 1.0 if a == b else 2.0
            at += 1
    for a in range(FDIM):
        for h in range(heads):
            left[h, h * FDIM + a, at] = 0.5
        consts[1, at] = 1.0
        consts[2, at] = 1.0
        consts[3, at] = 1.0
        at += 1
    consts[0, at] = consts[1, at] = consts[2, at] = consts[3, at] = 1.0
    return jnp.asarray(left, bf16), jnp.asarray(right, bf16), jnp.asarray(consts)


def with_one(values):
    rows = values.shape[0]
    lane = lax.broadcasted_iota(jnp.int32, (rows, LANES - HDIM), 1)
    extra = jnp.where(lane == 0, 1.0, 0.0).astype(values.dtype)
    return jnp.concatenate([values, extra], axis=1)


def head_cols(h):
    return slice(h * HDIM, (h + 1) * HDIM)


def features(rows, left, right, consts):
    a = mul(rows, left) + consts[0:1]
    b = mul(rows, right) + consts[1:2]
    return a, b, (a * b * consts[2:3]).astype(bf16)


def own_kernel(ic, qk, v, left, right, consts, state):
    heads = v.shape[2] // HDIM
    width = qk.shape[2] // 2
    keys = qk[0, :, width:]
    last = ic[0, :, 2:3].astype(f32)
    table = consts[...]
    for h in range(heads):
        _, _, phi = features(keys, left[h], right[h], table)
        phi = (phi.astype(f32) * last).astype(bf16)
        state[0, h] = t_mul(phi, with_one(v[0, :, head_cols(h)])).astype(bf16)


def linear_mask(ic, ir, t):
    rows, cols = TILE, TILE * (t + 1)
    i = lax.broadcasted_iota(jnp.int32, (rows, cols), 0) + t * TILE
    j = lax.broadcasted_iota(jnp.int32, (rows, cols), 1)
    slot = ic[0, t * TILE : (t + 1) * TILE, 0:1]
    kslot = ir[0, 1:2, 0:cols]
    return ((kslot == slot) & (j <= i)) | (j == i)


def window_mask(ic, ir, t):
    rows, cols = TILE, TILE + WIN
    i = lax.broadcasted_iota(jnp.int32, (rows, cols), 0)
    j = lax.broadcasted_iota(jnp.int32, (rows, cols), 1) - WIN
    slot = ic[0, t * TILE : (t + 1) * TILE, 0:1]
    kslot = ir[0, 0:1, t * TILE : t * TILE + cols]
    return ((kslot == slot) & (j <= i) & (i - j <= WIN)) | (j == i)


def fill_masks(ic, ir, lmask, wmask, tiles):
    for t in range(tiles):
        lmask[t * TILE : (t + 1) * TILE, 0 : TILE * (t + 1)] = jnp.where(
            linear_mask(ic, ir, t), 1.0, 0.0
        )
        wmask[t * TILE : (t + 1) * TILE, :] = jnp.where(window_mask(ic, ir, t), 0.0, -1e30)


def window_probs(wq_rows, wk_rows, mask):
    scores = mul_t(wq_rows, wk_rows) * (1.0 / math.sqrt(HDIM)) + mask
    top = jnp.max(scores, axis=1, keepdims=True)
    exponent = jnp.exp(scores - top)
    return exponent / jnp.sum(exponent, axis=1, keepdims=True)


def head_rows(rows, h):
    lane = lax.broadcasted_iota(jnp.int32, rows.shape, 1)
    return jnp.where(lane // FDIM == h, rows.astype(f32), 0.0).astype(bf16)


def mix_kernel(
    ic, ir, qk, v, wq, wk, cg, ci, wkp, vp, prefix, left, right, consts,
    mixed, linear, rden, lmask, wmask, kext, vext,
):
    heads = v.shape[2] // HDIM
    rows = v.shape[1]
    tiles = rows // TILE
    width = qk.shape[2] // 2
    fill_masks(ic, ir, lmask, wmask, tiles)
    queries = qk[0, :, :width]
    keys = qk[0, :, width:]
    carried = ic[0, :, 1:2].astype(f32)
    table = consts[...]
    lane = lax.broadcasted_iota(jnp.int32, (rows, LANES), 1)
    inverse = jnp.zeros((rows, LANES), f32)
    kext[0:WIN, :] = wkp[0]
    kext[WIN:, :] = wk[0]
    vext[0:WIN, :] = vp[0]
    vext[WIN:, :] = v[0]
    for h in range(heads):
        hc = head_cols(h)
        vh = with_one(vext[:, hc])
        kh = kext[:, hc]
        qh = head_rows(queries, h)
        _, _, phi = features(queries, left[h], right[h], table)
        phi = (phi.astype(f32) * (carried * table[3:4])).astype(bf16)
        for t in range(tiles):
            r = slice(t * TILE, (t + 1) * TILE)
            n = TILE * (t + 1)
            a = 0.25 * mul_t(qh[r], keys[0:n])
            weight = ((1.0 + a + 0.5 * (a * a)) * lmask[r, 0:n]).astype(bf16)
            numer = mul(weight, vh[WIN : WIN + n]) + mul(phi[r], prefix[0, h])
            inv = 1.0 / numer[:, HDIM : HDIM + 1]
            inverse_t = jnp.where(lane[r] == h, inv, 0.0)
            lin = (numer * inv)[:, :HDIM]
            probs = window_probs(wq[0, r, hc], kh[r.start : r.start + TILE + WIN], wmask[r, :])
            win = mul(probs.astype(bf16), vh[r.start : r.start + TILE + WIN])[:, :HDIM]
            conv = ci[0, r, hc].astype(f32) * cg[0, r, hc].astype(f32)
            mixed[0, r, hc] = (lin + win + conv).astype(bf16)
            linear[0, r, hc] = lin.astype(bf16)
            if h == 0:
                rden[0, r, :] = inverse_t
            else:
                rden[0, r, :] += inverse_t


def d_numer(dm, linear, rden, h, r):
    hc = head_cols(h)
    inv = rden[0, r, h : h + 1]
    dn = dm[0, r, hc].astype(f32) * inv
    dd = -jnp.sum(dn * linear[0, r, hc].astype(f32), axis=1, keepdims=True)
    return dn, dd


def with_total(dn, dd):
    rows = dn.shape[0]
    high = dd.astype(bf16).astype(f32)
    lane = lax.broadcasted_iota(jnp.int32, (rows, LANES - HDIM), 1)
    extra = jnp.where(lane == 0, high, jnp.where(lane == 1, dd - high, 0.0))
    return jnp.concatenate([dn, extra], axis=1).astype(bf16)


def prefix_grad_kernel(ic, qk, dm, linear, rden, left, right, consts, d_prefix):
    heads = dm.shape[2] // HDIM
    rows = dm.shape[1]
    width = qk.shape[2] // 2
    queries = qk[0, :, :width]
    carried = ic[0, :, 1:2].astype(f32)
    table = consts[...]
    for h in range(heads):
        _, _, phi = features(queries, left[h], right[h], table)
        phi = (phi.astype(f32) * (carried * table[3:4])).astype(bf16)
        dn, dd = d_numer(dm, linear, rden, h, slice(0, rows))
        d_prefix[0, h] = t_mul(phi, with_total(dn, dd)).astype(bf16)


def mix_grad_kernel(
    ic, ir, qk, v, wq, wk, cg, ci, wkp, vp, prefix, left, right, consts, dm, linear, rden,
    dq, dk, dv, dwq, dwk, dcg, dci, dwkp, dvp, lmask, wmask, kext, vext, dqs, dks, dvs, dwks,
):
    heads = v.shape[2] // HDIM
    rows = v.shape[1]
    tiles = rows // TILE
    width = qk.shape[2] // 2
    fill_masks(ic, ir, lmask, wmask, tiles)
    queries = qk[0, :, :width]
    keys = qk[0, :, width:]
    carried = ic[0, :, 1:2].astype(f32)
    table = consts[...]
    kext[0:WIN, :] = wkp[0]
    kext[WIN:, :] = wk[0]
    vext[0:WIN, :] = vp[0]
    vext[WIN:, :] = v[0]
    grad_rows = dm[0].astype(f32)
    dci[0] = (grad_rows * cg[0].astype(f32)).astype(bf16)
    dcg[0] = (grad_rows * ci[0].astype(f32)).astype(bf16)
    lane_q = lax.broadcasted_iota(jnp.int32, (TILE, width), 1)
    lane_f = lax.broadcasted_iota(jnp.int32, (PHI, LANES), 1)
    dqs[...] = jnp.zeros_like(dqs)
    dks[...] = jnp.zeros_like(dks)
    for h in range(heads):
        hc = head_cols(h)
        vh = vext[:, hc]
        kh = kext[:, hc]
        qh = head_rows(queries, h)
        khead = head_rows(keys, h)
        state = prefix[0, h].astype(f32)
        state = jnp.where(lane_f == HDIM + 1, state[:, HDIM : HDIM + 1], state).astype(bf16)
        dvs[...] = jnp.zeros_like(dvs)
        dwks[...] = jnp.zeros_like(dwks)
        for t in range(tiles):
            r = slice(t * TILE, (t + 1) * TILE)
            n = TILE * (t + 1)
            e = slice(t * TILE, t * TILE + TILE + WIN)
            dmt = dm[0, r, hc]
            probs = window_probs(wq[0, r, hc], kh[e], wmask[r, :])
            dp = mul_t(dmt, vh[e])
            ds = probs * (dp - jnp.sum(dp * probs, axis=1, keepdims=True))
            ds = (ds * (1.0 / math.sqrt(HDIM))).astype(bf16)
            dwq[0, r, hc] = mul(ds, kh[e]).astype(bf16)
            dwks[e, :] += t_mul(ds, wq[0, r, hc])
            dvs[e, :] += t_mul(probs.astype(bf16), dmt)

            dn, dd = d_numer(dm, linear, rden, h, r)
            dnb = dn.astype(bf16)
            a = 0.25 * mul_t(qh[r], keys[0:n])
            mask = lmask[r, 0:n]
            weight = ((1.0 + a + 0.5 * (a * a)) * mask).astype(bf16)
            dkern = mul_t(dnb, vh[WIN : WIN + n]) + dd
            da = (dkern * (1.0 + a) * (0.25 * mask)).astype(bf16)
            dvs[WIN : WIN + n, :] += t_mul(weight, dnb)
            dks[0:n, :] += t_mul(da, qh[r])
            g = mul_t(with_total(dn, dd), state) * (
                carried[r] * (table[2:3] * table[3:4])
            )
            fa, fb, _ = features(queries[r], left[h], right[h], table)
            dqs[r, :] += (
                mul(da, khead[0:n])
                + mul_t((g * fb).astype(bf16), left[h])
                + mul_t((g * fa).astype(bf16), right[h])
            )
        dv[0, :, hc] = dvs[WIN:, :]
        dvp[0, :, hc] = dvs[0:WIN, :].astype(bf16)
        dwk[0, :, hc] = dwks[WIN:, :]
        dwkp[0, :, hc] = dwks[0:WIN, :].astype(bf16)
    dq[0] = dqs[...].astype(bf16)
    dk[0] = dks[...]


def finish_kernel(
    ic, qk, v, d_own, left, right, consts, dk, dv, dwk, dwq, dcg, dq, back_k, back_v, out
):
    heads = v.shape[2] // HDIM
    rows = v.shape[1]
    half = v.shape[2]
    width = qk.shape[2] // 2
    keys = qk[0, :, width:]
    last = ic[0, :, 2:3].astype(f32)
    table = consts[...]
    d_keys = dk[0]
    for h in range(heads):
        hc = head_cols(h)
        grad = d_own[0, h]
        fa, fb, phi = features(keys, left[h], right[h], table)
        phi = (phi.astype(f32) * last).astype(bf16)
        part = dv[0, :, hc] + mul(phi, grad)[:, :HDIM]
        out[0, 0 : rows - WIN, hc] = part[0 : rows - WIN].astype(bf16)
        out[0, rows - WIN :, hc] = (part[rows - WIN :] + back_v[0, :, hc].astype(f32)).astype(bf16)
        g = mul_t(with_one(v[0, :, hc]), grad) * (last * table[2:3])
        d_keys = (
            d_keys
            + mul_t((g * fb).astype(bf16), left[h])
            + mul_t((g * fa).astype(bf16), right[h])
        )
    out[0, :, half : 2 * half] = dwq[0]
    out[0, 0 : rows - WIN, 2 * half : 3 * half] = dwk[0, 0 : rows - WIN].astype(bf16)
    out[0, rows - WIN :, 2 * half : 3 * half] = (
        dwk[0, rows - WIN :] + back_k[0].astype(f32)
    ).astype(bf16)
    out[0, :, 3 * half : 4 * half] = dcg[0]
    out[0, :, 4 * half : 4 * half + width] = dq[0]
    out[0, :, 4 * half + width :] = d_keys.astype(bf16)


def micro_spec(array, block=None, at=0):
    shape = array.shape
    if block is None:
        return pl.BlockSpec((1,) + shape[1:], lambda m: (m,) + (0,) * (len(shape) - 1))
    return pl.BlockSpec((1, shape[1], block), lambda m: (m, 0, at))


def whole_spec(array):
    rank = len(array.shape)
    return pl.BlockSpec(array.shape, lambda m: (0,) * rank)


def call(kernel, micros, ins, outs, scratch, flops):
    return pl.pallas_call(
        kernel,
        grid=(micros,),
        in_specs=[spec for _, spec in ins],
        out_specs=[micro_spec(o) for o in outs],
        out_shape=[jax.ShapeDtypeStruct(o.shape, o.dtype) for o in outs],
        scratch_shapes=scratch,
        compiler_params=pltpu.CompilerParams(vmem_limit_bytes=VMEM_BYTES),
        cost_estimate=pl.CostEstimate(
            flops=flops,
            bytes_accessed=sum(math.prod(o.shape) * o.dtype.itemsize for o in outs) * 3,
            transcendentals=0,
        ),
    )(*[a for a, _ in ins])


def struct(*shape, dtype=bf16):
    return jax.ShapeDtypeStruct(shape, dtype)


def projected(proj, half):
    width = proj.shape[2] - 4 * half
    return [(proj, micro_spec(proj, half, i)) for i in range(4)] + [
        (proj, micro_spec(proj, width, 4 * half // width))
    ]


def own_states(ic, proj, half, tables):
    micros = proj.shape[0]
    heads = half // HDIM
    v, _, _, _, qk = projected(proj, half)
    ins = [(ic, micro_spec(ic)), qk, v] + [(t, whole_spec(t)) for t in tables]
    return call(own_kernel, micros, ins, [struct(micros, heads, PHI, LANES)], [], 10**9)[0]


def mix_forward(ic, ir, proj, half, conv_in, tail_k, tail_v, prefix, tables):
    micros, rows, _ = proj.shape
    v, wq, wk, cg, qk = projected(proj, half)
    rest = [(a, micro_spec(a)) for a in (conv_in, tail_k, tail_v, prefix)]
    ins = (
        [(ic, micro_spec(ic)), (ir, micro_spec(ir)), qk, v, wq, wk, cg]
        + rest
        + [(t, whole_spec(t)) for t in tables]
    )
    outs = [
        struct(micros, rows, half),
        struct(micros, rows, half),
        struct(micros, rows, LANES, dtype=f32),
    ]
    scratch = [
        pltpu.VMEM((rows, rows), f32),
        pltpu.VMEM((rows, TILE + WIN), f32),
        pltpu.VMEM((rows + WIN, half), bf16),
        pltpu.VMEM((rows + WIN, half), bf16),
    ]
    return call(mix_kernel, micros, ins, outs, scratch, 10**10)


def prefix_gradient(ic, proj, half, dm, linear, rden, tables):
    micros = proj.shape[0]
    heads = half // HDIM
    qk = projected(proj, half)[4]
    ins = (
        [(ic, micro_spec(ic)), qk]
        + [(a, micro_spec(a)) for a in (dm, linear, rden)]
        + [(t, whole_spec(t)) for t in tables]
    )
    return call(
        prefix_grad_kernel, micros, ins, [struct(micros, heads, PHI, LANES)], [], 10**9
    )[0]


def mix_backward(ic, ir, proj, half, conv_in, tail_k, tail_v, prefix, tables, dm, linear, rden):
    micros, rows, _ = proj.shape
    width = (proj.shape[2] - 4 * half) // 2
    v, wq, wk, cg, qk = projected(proj, half)
    ins = (
        [(ic, micro_spec(ic)), (ir, micro_spec(ir)), qk, v, wq, wk, cg]
        + [(a, micro_spec(a)) for a in (conv_in, tail_k, tail_v, prefix)]
        + [(t, whole_spec(t)) for t in tables]
        + [(a, micro_spec(a)) for a in (dm, linear, rden)]
    )
    outs = [
        struct(micros, rows, width),
        struct(micros, rows, width, dtype=f32),
        struct(micros, rows, half, dtype=f32),
        struct(micros, rows, half),
        struct(micros, rows, half, dtype=f32),
        struct(micros, rows, half),
        struct(micros, rows, half),
        struct(micros, WIN, half),
        struct(micros, WIN, half),
    ]
    scratch = [
        pltpu.VMEM((rows, rows), f32),
        pltpu.VMEM((rows, TILE + WIN), f32),
        pltpu.VMEM((rows + WIN, half), bf16),
        pltpu.VMEM((rows + WIN, half), bf16),
        pltpu.VMEM((rows, width), f32),
        pltpu.VMEM((rows, width), f32),
        pltpu.VMEM((rows + WIN, HDIM), f32),
        pltpu.VMEM((rows + WIN, HDIM), f32),
    ]
    return call(mix_grad_kernel, micros, ins, outs, scratch, 2 * 10**10)


def finish_gradients(ic, proj, half, d_own, tables, dk, dv, dwk, dwq, dcg, dq, back_k, back_v):
    micros = proj.shape[0]
    v, _, _, _, qk = projected(proj, half)
    ins = (
        [(ic, micro_spec(ic)), qk, v, (d_own, micro_spec(d_own))]
        + [(t, whole_spec(t)) for t in tables]
        + [(a, micro_spec(a)) for a in (dk, dv, dwk, dwq, dcg, dq, back_k, back_v)]
    )
    return call(finish_kernel, micros, ins, [struct(*proj.shape)], [], 2 * 10**9)[0]


def cut_axis(size):
    side = max(s for s in range(1, size + 1) if s**3 <= size and size % (s * s) == 0)
    return (size // (side * side), side, side)


def strides(dims):
    return (dims[1] * dims[2], dims[2], 1)


def coords(index, dims):
    return tuple((index // st) % d for st, d in zip(strides(dims), dims))


def ring_pairs(dims, axis, shift):
    stride, size = strides(dims)[axis], dims[axis]
    pairs = []
    for i in range(math.prod(dims)):
        c = (i // stride) % size
        pairs.append((i, i + ((c + shift) % size - c) * stride))
    return pairs


def along(x, dims, axis, shift):
    return lax.ppermute(x, "seq", ring_pairs(dims, axis, shift))


def gather_pieces(shard, order, dims):
    pieces = [(shard[None], [(0, 0, 0)])]
    for step, axis in enumerate(order):
        arrived = []
        for shift in range(1, dims[axis]):
            for piece, offsets in pieces:
                moved = [o[:axis] + (shift,) + o[axis + 1 :] for o in offsets]
                arrived.append((along(piece, dims, axis, -shift), moved))
        pieces = pieces + arrived
        if step == 0 and len(pieces) > 1:
            pieces = [
                (
                    jnp.concatenate([p for p, _ in pieces], axis=0),
                    [o for _, offsets in pieces for o in offsets],
                )
            ]
    return pieces


def lay_kernel(dims, rows, plan, *refs):
    ins, out, stage, taken, put = refs[: len(plan)], *refs[len(plan) :]
    here = coords(lax.axis_index("seq"), dims)
    loads, stores = [], []
    for ref, (column, offsets) in zip(ins, plan):
        for b, offset in enumerate(offsets):
            there = sum(
                lax.rem(c + o, d) * st for c, o, d, st in zip(here, offset, dims, strides(dims))
            )
            place = (pl.ds(pl.multiple_of(there * rows, rows), rows), pl.ds(column, ref.shape[2]))
            k = len(loads)
            loads.append(pltpu.make_async_copy(ref.at[b], stage.at[place], taken.at[k]))
            stores.append(pltpu.make_async_copy(stage.at[place], out.at[place], put.at[k]))
    for load in loads:
        load.start()
    for load, store in zip(loads, stores):
        load.wait()
        store.start()
    for store in stores:
        store.wait()


def lay_blocks(pieces, dims):
    blocks = jnp.concatenate([p for p, _ in pieces], axis=0)
    known = [coords_place(o, dims) for _, offsets in pieces for o in offsets]
    slot_of = jnp.asarray(np.argsort(np.array(known)), jnp.int32)
    here = coords(lax.axis_index("seq"), dims)
    there = coords(jnp.arange(math.prod(dims), dtype=jnp.int32), dims)
    offset = [lax.rem(t - h + d, d) for t, h, d in zip(there, here, dims)]
    return blocks[slot_of[coords_place(offset, dims)]].reshape(-1, blocks.shape[2])


def coords_place(offset, dims):
    return sum(o * st for o, st in zip(offset, strides(dims)))


def lay_out(parts, dims):
    plan, arrays, column = [], [], 0
    for pieces in parts:
        for piece, offsets in pieces:
            plan.append((column, offsets))
            arrays.append(piece)
        column += pieces[0][0].shape[2]
    rows = arrays[0].shape[1]
    if rows % (2 * 8):
        return jnp.concatenate([lay_blocks(pieces, dims) for pieces in parts], axis=1)
    count = sum(len(offsets) for _, offsets in plan)
    size = math.prod(dims) * rows * column * arrays[0].dtype.itemsize
    return pl.pallas_call(
        functools.partial(lay_kernel, dims, rows, plan),
        in_specs=[pl.BlockSpec(memory_space=pl.ANY)] * len(arrays),
        out_specs=pl.BlockSpec(memory_space=pl.ANY),
        out_shape=jax.ShapeDtypeStruct((math.prod(dims) * rows, column), arrays[0].dtype),
        scratch_shapes=[
            pltpu.VMEM((math.prod(dims) * rows, column), arrays[0].dtype),
            pltpu.SemaphoreType.DMA((count,)),
            pltpu.SemaphoreType.DMA((count,)),
        ],
        compiler_params=pltpu.CompilerParams(vmem_limit_bytes=VMEM_BYTES),
        cost_estimate=pl.CostEstimate(flops=0, bytes_accessed=2 * size, transcendentals=0),
    )(*arrays)


def gather_rows(shard, orders, dims):
    total, used, parts = sum(share for _, share in orders), 0, []
    columns, done = shard.shape[1], 0
    for order, share in orders:
        done += share
        end = columns if done == total else columns * done // total // LANES * LANES
        parts.append(gather_pieces(shard[:, used:end], order, dims))
        used = end
    return lay_out(parts, dims)


def scatter_part(grad, order, dims):
    rows = grad.shape[0] // math.prod(dims)
    here = coords(lax.axis_index("seq"), dims)
    x = grad.reshape(dims + (rows, grad.shape[1]))
    for axis in order:
        total = lax.dynamic_index_in_dim(x, here[axis], axis).astype(f32)
        for shift in range(1, dims[axis]):
            to = lax.rem(here[axis] + shift, dims[axis])
            total = total + along(
                lax.dynamic_index_in_dim(x, to, axis), dims, axis, shift
            ).astype(f32)
        x = total.astype(grad.dtype)
    return total.reshape(rows, grad.shape[1])


def scatter_rows(grad, orders, dims):
    total, used, parts = sum(share for _, share in orders), 0, []
    columns, done = grad.shape[1], 0
    for order, share in orders:
        done += share
        end = columns if done == total else columns * done // total // LANES * LANES
        parts.append(scatter_part(grad[:, used:end], order[::-1], dims))
        used = end
    return parts[0] if len(parts) == 1 else jnp.concatenate(parts, axis=1)


def other_core(x):
    return lax.ppermute(x, "head", [(0, 1), (1, 0)])


def both_halves(x):
    y = other_core(x)
    first = lax.axis_index("head") == 0
    return jnp.concatenate([jnp.where(first, x, y), jnp.where(first, y, x)], axis=-1)


def core_sum(x):
    low = x.astype(bf16)
    return low.astype(f32) + other_core(low).astype(f32)


def shifted(x, by):
    size = lax.axis_size("seq")
    return lax.ppermute(x, "seq", [(i, i + by) for i in range(size) if 0 <= i + by < size])


def layout(lengths, order, positions):
    places = jnp.arange(lengths.shape[0], dtype=jnp.int32)
    picked = (order[:, None] == places[None, :]).astype(jnp.int32)
    ordered = jnp.sum(picked * lengths[None, :], axis=1, dtype=jnp.int32)
    tiles = (ordered + TILE - 1) // TILE
    first_tile = jnp.cumsum(tiles, dtype=jnp.int32) - tiles
    row_tile = positions // TILE
    after = (row_tile[:, None] >= first_tile[None, :]).astype(jnp.int32)
    slot = jnp.sum(after, axis=1, dtype=jnp.int32) - 1
    chosen = (slot[:, None] == places[None, :]).astype(jnp.int32)
    start = jnp.sum(chosen * first_tile[None, :], axis=1, dtype=jnp.int32) * TILE
    length = jnp.sum(chosen * ordered[None, :], axis=1, dtype=jnp.int32)
    return slot, start, positions - start < length


def carry_over(own, starts, rows, dims, backward):
    me = lax.axis_index("seq")
    here = coords(me, dims)

    def unbroken(a, b):
        last = lax.dynamic_index_in_dim(starts, jnp.maximum(b, 0), 1, keepdims=False)
        return (a > b) | (last < a * rows)

    def weigh(flag, x):
        return jnp.where(flag[:, None, None, None], x.astype(f32), 0.0)

    result = None
    total = own
    for axis in (2, 1, 0):
        size, stride = dims[axis], strides(dims)[axis]
        base = me // (stride * size) * (stride * size)
        c = here[axis]
        if size == 1:
            continue

        def gap(j):
            if backward:
                return unbroken(base, base + j * stride - 1)
            return unbroken(base + (j + 1) * stride, base + size * stride - 1)

        added = weigh(gap(c), total)
        for shift in range(1, size):
            j = lax.rem(c + size - shift, size)
            got = along(total, dims, axis, shift)
            if backward:
                near = (j > c) & unbroken(me + 1, base + j * stride - 1)
            else:
                near = (j < c) & unbroken(base + (j + 1) * stride, me - 1)
            part = weigh(near, got)
            result = part if result is None else result + part
            added = added + weigh(gap(j), got)
        total = added.astype(own.dtype)
    return result.astype(own.dtype)


def rsq(v):
    return lax.rsqrt(jnp.mean(v * v, axis=-1, keepdims=True) + 1e-05)


def norm_back(v, r, gain, dy):
    inner = jnp.mean(v * gain * dy, axis=-1, keepdims=True)
    return r * gain * dy - v * (r * r * r * inner), jnp.sum(dy * v * r, axis=0)


def dot_nt(a, b):
    return mul_t(a, b)


def per_device(
    layer_input,
    cotangent,
    lengths,
    doc_order,
    norm_gains,
    conv_filter,
    w_query,
    w_key,
    w_value,
    w_wquery,
    w_wkey,
    w_conv_in,
    w_conv_gate,
    w_out,
    w_gate,
    w_up,
    w_down,
):
    micros, rows, half = layer_input.shape
    dims = cut_axis(lax.axis_size("seq"))
    me = lax.axis_index("seq")
    head = lax.axis_index("head")
    place = me * rows
    tables = feature_tables(half // HDIM)
    qk = w_query.shape[1]
    ff = w_gate.shape[1]
    zyx, zxy, xzy, yzx = (0, 1, 2), (0, 2, 1), (2, 0, 1), (1, 0, 2)

    small = jnp.concatenate([norm_gains, conv_filter], axis=0).T
    small = jnp.pad(small, ((0, 0), (0, LANES - small.shape[1])))
    pack_in = jnp.concatenate([w_value, w_wquery, w_wkey, w_conv_gate, w_query, w_key], axis=1)
    pack_ff = jnp.concatenate([w_gate, w_up], axis=1)
    wide = [(zyx, 1), (zxy, 1)]
    narrow = [(xzy, 10), (yzx, 9)]
    small_all = gather_rows(small, [(zyx, 1)], dims)
    full_in = gather_rows(pack_in, wide, dims)
    full_conv = gather_rows(w_conv_in, [(xzy, 1)], dims)
    full_out = gather_rows(w_out.T, [(yzx, 1)], dims)
    full_ff = gather_rows(pack_ff, wide, dims)
    full_down = gather_rows(w_down.T, narrow, dims)
    vectors = small_all[:, : norm_gains.shape[0] + KCONV].astype(f32).T
    gain1, gain2 = vectors[0:1], vectors[1:2]
    taps = vectors[2:]

    positions = place + jnp.arange(rows, dtype=jnp.int32)
    window_place = place - WIN + jnp.arange(WIN, dtype=jnp.int32)
    conv_place = place - (KCONV - 1) + jnp.arange(KCONV - 1, dtype=jnp.int32)
    ends = (jnp.arange(lax.axis_size("seq"), dtype=jnp.int32) + 1) * rows - 1
    info_cols, info_rows, starts, same = [], [], [], []
    for m in range(micros):
        slot, start, valid = layout(lengths[m], doc_order[m], positions)
        wslot, _, wvalid = layout(lengths[m], doc_order[m], window_place)
        cslot, _, _ = layout(lengths[m], doc_order[m], conv_place)
        starts.append(layout(lengths[m], doc_order[m], ends)[1])
        last = (slot == slot[rows - 1]) & valid
        cols = jnp.stack([slot, (start < place).astype(jnp.int32), last.astype(jnp.int32)], axis=1)
        info_cols.append(jnp.pad(cols, ((0, 0), (0, 5))))
        own = jnp.where(valid, slot, -1)
        ext = jnp.concatenate([jnp.where(wvalid, wslot, -1), own])
        ext = jnp.pad(ext, (0, WIN), constant_values=-1)
        own = jnp.pad(own, (0, 2 * WIN), constant_values=-1)
        info_rows.append(jnp.pad(jnp.stack([ext, own]), ((0, 6), (0, 0))))
        stack = jnp.concatenate([cslot, slot])
        same.append(
            jnp.stack(
                [
                    stack[KCONV - 1 - s : KCONV - 1 - s + rows] == slot
                    for s in range(1, KCONV)
                ]
            )
        )
    ic, ir, starts = jnp.stack(info_cols), jnp.stack(info_rows), jnp.stack(starts)
    same = jnp.stack(same).astype(f32)[..., None]

    x_low = both_halves(layer_input)
    cot_low = both_halves(cotangent)
    x = x_low.astype(f32)
    r1 = rsq(x)
    h1 = (x * r1 * gain1).astype(bf16)
    width = h1.shape[2]
    h1_prev = shifted(h1[:, rows - (KCONV - 1) :], 1)
    flat_h1 = h1.reshape(micros * rows, width)
    proj = mul(flat_h1, full_in).astype(bf16).reshape(micros, rows, -1)

    tail_v = shifted(proj[:, rows - WIN :, :half], 1)
    tail_k = shifted(proj[:, rows - WIN :, 2 * half : 3 * half], 1)
    own = own_states(ic, proj, half, tables)
    prefix = carry_over(own, starts, rows, dims, False)

    stacked = jnp.concatenate([h1_prev, h1], axis=1)
    h1f = h1.astype(f32)
    earlier = [
        stacked[:, KCONV - 1 - s : KCONV - 1 - s + rows].astype(f32) * same[:, s - 1]
        for s in range(1, KCONV)
    ]
    conv = taps[0] * h1f
    for s in range(1, KCONV):
        conv = conv + taps[s] * earlier[s - 1]
    conv = conv.astype(bf16)
    flat_conv = conv.reshape(micros * rows, width)
    conv_in = mul(flat_conv, full_conv).astype(bf16).reshape(micros, rows, half)

    mixed, linear, rden = mix_forward(
        ic, ir, proj, half, conv_in, tail_k, tail_v, prefix, tables
    )
    flat_mixed = mixed.reshape(micros * rows, half)
    resid = x.reshape(micros * rows, width) + core_sum(mul_t(flat_mixed, full_out))

    r2 = rsq(resid)
    h2 = (resid * r2 * gain2).astype(bf16)
    gate_up = mul(h2, full_ff).astype(bf16)
    gate, up = gate_up[:, :ff].astype(f32), gate_up[:, ff:].astype(f32)
    sig = 1.0 / (1.0 + jnp.exp(-gate))
    hidden = (gate * sig * up).astype(bf16)
    flat_cot = cot_low.reshape(micros * rows, width)
    grad_down = t_mul(flat_cot, hidden).astype(bf16)
    sum_down = scatter_rows(grad_down, narrow, dims)
    ffn = mul_t(hidden, full_down).astype(bf16)

    def pick(a, which):
        return lax.dynamic_slice_in_dim(a, which * half, half, a.ndim - 1)

    ffn_other = other_core(pick(ffn, 1 - head))
    output = pick(resid, head) + (pick(ffn, head).astype(f32) + ffn_other.astype(f32))
    output = output.astype(bf16).reshape(micros, rows, half)

    d_hidden = mul(flat_cot, full_down)
    d_gate = (d_hidden * up * (sig * (1.0 + gate * (1.0 - sig)))).astype(bf16)
    d_up = (d_hidden * (gate * sig)).astype(bf16)
    d_ff = jnp.concatenate([d_gate, d_up], axis=1)
    grad_ff = t_mul(h2, d_ff).astype(bf16)
    sum_ff = scatter_rows(grad_ff, wide, dims)
    d_h2 = core_sum(mul_t(d_ff, full_ff))
    d_resid, d_gain2 = norm_back(resid, r2, gain2, d_h2)
    d_resid = flat_cot.astype(f32) + d_resid
    d_resid_low = d_resid.astype(bf16)

    grad_out = t_mul(d_resid_low, flat_mixed).astype(bf16)
    sum_out = scatter_rows(grad_out, [(yzx, 1)], dims)
    d_mixed = mul(d_resid_low, full_out).astype(bf16).reshape(micros, rows, half)
    d_prefix = prefix_gradient(ic, proj, half, d_mixed, linear, rden, tables)
    d_own = carry_over(d_prefix, starts, rows, dims, True)
    dq, dk, dv, dwq, dwk, dcg, dci, back_k, back_v = mix_backward(
        ic, ir, proj, half, conv_in, tail_k, tail_v, prefix, tables, d_mixed, linear, rden
    )
    back_k = shifted(back_k, -1)
    back_v = shifted(back_v, -1)
    flat_dci = dci.reshape(micros * rows, half)
    grad_conv = t_mul(flat_conv, flat_dci).astype(bf16)
    sum_conv = scatter_rows(grad_conv, [(xzy, 1)], dims)
    d_conv = mul_t(flat_dci, full_conv).reshape(micros, rows, width)
    d_h1 = taps[0] * d_conv
    d_taps = [jnp.sum(d_conv * h1f, axis=(0, 1))]
    before = jnp.zeros((micros, KCONV - 1, width), f32)
    for s in range(1, KCONV):
        through = d_conv * same[:, s - 1]
        d_taps.append(jnp.sum(d_conv * earlier[s - 1], axis=(0, 1)))
        moved = taps[s] * through
        d_h1 = d_h1 + jnp.pad(moved[:, s:], ((0, 0), (0, s), (0, 0)))
        before = before + jnp.pad(moved[:, :s], ((0, 0), (KCONV - 1 - s, 0), (0, 0)))
    returned = shifted(before.astype(bf16), -1).astype(f32)
    d_h1 = d_h1 + jnp.pad(returned, ((0, 0), (rows - (KCONV - 1), 0), (0, 0)))
    d_proj = finish_gradients(
        ic, proj, half, d_own, tables, dk, dv, dwk, dwq, dcg, dq, back_k, back_v
    ).reshape(micros * rows, -1)
    grad_in = t_mul(flat_h1, d_proj).astype(bf16)
    sum_in = scatter_rows(grad_in, wide, dims)
    d_h1 = core_sum(d_h1.reshape(micros * rows, width) + mul_t(d_proj, full_in))
    d_x, d_gain1 = norm_back(
        x.reshape(micros * rows, width), r1.reshape(micros * rows, 1), gain1, d_h1
    )
    grad_input = pick(d_resid + d_x, head).astype(bf16).reshape(micros, rows, half)

    d_taps = jnp.stack(d_taps)
    d_taps = d_taps + other_core(d_taps)
    d_small = jnp.concatenate([d_gain1[None], d_gain2[None], d_taps], axis=0).T
    d_small = jnp.pad(d_small, ((0, 0), (0, LANES - d_small.shape[1])))
    sum_small = scatter_rows(d_small, [(zyx, 1)], dims).T
    gains_count = norm_gains.shape[0]
    return (
        output,
        grad_input,
        sum_small[:gains_count],
        sum_small[gains_count : gains_count + KCONV],
        sum_in[:, 4 * half : 4 * half + qk],
        sum_in[:, 4 * half + qk :],
        sum_in[:, :half],
        sum_in[:, half : 2 * half],
        sum_in[:, 2 * half : 3 * half],
        sum_conv,
        sum_in[:, 3 * half : 4 * half],
        sum_out.T,
        sum_ff[:, :ff],
        sum_ff[:, ff:],
        sum_down.T,
    )


def solution(mesh):
    rows_split = P(None, "seq", "head")
    vectors = P(None, "seq")
    by_rows = P("seq", "head")
    by_columns = P("head", "seq")
    weights = (by_rows,) * 7 + (by_columns, by_rows, by_rows, by_columns)
    return jax.shard_map(
        per_device,
        mesh=mesh,
        in_specs=(rows_split, rows_split, P(), P(), vectors, vectors) + weights,
        out_specs=(rows_split, rows_split, vectors, vectors) + weights,
        check_vma=False,
    )
```

time: 4200 us -> 1830 us (0.44)
  waiting for transfers between devices: 2600 us -> 819 us
  matrix products: 688 us -> 252 us
  blocking collectives: 368 us -> 0 us
  starting transfers between devices: 9.9 us -> 310 us
  Pallas kernels: 0 us -> 208 us
  local copies, waits for them, and re-layouts: 253 us -> 86.8 us
  other arithmetic: 209 us -> 139 us
  loops' own time: 44.6 us -> 0 us
    reduce_scatter x11 -> x0, waiting for transfers between devices: 2110 us -> none  [the longest x1 368 us: reduce_grads(): lax.psum_scatter(grads[10], 'seq', scatter_dimension=0, tiled=True)]
    ppermute x4 -> x130, waiting for transfers between devices: 0.01 us -> 819 us  [the longest x117 819 us: along(): return lax.ppermute(x, 'seq', ring_pairs(dims, axis, shift))]
    all_gather x17 -> x0, waiting for transfers between devices: 443 us -> none  [the longest x1 119 us: fetch_weights(): lax.all_gather(shards[12], 'seq', axis=1, tiled=True)]
    dot_general x106 -> x15, matrix products: 688 us -> 252 us  [the longest x5 104 us: mul_t(): lax.dot_general(a, b, (((1,), (1,)), ((), ())), preferred_element_type=f32)]
    all_gather x8 -> x0, blocking collectives: 325 us -> none  [the longest x4 165 us: entering(): lax.all_gather(part.astype(kind), axis)]
    ppermute x4 -> x130, starting transfers between devices: 7.04 us -> 310 us  [the longest x117 295 us: along(): return lax.ppermute(x, 'seq', ring_pairs(dims, axis, shift))]
    pallas_call x0 -> x11, Pallas kernels: none -> 208 us  [the longest x5 169 us: call(): pl.pallas_call(kernel, grid=(micros,), in_specs=[spec for _, spec in ins]...]
    dynamic_slice x128 -> x29, local copies, waits for them, and re-layouts: 108 us -> 26.5 us  [the longest x27 23.8 us: scatter_part(): lax.dynamic_index_in_dim(x, to, axis)]
  transfers between devices with their start and end apart: 39 -> 130, of which waited for: 18 -> 51; matrix products, arithmetic and copies ran while one was open for 25% -> 17% of each run, Pallas kernels for 0% -> 11%
where the time goes in v1:
time: 1830 us; the launch traced here: 1820 us
  waiting for transfers between devices  819 us (45%)
  starting transfers between devices  310 us (17%)
  matrix products  252 us (14%)
  Pallas kernels  208 us (11%)
  other arithmetic  139 us (8%)
  local copies, waits for them, and re-layouts  86.8 us (5%)
    ppermute x117, waiting for transfers between devices, along(): return lax.ppermute(x, 'seq', ring_pairs(dims, axis, shift))  819 us
    ppermute x117, starting transfers between devices, along(): return lax.ppermute(x, 'seq', ring_pairs(dims, axis, shift))  295 us
    pallas_call x5, Pallas kernels, call(): pl.pallas_call(kernel, grid=(micros,), in_specs=[spec for _, spec in ins]...  169 us
    dot_general x5, matrix products, mul_t(): lax.dot_general(a, b, (((1,), (1,)), ((), ())), preferred_element_type=f32)  104 us
    dot_general x5, matrix products, t_mul(): lax.dot_general(a, b, (((0,), (0,)), ((), ())), preferred_element_type=f32)  75.4 us
    dot_general x5, matrix products, mul(): lax.dot_general(a, b, (((1,), (0,)), ((), ())), preferred_element_type=f32)  72.9 us
    pallas_call x6, Pallas kernels, lay_out(): pl.pallas_call(functools.partial(lay_kernel, dims, rows, plan), in_specs=...  39 us
  transfers between devices with their start and end apart: 130, of which 51 were waited for; matrix products, arithmetic and copies ran while one was open for 17% of the time, Pallas kernels for 11%

profile of v1, /device:TPU:0, one launch (start us, length us, event | category | flops | bytes accessed | tf_op | source)
XLA Modules:
  0.0 1819.1 jit_solution(2580124756320452210)
XLA Ops:
  35.5 22.9 %collective-permute-done.14 = bf16[1,112,1920]{2,1,0:T(8,128)(2,1)S(1)} collective-permute-done((bf16[1,112,1920]{2,1,0:T(8,128)(2,1)S(1)}, bf16[1,112,1920]{2,1,0:T(8,128)(2,1)S(1)}, u32[]{:S(2)}, u32[]{:S(2)}) %collective-permute-start.14) | collective-permute-done | bytes 430112 | tf_op jit(solution)/shard_map/ppermute | solution.py:465
  107.1 20.8 %collective-permute-done.45 = bf16[1,112,2432]{2,1,0:T(8,128)(2,1)S(1)} collective-permute-done((bf16[1,112,2432]{2,1,0:T(8,128)(2,1)S(1)}, bf16[1,112,2432]{2,1,0:T(8,128)(2,1)S(1)}, u32[]{:S(2)}, u32[]{:S(2)}) %collective-permute-start.45) | collective-permute-done | bytes 544800 | tf_op jit(solution)/shard_map/ppermute | solution.py:465
  224.6 28.6 %collective-permute-done.12.refs_3_ = bf16[4,112,1920]{2,1,0:T(8,128)(2,1)S(1)} collective-permute-done((bf16[4,112,1920]{2,1,0:T(8,128)(2,1)}, bf16[4,112,1920]{2,1,0:T(8,128)(2,1)S(1)}, u32[]{:S(2)}, u32[]{:S(2)}) %collective-permute-start.12) | collective-permute-done | bytes 1720352 | tf_op jit(solution)/shard_map/ppermute | solution.py:465
  287.5 18.8 %convolution_convert_fusion.3 = bf16[1024,3840]{1,0:T(8,128)(2,1)} fusion(bf16[1792,3840]{1,0:T(8,128)(2,1)} %shard_map.308, f32[1792]{0:T(1024)S(1)} %get-tuple-element.110, f32[1024]{0:T(1024)S(1)} %bitcast.240, bf16[1024,896]{1,0:T(8,128)(2,1)S(1)} %bitcast.180, bf16[1024,896]{1,0:T(8,128)(2,1)S(1)} %bitcast.184), kind=kOutput, calls=%fused_computation.25 | convolution fusion | flops 14109638656 | bytes 25308160 | tf_op jit(solution)/shard_map/dot_general | solution.py:26
  388.9 34.7 %collective-permute-start.66 = (bf16[2,112,1152]{2,1,0:T(8,128)(2,1)}, bf16[2,112,1152]{2,1,0:T(8,128)(2,1)}, u32[]{:S(2)}, u32[]{:S(2)}) collective-permute-start(bf16[2,112,1152]{2,1,0:T(8,128)(2,1)} %pad_maximum_fusion.14.refs_8_), channel_id=1, source_target_pairs={{0,16},{2,18},{4,20},{6,22},{8,24},{10,26},{12,28},{14,30},{16,0},... | collective-permute-start | bytes 1548296 | tf_op jit(solution)/shard_map/ppermute | solution.py:465
  423.5 20.0 %collective-permute-done.33 = bf16[2,8,160,128]{3,2,1,0:T(8,128)(2,1)S(1)} collective-permute-done((bf16[2,8,160,128]{3,2,1,0:T(8,128)(2,1)S(1)}, bf16[2,8,160,128]{3,2,1,0:T(8,128)(2,1)S(1)}, u32[]{:S(2)}, u32[]{:S(2)}) %collective-permute-start.33) | collective-permute-done | bytes 655392 | tf_op jit(solution)/shard_map/ppermute | solution.py:465
  454.3 18.4 %collective-permute-start.58 = (bf16[2,112,1280]{2,1,0:T(8,128)(2,1)S(1)}, bf16[2,112,1280]{2,1,0:T(8,128)(2,1)S(1)}, u32[]{:S(2)}, u32[]{:S(2)}) collective-permute-start(bf16[2,112,1280]{2,1,0:T(8,128)(2,1)S(1)} %copy-done.38), channel_id=1, source_target_pairs={{0,16},{2,18},{4,20},{6,22},{8,24},{10,26},{12,28},{14,30},{16,0},... | collective-permute-start | bytes 1720328 | tf_op jit(solution)/shard_map/ppermute | solution.py:465
  472.7 34.2 %shard_map.311 = (bf16[2,512,896]{2,1,0:T(8,128)(2,1)}, bf16[2,512,896]{2,1,0:T(8,128)(2,1)}, f32[2,512,128]{2,1,0:T(8,128)}) custom-call(s32[2,512,8]{2,1,0:T(8,128)} %copy.85.ic, s32[2,8,640]{2,1,0:T(8,128)} %pad_add_fusion.ir, bf16[2,512,3840]{2,1,0:T(8,128)(2,1)} %bitcast.165, bf16[2,512,3840]{2,1,0:T(8,128)(2,1)} %bitcast.166, ...), custom_call_target="tpu_custom_call" | custom-call | flops 10000000000 | bytes 12582912 | tf_op jit(solution)/shard_map/pallas_call | solution.py:325
  521.5 48.6 %collective-permute-done.71.refs_15_ = bf16[2,112,1152]{2,1,0:T(8,128)(2,1)S(1)} collective-permute-done((bf16[2,112,1152]{2,1,0:T(8,128)(2,1)}, bf16[2,112,1152]{2,1,0:T(8,128)(2,1)S(1)}, u32[]{:S(2)}, u32[]{:S(2)}) %collective-permute-start.71) | collective-permute-done | bytes 516128 | tf_op jit(solution)/shard_map/ppermute | solution.py:465
  636.9 27.7 %collective-permute-done.54.refs_6_ = bf16[4,112,2432]{2,1,0:T(8,128)(2,1)} collective-permute-done((bf16[4,112,2432]{2,1,0:T(8,128)(2,1)}, bf16[4,112,2432]{2,1,0:T(8,128)(2,1)}, u32[]{:S(2)}, u32[]{:S(2)}) %collective-permute-start.54) | collective-permute-done | bytes 2179104 | tf_op jit(solution)/shard_map/ppermute | solution.py:465
  668.4 38.8 %collective-permute-done.55.refs_7_ = bf16[4,112,2432]{2,1,0:T(8,128)(2,1)} collective-permute-done((bf16[4,112,2432]{2,1,0:T(8,128)(2,1)}, bf16[4,112,2432]{2,1,0:T(8,128)(2,1)}, u32[]{:S(2)}, u32[]{:S(2)}) %collective-permute-start.55) | collective-permute-done | bytes 2179104 | tf_op jit(solution)/shard_map/ppermute | solution.py:465
  727.2 25.3 %convolution_convert_fusion.2 = bf16[1024,4864]{1,0:T(8,128)(2,1)} fusion(bf16[1792,4864]{1,0:T(8,128)(2,1)} %shard_map.313, f32[1024,1792]{1,0:T(8,128)S(1)} %get-tuple-element.146, f32[1792]{0:T(1024)S(1)} %copy-done.100, f32[1024]{0:T(1024)S(1)} %add_rsqrt_fusion), kind=kOutput, calls=%fused_computation.18 | convolution fusion | flops 17861443584 | bytes 34745344 | tf_op jit(solution)/shard_map/dot_general | solution.py:26
  752.4 18.1 convolution_convert_fusion.4
  770.5 18.7 %fusion.2 = (bf16[1024,2432]{1,0:T(8,128)(2,1)}, bf16[1024,2432]{1,0:T(8,128)(2,1)}) fusion(bf16[1024,4864]{1,0:T(8,128)(2,1)} %convolution_convert_fusion.2, bf16[1024,1792]{1,0:T(8,128)(2,1)S(1)} %bitcast.210, bf16[1792,2432]{1,0:T(8,128)(2,1)} %shard_map.314), kind=kOutput, calls=%fused_computation.10 | convolution fusion | flops 8962834432 | bytes 32309248 | tf_op jit(solution)/shard_map/dot_general | solution.py:26
  805.7 42.1 %fusion.17 = bf16[1024,1792]{1,0:T(8,128)(2,1)} fusion(bf16[1792,4864]{1,0:T(8,128)(2,1)} %shard_map.313, bf16[1024,2432]{1,0:T(8,128)(2,1)} %get-tuple-element.148, bf16[1024,2432]{1,0:T(8,128)(2,1)} %get-tuple-element.147), kind=kOutput, calls=%fused_computation.61 | convolution fusion | flops 17872715776 | bytes 31064064 | tf_op jit(solution)/shard_map/dot_general | solution.py:30
  847.9 27.7 %convolution_convert_fusion = bf16[1792,4864]{1,0:T(8,128)(2,1)} fusion(bf16[1024,2432]{1,0:T(8,128)(2,1)} %get-tuple-element.148, bf16[1024,2432]{1,0:T(8,128)(2,1)} %get-tuple-element.147, f32[1024,1792]{1,0:T(8,128)} %copy-done, f32[1792]{0:T(1024)S(1)} %copy-done.100, f32[1024]{0:T(1024)S(1)} %add_rsqrt_fusion), kind=kOutput, calls=%fused_computation.1 | convolution fusion | flops 17885102080 | bytes 34745344 | tf_op jit(solution)/shard_map/dot_general | solution.py:34
  912.6 20.9 %collective-permute-done.125 = bf16[4,2,1,112,1152]{4,3,2,1,0:T(8,128)(2,1)} collective-permute-done((bf16[4,2,1,112,1152]{4,3,2,1,0:T(8,128)(2,1)}, bf16[4,2,1,112,1152]{4,3,2,1,0:T(8,128)(2,1)}, u32[]{:S(2)}, u32[]{:S(2)}) %collective-permute-start.125) | collective-permute-done | bytes 2064416 | tf_op jit(solution)/shard_map/ppermute | solution.py:465
  966.9 30.2 %collective-permute-done.127 = bf16[1,2,1,112,1152]{4,3,2,1,0:T(8,128)(2,1)S(1)} collective-permute-done((bf16[1,2,1,112,1152]{4,3,2,1,0:T(8,128)(2,1)S(1)}, bf16[1,2,1,112,1152]{4,3,2,1,0:T(8,128)(2,1)S(1)}, u32[]{:S(2)}, u32[]{:S(2)}) %collective-permute-start.127) | collective-permute-done | bytes 516128 | tf_op jit(solution)/shard_map/ppermute | solution.py:465
  1003.4 30.2 %collective-permute-done.122 = bf16[1,1,2,112,1280]{4,3,2,1,0:T(8,128)(2,1)S(1)} collective-permute-done((bf16[1,1,2,112,1280]{4,3,2,1,0:T(8,128)(2,1)S(1)}, bf16[1,1,2,112,1280]{4,3,2,1,0:T(8,128)(2,1)S(1)}, u32[]{:S(2)}, u32[]{:S(2)}) %collective-permute-start.122) | collective-permute-done | bytes 573472 | tf_op jit(solution)/shard_map/ppermute | solution.py:465
  1039.8 59.8 %collective-permute-done.124 = bf16[1,1,1,112,1280]{4,3,2,1,0:T(8,128)(2,1)S(1)} collective-permute-done((bf16[1,1,1,112,1280]{4,3,2,1,0:T(8,128)(2,1)S(1)}, bf16[1,1,1,112,1280]{4,3,2,1,0:T(8,128)(2,1)S(1)}, u32[]{:S(2)}, u32[]{:S(2)}) %collective-permute-start.124) | collective-permute-done | bytes 286752 | tf_op jit(solution)/shard_map/ppermute | solution.py:465
  1138.5 96.9 %shard_map.315 = (bf16[2,512,128]{2,1,0:T(8,128)(2,1)}, f32[2,512,128]{2,1,0:T(8,128)}, f32[2,512,896]{2,1,0:T(8,128)}, bf16[2,512,896]{2,1,0:T(8,128)(2,1)}, f3...) custom-call(s32[2,512,8]{2,1,0:T(8,128)} %copy.85.ic, ...), custom_call_target="tpu_custom_call" | custom-call | flops 20000000000 | bytes 42270720 | tf_op jit(solution)/shard_map/pallas_call | solution.py:325
  1301.1 35.7 %collective-permute-done.77 = bf16[2,8,160,128]{3,2,1,0:T(8,128)(2,1)} collective-permute-done((bf16[2,8,160,128]{3,2,1,0:T(8,128)(2,1)S(1)}, bf16[2,8,160,128]{3,2,1,0:T(8,128)(2,1)}, u32[]{:S(2)}, u32[]{:S(2)}) %collective-permute-start.77) | collective-permute-done | bytes 655392 | tf_op jit(solution)/shard_map/ppermute | solution.py:465
  1338.3 24.0 %collective-permute-start.80 = (bf16[2,8,160,128]{3,2,1,0:T(8,128)(2,1)S(1)}, bf16[2,8,160,128]{3,2,1,0:T(8,128)(2,1)S(1)}, u32[]{:S(2)}, u32[]{:S(2)}) collective-permute-start(bf16[2,8,160,128]{3,2,1,0:T(8,128)(2,1)S(1)} %fusion.48), channel_id=1, source_target_pairs={{0,24},{2,26},{4,28},{6,30},{8,0},{10,2},{12,4},{14,6},{16,8},{18,... | collective-permute-start | bytes 1966088 | tf_op jit(solution)/shard_map/ppermute | solution.py:465
  1379.6 39.5 %collective-permute-done.79 = bf16[2,8,160,128]{3,2,1,0:T(8,128)(2,1)S(1)} collective-permute-done((bf16[2,8,160,128]{3,2,1,0:T(8,128)(2,1)S(1)}, bf16[2,8,160,128]{3,2,1,0:T(8,128)(2,1)S(1)}, u32[]{:S(2)}, u32[]{:S(2)}) %collective-permute-start.79) | collective-permute-done | bytes 655392 | tf_op jit(solution)/shard_map/ppermute | solution.py:465
  1443.8 20.9 %bitcast_convert_fusion = bf16[1792,3840]{1,0:T(8,128)(2,1)} fusion(bf16[2,512,1792]{2,1,0:T(8,128)(2,1)S(1)} %copy-done.16, bf16[2,512,3840]{2,1,0:T(8,128)(2,1)} %shard_map.317), kind=kOutput, calls=%fused_computation | convolution fusion | flops 14099742720 | bytes 25296896 | tf_op jit(solution)/shard_map/dot_general | solution.py:34
  1464.7 22.5 %fusion.15 = bf16[1024,1792]{1,0:T(8,128)(2,1)} fusion(f32[2,512,1792]{2,1,0:T(8,128)} %convert_add_fusion.1, bf16[1024,3840]{1,0:T(8,128)(2,1)} %bitcast.212, bf16[1792,3840]{1,0:T(8,128)(2,1)} %shard_map.308), kind=kOutput, calls=%fused_computation.34 | convolution fusion | flops 14096531456 | bytes 32636928 | tf_op jit(solution)/shard_map/dot_general | solution.py:30
  1539.8 39.2 %collective-permute-done.109 = bf16[1,1,1,112,896]{4,3,2,1,0:T(8,128)(2,1)S(1)} collective-permute-done((bf16[1,1,1,112,896]{4,3,2,1,0:T(8,128)(2,1)S(1)}, bf16[1,1,1,112,896]{4,3,2,1,0:T(8,128)(2,1)S(1)}, u32[]{:S(2)}, u32[]{:S(2)}) %collective-permute-start.109) | collective-permute-done | bytes 200736 | tf_op jit(solution)/shard_map/ppermute | solution.py:465
  1633.4 23.0 %collective-permute-done.113 = bf16[1,1,1,112,2432]{4,3,2,1,0:T(8,128)(2,1)S(1)} collective-permute-done((bf16[1,1,1,112,2432]{4,3,2,1,0:T(8,128)(2,1)S(1)}, bf16[1,1,1,112,2432]{4,3,2,1,0:T(8,128)(2,1)S(1)}, u32[]{:S(2)}, u32[]{:S(2)}) %collective-permute-start.113) | collective-permute-done | bytes 544800 | tf_op jit(solution)/shard_map/ppermute | solution.py:465
  1686.6 34.9 %collective-permute-done.85 = f32[4,2,1,112,128]{4,3,2,1,0:T(8,128)S(1)} collective-permute-done((f32[4,2,1,112,128]{4,3,2,1,0:T(8,128)S(1)}, f32[4,2,1,112,128]{4,3,2,1,0:T(8,128)S(1)}, u32[]{:S(2)}, u32[]{:S(2)}) %collective-permute-start.85) | collective-permute-done | bytes 458784 | tf_op jit(solution)/shard_map/ppermute | solution.py:465
  1747.9 17.7 collective-permute-done.96
  1776.4 23.3 %collective-permute-done.93 = bf16[1,1,1,112,1920]{4,3,2,1,0:T(8,128)(2,1)S(1)} collective-permute-done((bf16[1,1,1,112,1920]{4,3,2,1,0:T(8,128)(2,1)S(1)}, bf16[1,1,1,112,1920]{4,3,2,1,0:T(8,128)(2,1)S(1)}, u32[]{:S(2)}, u32[]{:S(2)}) %collective-permute-start.93) | collective-permute-done | bytes 430112 | tf_op jit(solution)/shard_map/ppermute | solution.py:465
  1800.5 16.9 collective-permute-done.98
  (779 shorter events, 834.7 us)
Async XLA Ops:
  78.7 97.5 %collective-permute-start = (bf16[2,512,896]{2,1,0:T(8,128)(2,1)}, bf16[2,512,896]{2,1,0:T(8,128)(2,1)}, u32[]{:S(2)}, u32[]{:S(2)}) collective-permute-start(bf16[2,512,896]{2,1,0:T(8,128)(2,1)} %param.20), channel_id=1, source_target_pairs={{0,1},{1,0},{2,3},{3,2},{4,5},{5,4},{6,7},{7,6},{8,9},{9,8},{10,11... | collective-permute-start | bytes 5505032 | tf_op jit(solution)/shard_map/ppermute | solution.py:588
  91.9 85.9 %collective-permute-start.10 = (bf16[4,112,1920]{2,1,0:T(8,128)(2,1)}, bf16[4,112,1920]{2,1,0:T(8,128)(2,1)}, u32[]{:S(2)}, u32[]{:S(2)}) collective-permute-start(bf16[4,112,1920]{2,1,0:T(8,128)(2,1)} %pad_maximum_fusion.11.refs_0_), channel_id=1, source_target_pairs={{0,4},{2,6},{4,0},{6,2},{8,12},{10,14},{12,8},{14,10},{16,20},{18,... | collective-permute-start | bytes 5160968 | tf_op jit(solution)/shard_map/ppermute | solution.py:465
  93.4 85.8 %collective-permute-start.16 = (bf16[4,112,1920]{2,1,0:T(8,128)(2,1)S(1)}, bf16[4,112,1920]{2,1,0:T(8,128)(2,1)}, u32[]{:S(2)}, u32[]{:S(2)}) collective-permute-start(bf16[4,112,1920]{2,1,0:T(8,128)(2,1)S(1)} %pad_maximum_fusion.12.refs_4_), channel_id=1, source_target_pairs={{0,2},{2,0},{4,6},{6,4},{8,10},{10,8},{12,14},{14,12},{16,18},{18,... | collective-permute-start | bytes 5160968 | tf_op jit(solution)/shard_map/ppermute | solution.py:465
  177.7 75.4 %collective-permute-start.12 = (bf16[4,112,1920]{2,1,0:T(8,128)(2,1)}, bf16[4,112,1920]{2,1,0:T(8,128)(2,1)S(1)}, u32[]{:S(2)}, u32[]{:S(2)}) collective-permute-start(bf16[4,112,1920]{2,1,0:T(8,128)(2,1)} %collective-permute-done.10.refs_1_), channel_id=1, source_target_pairs={{0,2},{2,0},{4,6},{6,4},{8,10},{10,8},{12,14},{14,12},{16,18},{18,... | collective-permute-start | bytes 5160968 | tf_op jit(solution)/shard_map/ppermute | solution.py:465
  179.2 75.7 %collective-permute-start.18 = (bf16[4,112,1920]{2,1,0:T(8,128)(2,1)}, bf16[4,112,1920]{2,1,0:T(8,128)(2,1)}, u32[]{:S(2)}, u32[]{:S(2)}) collective-permute-start(bf16[4,112,1920]{2,1,0:T(8,128)(2,1)} %collective-permute-done.16.refs_5_), channel_id=1, source_target_pairs={{0,4},{2,6},{4,0},{6,2},{8,12},{10,14},{12,8},{14,10},{16,20},{18,... | collective-permute-start | bytes 5160968 | tf_op jit(solution)/shard_map/ppermute | solution.py:465
  203.1 67.7 %collective-permute-start.39 = (bf16[2,112,896]{2,1,0:T(8,128)(2,1)S(1)}, bf16[2,112,896]{2,1,0:T(8,128)(2,1)S(1)}, u32[]{:S(2)}, u32[]{:S(2)}) collective-permute-start(bf16[2,112,896]{2,1,0:T(8,128)(2,1)S(1)} %pad_maximum_fusion.22.refs_0_), channel_id=1, source_target_pairs={{0,2},{2,0},{4,6},{6,4},{8,10},{10,8},{12,14},{14,12},{16,18},{18,... | collective-permute-start | bytes 1204232 | tf_op jit(solution)/shard_map/ppermute | solution.py:465
  327.3 124.6 %collective-permute-start.68 = (bf16[2,112,1152]{2,1,0:T(8,128)(2,1)}, bf16[2,112,1152]{2,1,0:T(8,128)(2,1)S(1)}, u32[]{:S(2)}, u32[]{:S(2)}) collective-permute-start(bf16[2,112,1152]{2,1,0:T(8,128)(2,1)} %pad_maximum_fusion.14.refs_8_), channel_id=1, source_target_pairs={{0,2},{2,0},{4,6},{6,4},{8,10},{10,8},{12,14},{14,12},{16,18},{18,... | collective-permute-start | bytes 1548296 | tf_op jit(solution)/shard_map/ppermute | solution.py:465
  336.0 116.7 %collective-permute-start.67 = (bf16[2,112,1152]{2,1,0:T(8,128)(2,1)}, bf16[2,112,1152]{2,1,0:T(8,128)(2,1)}, u32[]{:S(2)}, u32[]{:S(2)}) collective-permute-start(bf16[2,112,1152]{2,1,0:T(8,128)(2,1)} %pad_maximum_fusion.14.refs_8_), channel_id=1, source_target_pairs={{0,8},{2,10},{4,12},{6,14},{8,16},{10,18},{12,20},{14,22},{16,24},... | collective-permute-start | bytes 1548296 | tf_op jit(solution)/shard_map/ppermute | solution.py:465
  373.7 69.9 %collective-permute-start.33 = (bf16[2,8,160,128]{3,2,1,0:T(8,128)(2,1)S(1)}, bf16[2,8,160,128]{3,2,1,0:T(8,128)(2,1)S(1)}, u32[]{:S(2)}, u32[]{:S(2)}) collective-permute-start(bf16[2,8,160,128]{3,2,1,0:T(8,128)(2,1)S(1)} %fusion.39), channel_id=1, source_target_pairs={{0,16},{2,18},{4,20},{6,22},{8,24},{10,26},{12,28},{14,30},{16,0},... | collective-permute-start | bytes 1966088 | tf_op jit(solution)/shard_map/ppermute | solution.py:465
  374.7 71.8 %collective-permute-start.32 = (bf16[2,8,160,128]{3,2,1,0:T(8,128)(2,1)S(1)}, bf16[2,8,160,128]{3,2,1,0:T(8,128)(2,1)S(1)}, u32[]{:S(2)}, u32[]{:S(2)}) collective-permute-start(bf16[2,8,160,128]{3,2,1,0:T(8,128)(2,1)S(1)} %fusion.39), channel_id=1, source_target_pairs={{0,8},{2,10},{4,12},{6,14},{8,16},{10,18},{12,20},{14,22},{16,24},... | collective-permute-start | bytes 1966088 | tf_op jit(solution)/shard_map/ppermute | solution.py:465
  388.9 118.1 %collective-permute-start.66 = (bf16[2,112,1152]{2,1,0:T(8,128)(2,1)}, bf16[2,112,1152]{2,1,0:T(8,128)(2,1)}, u32[]{:S(2)}, u32[]{:S(2)}) collective-permute-start(bf16[2,112,1152]{2,1,0:T(8,128)(2,1)} %pad_maximum_fusion.14.refs_8_), channel_id=1, source_target_pairs={{0,16},{2,18},{4,20},{6,22},{8,24},{10,26},{12,28},{14,30},{16,0},... | collective-permute-start | bytes 1548296 | tf_op jit(solution)/shard_map/ppermute | solution.py:465
  508.5 109.8 %collective-permute-start.53 = (bf16[4,112,2432]{2,1,0:T(8,128)(2,1)}, bf16[4,112,2432]{2,1,0:T(8,128)(2,1)}, u32[]{:S(2)}, u32[]{:S(2)}) collective-permute-start(bf16[4,112,2432]{2,1,0:T(8,128)(2,1)} %pad_maximum_fusion.10.refs_4_), channel_id=1, source_target_pairs={{0,2},{2,0},{4,6},{6,4},{8,10},{10,8},{12,14},{14,12},{16,18},{18,... | collective-permute-start | bytes 6537224 | tf_op jit(solution)/shard_map/ppermute | solution.py:465
  508.5 111.6 %collective-permute-start.47 = (bf16[4,112,2432]{2,1,0:T(8,128)(2,1)}, bf16[4,112,2432]{2,1,0:T(8,128)(2,1)}, u32[]{:S(2)}, u32[]{:S(2)}) collective-permute-start(bf16[4,112,2432]{2,1,0:T(8,128)(2,1)} %pad_maximum_fusion.9.refs_0_), channel_id=1, source_target_pairs={{0,4},{2,6},{4,0},{6,2},{8,12},{10,14},{12,8},{14,10},{16,20},{18,... | collective-permute-start | bytes 6537224 | tf_op jit(solution)/shard_map/ppermute | solution.py:465
  521.5 198.5 %collective-permute-start.43 = (bf16[1024,1792]{1,0:T(8,128)(2,1)}, bf16[1024,1792]{1,0:T(8,128)(2,1)}, u32[]{:S(2)}, u32[]{:S(2)}) collective-permute-start(bf16[1024,1792]{1,0:T(8,128)(2,1)} %convolution_convert_fusion.5), channel_id=1, source_target_pairs={{0,1},{1,0},{2,3},{3,2},{4,5},{5,4},{6,7},{7,6},{8,9},{9,8},{10,11... | collective-permute-start | bytes 11010056 | tf_op jit(solution)/shard_map/ppermute | solution.py:588
  618.3 88.9 %collective-permute-start.55 = (bf16[4,112,2432]{2,1,0:T(8,128)(2,1)}, bf16[4,112,2432]{2,1,0:T(8,128)(2,1)}, u32[]{:S(2)}, u32[]{:S(2)}) collective-permute-start(bf16[4,112,2432]{2,1,0:T(8,128)(2,1)} %collective-permute-done.53.refs_5_), channel_id=1, source_target_pairs={{0,4},{2,6},{4,0},{6,2},{8,12},{10,14},{12,8},{14,10},{16,20},{18,... | collective-permute-start | bytes 6537224 | tf_op jit(solution)/shard_map/ppermute | solution.py:465
  620.1 87.1 %collective-permute-start.49 = (bf16[4,112,2432]{2,1,0:T(8,128)(2,1)}, bf16[4,112,2432]{2,1,0:T(8,128)(2,1)}, u32[]{:S(2)}, u32[]{:S(2)}) collective-permute-start(bf16[4,112,2432]{2,1,0:T(8,128)(2,1)} %collective-permute-done.47.refs_1_), channel_id=1, source_target_pairs={{0,2},{2,0},{4,6},{6,4},{8,10},{10,8},{12,14},{14,12},{16,18},{18,... | collective-permute-start | bytes 6537224 | tf_op jit(solution)/shard_map/ppermute | solution.py:465
  884.4 216.4 %collective-permute-start.74 = (bf16[1024,1792]{1,0:T(8,128)(2,1)}, bf16[1024,1792]{1,0:T(8,128)(2,1)}, u32[]{:S(2)}, u32[]{:S(2)}) collective-permute-start(bf16[1024,1792]{1,0:T(8,128)(2,1)} %fusion.17), channel_id=1, source_target_pairs={{0,1},{1,0},{2,3},{3,2},{4,5},{5,4},{6,7},{7,6},{8,9},{9,8},{10,11... | collective-permute-start | bytes 11010056 | tf_op jit(solution)/shard_map/ppermute | solution.py:588
  899.9 388.6 %collective-permute-start.115 = (bf16[4,1,2,112,2432]{4,3,2,1,0:T(8,128)(2,1)}, bf16[4,1,2,112,2432]{4,3,2,1,0:T(8,128)(2,1)}, u32[]{:S(2)}, u32[]{:S(2)}) collective-permute-start(bf16[4,1,2,112,2432]{4,3,2,1,0:T(8,128)(2,1)} %constant_dynamic-slice_fusion.14), channel_id=1, source_target_pairs={{0,4},{2,6},{4,0},{6,2},{8,12},{10,14},{12,8},{14,10},{16,20},{18,... | collective-permute-start | bytes 13074440 | tf_op jit(solution)/shard_map/ppermute | solution.py:465
  997.5 295.2 %collective-permute-start.110 = (bf16[4,2,1,112,2432]{4,3,2,1,0:T(8,128)(2,1)}, bf16[4,2,1,112,2432]{4,3,2,1,0:T(8,128)(2,1)}, u32[]{:S(2)}, u32[]{:S(2)}) collective-permute-start(bf16[4,2,1,112,2432]{4,3,2,1,0:T(8,128)(2,1)} %constant_dynamic-slice_fusion.19), channel_id=1, source_target_pairs={{0,2},{2,0},{4,6},{6,4},{8,10},{10,8},{12,14},{14,12},{16,18},{18,... | collective-permute-start | bytes 13074440 | tf_op jit(solution)/shard_map/ppermute | solution.py:465
  1135.0 147.1 %collective-permute-start.76 = (bf16[2,8,160,128]{3,2,1,0:T(8,128)(2,1)}, bf16[2,8,160,128]{3,2,1,0:T(8,128)(2,1)S(1)}, u32[]{:S(2)}, u32[]{:S(2)}) collective-permute-start(bf16[2,8,160,128]{3,2,1,0:T(8,128)(2,1)} %shard_map.316), channel_id=1, source_target_pairs={{0,2},{2,0},{4,6},{6,4},{8,10},{10,8},{12,14},{14,12},{16,18},{18,... | collective-permute-start | bytes 1966088 | tf_op jit(solution)/shard_map/ppermute | solution.py:465
  1137.2 225.1 %collective-permute-start.105 = (bf16[4,2,1,112,896]{4,3,2,1,0:T(8,128)(2,1)}, bf16[4,2,1,112,896]{4,3,2,1,0:T(8,128)(2,1)}, u32[]{:S(2)}, u32[]{:S(2)}) collective-permute-start(bf16[4,2,1,112,896]{4,3,2,1,0:T(8,128)(2,1)} %constant_dynamic-slice_fusion.24), channel_id=1, source_target_pairs={{0,2},{2,0},{4,6},{6,4},{8,10},{10,8},{12,14},{14,12},{16,18},{18,... | collective-permute-start | bytes 4816904 | tf_op jit(solution)/shard_map/ppermute | solution.py:465
  1280.5 141.7 %collective-permute-start.81 = (bf16[2,64,896]{2,1,0:T(8,128)(2,1)}, bf16[2,64,896]{2,1,0:T(8,128)(2,1)}, u32[]{:S(2)}, u32[]{:S(2)}) collective-permute-start(bf16[2,64,896]{2,1,0:T(8,128)(2,1)} %get-tuple-element.37), channel_id=1, source_target_pairs={{2,0},{4,2},{6,4},{8,6},{10,8},{12,10},{14,12},{16,14},{18,16},{20... | collective-permute-start | bytes 688136 | tf_op jit(solution)/shard_map/ppermute | solution.py:604
  1282.1 84.3 %collective-permute-start.100 = (bf16[4,1,2,112,896]{4,3,2,1,0:T(8,128)(2,1)}, bf16[4,1,2,112,896]{4,3,2,1,0:T(8,128)(2,1)}, u32[]{:S(2)}, u32[]{:S(2)}) collective-permute-start(bf16[4,1,2,112,896]{4,3,2,1,0:T(8,128)(2,1)} %constant_dynamic-slice_fusion.29), channel_id=1, source_target_pairs={{0,4},{2,6},{4,0},{6,2},{8,12},{10,14},{12,8},{14,10},{16,20},{18,... | collective-permute-start | bytes 4816904 | tf_op jit(solution)/shard_map/ppermute | solution.py:465
  1377.5 151.4 %collective-permute-start.116 = (bf16[4,1,1,112,2432]{4,3,2,1,0:T(8,128)(2,1)}, bf16[4,1,1,112,2432]{4,3,2,1,0:T(8,128)(2,1)}, u32[]{:S(2)}, u32[]{:S(2)}) collective-permute-start(bf16[4,1,1,112,2432]{4,3,2,1,0:T(8,128)(2,1)} %constant_dynamic-slice_fusion.13), channel_id=1, source_target_pairs={{0,2},{2,0},{4,6},{6,4},{8,10},{10,8},{12,14},{14,12},{16,18},{18,... | collective-permute-start | bytes 6537224 | tf_op jit(solution)/shard_map/ppermute | solution.py:465
  1419.1 118.3 %collective-permute-start.111 = (bf16[4,1,1,112,2432]{4,3,2,1,0:T(8,128)(2,1)}, bf16[4,1,1,112,2432]{4,3,2,1,0:T(8,128)(2,1)}, u32[]{:S(2)}, u32[]{:S(2)}) collective-permute-start(bf16[4,1,1,112,2432]{4,3,2,1,0:T(8,128)(2,1)} %constant_dynamic-slice_fusion.18), channel_id=1, source_target_pairs={{0,4},{2,6},{4,0},{6,2},{8,12},{10,14},{12,8},{14,10},{16,20},{18,... | collective-permute-start | bytes 6537224 | tf_op jit(solution)/shard_map/ppermute | solution.py:465
  1419.6 73.8 %collective-permute-start.106 = (bf16[1,2,1,112,896]{4,3,2,1,0:T(8,128)(2,1)}, bf16[1,2,1,112,896]{4,3,2,1,0:T(8,128)(2,1)}, u32[]{:S(2)}, u32[]{:S(2)}) collective-permute-start(bf16[1,2,1,112,896]{4,3,2,1,0:T(8,128)(2,1)} %get-tuple-element.180), channel_id=1, source_target_pairs={{0,8},{2,10},{4,12},{6,14},{8,16},{10,18},{12,20},{14,22},{16,24},... | collective-permute-start | bytes 1204232 | tf_op jit(solution)/shard_map/ppermute | solution.py:465
  1422.2 71.2 %collective-permute-start.108 = (bf16[1,2,1,112,896]{4,3,2,1,0:T(8,128)(2,1)}, bf16[1,2,1,112,896]{4,3,2,1,0:T(8,128)(2,1)}, u32[]{:S(2)}, u32[]{:S(2)}) collective-permute-start(bf16[1,2,1,112,896]{4,3,2,1,0:T(8,128)(2,1)} %get-tuple-element.181), channel_id=1, source_target_pairs={{0,24},{2,26},{4,28},{6,30},{8,0},{10,2},{12,4},{14,6},{16,8},{18,... | collective-permute-start | bytes 1204232 | tf_op jit(solution)/shard_map/ppermute | solution.py:465
  1426.0 71.3 %collective-permute-start.107 = (bf16[1,2,1,112,896]{4,3,2,1,0:T(8,128)(2,1)}, bf16[1,2,1,112,896]{4,3,2,1,0:T(8,128)(2,1)}, u32[]{:S(2)}, u32[]{:S(2)}) collective-permute-start(bf16[1,2,1,112,896]{4,3,2,1,0:T(8,128)(2,1)} %get-tuple-element.182), channel_id=1, source_target_pairs={{0,16},{2,18},{4,20},{6,22},{8,24},{10,26},{12,28},{14,30},{16,0},... | collective-permute-start | bytes 1204232 | tf_op jit(solution)/shard_map/ppermute | solution.py:465
  1507.5 150.2 %collective-permute-start.90 = (bf16[4,1,2,112,1920]{4,3,2,1,0:T(8,128)(2,1)}, bf16[4,1,2,112,1920]{4,3,2,1,0:T(8,128)(2,1)}, u32[]{:S(2)}, u32[]{:S(2)}) collective-permute-start(bf16[4,1,2,112,1920]{4,3,2,1,0:T(8,128)(2,1)} %constant_dynamic-slice_fusion.39), channel_id=1, source_target_pairs={{0,4},{2,6},{4,0},{6,2},{8,12},{10,14},{12,8},{14,10},{16,20},{18,... | collective-permute-start | bytes 10321928 | tf_op jit(solution)/shard_map/ppermute | solution.py:465
  1510.8 163.0 %collective-permute-start.83 = (bf16[1024,1792]{1,0:T(8,128)(2,1)S(1)}, bf16[1024,1792]{1,0:T(8,128)(2,1)S(1)}, u32[]{:S(2)}, u32[]{:S(2)}) collective-permute-start(bf16[1024,1792]{1,0:T(8,128)(2,1)S(1)} %copy-done.23), channel_id=1, source_target_pairs={{0,1},{1,0},{2,3},{3,2},{4,5},{5,4},{6,7},{7,6},{8,9},{9,8},{10,11... | collective-permute-start | bytes 11010056 | tf_op jit(solution)/shard_map/ppermute | solution.py:588
  1595.1 87.2 %collective-permute-start.95 = (bf16[4,2,1,112,1920]{4,3,2,1,0:T(8,128)(2,1)}, bf16[4,2,1,112,1920]{4,3,2,1,0:T(8,128)(2,1)}, u32[]{:S(2)}, u32[]{:S(2)}) collective-permute-start(bf16[4,2,1,112,1920]{4,3,2,1,0:T(8,128)(2,1)} %constant_dynamic-slice_fusion.34), channel_id=1, source_target_pairs={{0,2},{2,0},{4,6},{6,4},{8,10},{10,8},{12,14},{14,12},{16,18},{18,... | collective-permute-start | bytes 10321928 | tf_op jit(solution)/shard_map/ppermute | solution.py:465
  1662.0 78.7 %collective-permute-start.91 = (bf16[4,1,1,112,1920]{4,3,2,1,0:T(8,128)(2,1)}, bf16[4,1,1,112,1920]{4,3,2,1,0:T(8,128)(2,1)}, u32[]{:S(2)}, u32[]{:S(2)}) collective-permute-start(bf16[4,1,1,112,1920]{4,3,2,1,0:T(8,128)(2,1)} %constant_dynamic-slice_fusion.38), channel_id=1, source_target_pairs={{0,2},{2,0},{4,6},{6,4},{8,10},{10,8},{12,14},{14,12},{16,18},{18,... | collective-permute-start | bytes 5160968 | tf_op jit(solution)/shard_map/ppermute | solution.py:465
  (256 other events, 9058.5 us)

commit v2 on v1

--- a/solution.py
+++ b/solution.py
@@ -19,7 +19,12 @@
 
 f32 = jnp.float32
 bf16 = jnp.bfloat16
-VMEM_BYTES = 56 * 1024 * 1024
+VMEM_BYTES = 60 * 1024 * 1024
+MESH = pl.DeviceIdType.MESH
+
+ZYX, ZXY, XZY, YZX, XYZ, YXZ = (0, 1, 2), (0, 2, 1), (2, 0, 1), (1, 0, 2), (2, 1, 0), (1, 2, 0)
+FIRST = [(ZXY, 4), (ZXY, 5), (ZYX, 3), (ZXY, 4), (YZX, 3), (ZYX, 3), (ZXY, 5), (ZYX, 5), (YXZ, 4), (XZY, 5), (ZYX, 4)]
+LAST = [(XZY, 5), (ZXY, 5), (YXZ, 3), (ZYX, 7), (YZX, 3), (ZYX, 3), (ZXY, 4), (ZYX, 3)]
 
 
 def mul(a, b):
@@ -449,7 +454,283 @@
 
 
 def coords(index, dims):
-    return tuple((index // st) % d for st, d in zip(strides(dims), dims))
+    return tuple(lax.rem(lax.div(index, st), d) for st, d in zip(strides(dims), dims))
+
+
+def partner(here, dims, axis, shift):
+    me = sum(c * st for c, st in zip(here, strides(dims)))
+    moved = lax.rem(here[axis] + shift, dims[axis])
+    return me + (moved - here[axis]) * strides(dims)[axis]
+
+
+def chunk_plan(widths, shares):
+    total, whole = sum(share for _, share in shares), sum(widths)
+    plan, done, used = [], 0, 0
+    for order, share in shares:
+        done += share
+        end = whole if done == total else whole * done // total // LANES * LANES
+        base = 0
+        for w, width in enumerate(widths):
+            first, last = max(used, base) - base, min(end, base + width) - base
+            if last > first:
+                plan.append((w, first, last, order))
+            base += width
+        used = end
+    return plan
+
+
+def transfer_script(plan, dims, depth, gather):
+    queues, script, now = [[], [], []], [], 0
+
+    def start(k, phase):
+        _, first, last, order = plan[k]
+        size = dims[order[phase]]
+        blocks = math.prod([dims[a] for a in (order[:phase] if gather else order[phase + 1 :])])
+        work = blocks * (last - first) * ((size + 1) // 2) * (size // 2) + 400
+        queues[order[phase]].append([work, k, phase])
+        script.append((True, k, phase))
+
+    def fill():
+        nonlocal now
+        while now < len(plan) and len(queues[plan[now][3][0]]) < depth:
+            start(now, 0)
+            now += 1
+
+    fill()
+    while any(queues):
+        step = min(queue[0][0] for queue in queues if queue)
+        ended = []
+        for queue in queues:
+            if queue:
+                queue[0][0] -= step
+                if queue[0][0] <= 0:
+                    ended.append(queue.pop(0))
+        for _, k, phase in ended:
+            script.append((False, k, phase))
+            if phase < 2:
+                start(k, phase + 1)
+        fill()
+    return script
+
+
+def greet(here, dims, head):
+    barrier = pltpu.get_barrier_semaphore()
+    count = 0
+    for axis, size in enumerate(dims):
+        for shift in range(1, size):
+            pl.semaphore_signal(
+                barrier,
+                inc=1,
+                device_id=(partner(here, dims, axis, shift), head),
+                device_id_type=MESH,
+            )
+            count += 1
+    pl.semaphore_wait(barrier, count)
+
+
+def gather_kernel(dims, plan, depth, count, later, *refs):
+    shards, passed = refs[:count], refs[count : count + later]
+    outs = refs[count + later : 2 * count + later]
+    handed = refs[2 * count + later : 2 * (count + later)]
+    own_sem, send, recv = refs[2 * (count + later) :]
+    here = coords(lax.axis_index("seq"), dims)
+    head = lax.axis_index("head")
+    per_chunk = sum(d - 1 for d in dims)
+    greet(here, dims, head)
+    owns = [
+        pltpu.make_async_copy(shards[w], outs[w].at[here], own_sem.at[w]) for w in range(count)
+    ] + [pltpu.make_async_copy(passed[i], handed[i], own_sem.at[count + i]) for i in range(later)]
+    started = {}
+
+    def start(k, phase):
+        w, c0, c1, order = plan[k]
+        axis, known = order[phase], order[:phase]
+        cols = pl.ds(c0, c1 - c0)
+        index = tuple(pl.ds(0, dims[a]) if a in known else here[a] for a in range(3))
+        dst = outs[w].at[index + (slice(None), cols)]
+        src = shards[w].at[:, cols] if phase == 0 else dst
+        at = k * per_chunk + sum(dims[a] - 1 for a in known)
+        started[k, phase] = [
+            pltpu.make_async_remote_copy(
+                src_ref=src,
+                dst_ref=dst,
+                send_sem=send.at[at + shift - 1],
+                recv_sem=recv.at[at + shift - 1],
+                device_id=(partner(here, dims, axis, shift), head),
+                device_id_type=MESH,
+            )
+            for shift in range(1, dims[axis])
+        ]
+        for copy in started[k, phase]:
+            copy.start()
+
+    for own in owns:
+        own.start()
+    placed = False
+    for begins, k, phase in transfer_script(plan, dims, depth, True):
+        if begins and phase > 0 and not placed:
+            for own in owns:
+                own.wait()
+            placed = True
+        if begins:
+            start(k, phase)
+        else:
+            for copy in started[k, phase]:
+                copy.wait_recv()
+    for copies in started.values():
+        for copy in copies:
+            copy.wait_send()
+
+
+def gather_all(shards, later, plan, dims, depth, collective_id):
+    count = len(shards)
+    sems = len(plan) * sum(d - 1 for d in dims)
+    size = 2 * math.prod(dims) * sum(math.prod(s.shape) for s in shards)
+    made = pl.pallas_call(
+        functools.partial(gather_kernel, dims, plan, depth, count, len(later)),
+        in_specs=[pl.BlockSpec(memory_space=pltpu.VMEM)] * (count + len(later)),
+        out_specs=[pl.BlockSpec(memory_space=pl.ANY)] * (count + len(later)),
+        out_shape=[jax.ShapeDtypeStruct(dims + s.shape, s.dtype) for s in shards]
+        + [jax.ShapeDtypeStruct(s.shape, s.dtype) for s in later],
+        scratch_shapes=[
+            pltpu.SemaphoreType.DMA((count + len(later),)),
+            pltpu.SemaphoreType.DMA((sems,)),
+            pltpu.SemaphoreType.DMA((sems,)),
+        ],
+        compiler_params=pltpu.CompilerParams(
+            collective_id=collective_id, has_side_effects=True, vmem_limit_bytes=VMEM_BYTES
+        ),
+        cost_estimate=pl.CostEstimate(flops=0, bytes_accessed=10 * size, transcendentals=0),
+    )(*shards, *later)
+    return made[:count], made[count:]
+
+
+def scatter_kernel(dims, plan, depth, count, *refs):
+    grads, outs = refs[:count], refs[count : 2 * count]
+    rest = refs[2 * count :]
+    n = len(plan)
+    landed, sums = rest[: 3 * n], rest[3 * n : 4 * n]
+    own_sem, send, recv = rest[4 * n :]
+    here = coords(lax.axis_index("seq"), dims)
+    head = lax.axis_index("head")
+    per_chunk = sum(d - 1 for d in dims)
+    greet(here, dims, head)
+    started, owns = {}, {}
+
+    def slab(order, phase, place):
+        done = order[:phase]
+        return tuple(
+            place if a == order[phase] else (here[a] if a in done else pl.ds(0, dims[a]))
+            for a in range(3)
+        )
+
+    def start(k, phase):
+        w, c0, c1, order = plan[k]
+        axis = order[phase]
+        if phase == 0:
+            owns[k] = pltpu.make_async_copy(
+                grads[w].at[slab(order, 0, here[axis]) + (slice(None), pl.ds(c0, c1 - c0))],
+                sums[k],
+                own_sem.at[k],
+            )
+        made = []
+        for shift in range(1, dims[axis]):
+            there = lax.rem(here[axis] + shift, dims[axis])
+            if phase == 0:
+                src = grads[w].at[slab(order, 0, there) + (slice(None), pl.ds(c0, c1 - c0))]
+            else:
+                src = sums[k].at[sum_index(order, phase, there)]
+            at = k * per_chunk + sum(dims[a] - 1 for a in order[:phase]) + shift - 1
+            made.append(
+                pltpu.make_async_remote_copy(
+                    src_ref=src,
+                    dst_ref=landed[3 * k + phase].at[shift - 1],
+                    send_sem=send.at[at],
+                    recv_sem=recv.at[at],
+                    device_id=(partner(here, dims, axis, shift), head),
+                    device_id_type=MESH,
+                )
+            )
+        started[k, phase] = made
+        for copy in made:
+            copy.start()
+        if phase == 0:
+            owns[k].start()
+
+    def sum_index(order, phase, place):
+        left = [a for a in range(3) if a != order[0]]
+        done = order[1:phase]
+        return tuple(
+            place if a == order[phase] else (here[a] if a in done else pl.ds(0, dims[a]))
+            for a in left
+        )
+
+    def arrive(k, phase):
+        w, c0, c1, order = plan[k]
+        for copy in started[k, phase]:
+            copy.wait_recv()
+        if phase == 0:
+            owns[k].wait()
+        left = [a for a in range(3) if a not in order[: phase + 1]]
+        size = math.prod([dims[a] for a in left])
+
+        def add(b, carry):
+            places, stride = {}, size
+            for a in left:
+                stride = stride // dims[a]
+                places[a] = lax.rem(lax.div(b, stride), dims[a])
+            at = tuple(places.get(a, here[a]) for a in range(3) if a != order[0])
+            total = sums[k][at].astype(f32)
+            for j in range(dims[order[phase]] - 1):
+                arrived = landed[3 * k + phase][(j,) + tuple(places[a] for a in left)]
+                total = total + arrived.astype(f32)
+            if phase < 2:
+                sums[k][at] = total.astype(bf16)
+            else:
+                outs[w][:, c0:c1] = total
+            return carry
+
+        if size == 1:
+            add(0, 0)
+        else:
+            lax.fori_loop(0, size, add, 0)
+
+    for begins, k, phase in transfer_script(plan, dims, depth, False):
+        (start if begins else arrive)(k, phase)
+    for copies in started.values():
+        for copy in copies:
+            copy.wait_send()
+
+
+def scatter_all(grads, plan, dims, depth, collective_id):
+    count = len(grads)
+    sems = len(plan) * sum(d - 1 for d in dims)
+    rows = grads[0].shape[3]
+    landed, sums = [], []
+    for _, c0, c1, order in plan:
+        for phase, axis in enumerate(order):
+            left = tuple(dims[a] for a in range(3) if a not in order[: phase + 1])
+            landed.append(pltpu.VMEM((dims[axis] - 1,) + left + (rows, c1 - c0), bf16))
+        keep = tuple(dims[a] for a in range(3) if a != order[0])
+        sums.append(pltpu.VMEM(keep + (rows, c1 - c0), bf16))
+    size = 2 * math.prod(dims) * sum(g.shape[3] * g.shape[4] for g in grads)
+    return pl.pallas_call(
+        functools.partial(scatter_kernel, dims, plan, depth, count),
+        in_specs=[pl.BlockSpec(memory_space=pl.ANY)] * count,
+        out_specs=[pl.BlockSpec(memory_space=pltpu.VMEM)] * count,
+        out_shape=[jax.ShapeDtypeStruct(g.shape[3:], f32) for g in grads],
+        scratch_shapes=landed
+        + sums
+        + [
+            pltpu.SemaphoreType.DMA((len(plan),)),
+            pltpu.SemaphoreType.DMA((sems,)),
+            pltpu.SemaphoreType.DMA((sems,)),
+        ],
+        compiler_params=pltpu.CompilerParams(
+            collective_id=collective_id, has_side_effects=True, vmem_limit_bytes=VMEM_BYTES
+        ),
+        cost_estimate=pl.CostEstimate(flops=0, bytes_accessed=10 * size, transcendentals=0),
+    )(*grads)
 
 
 def ring_pairs(dims, axis, shift):
@@ -463,125 +744,6 @@
 
 def along(x, dims, axis, shift):
     return lax.ppermute(x, "seq", ring_pairs(dims, axis, shift))
-
-
-def gather_pieces(shard, order, dims):
-    pieces = [(shard[None], [(0, 0, 0)])]
-    for step, axis in enumerate(order):
-        arrived = []
-        for shift in range(1, dims[axis]):
-            for piece, offsets in pieces:
-                moved = [o[:axis] + (shift,) + o[axis + 1 :] for o in offsets]
-                arrived.append((along(piece, dims, axis, -shift), moved))
-        pieces = pieces + arrived
-        if step == 0 and len(pieces) > 1:
-            pieces = [
-                (
-                    jnp.concatenate([p for p, _ in pieces], axis=0),
-                    [o for _, offsets in pieces for o in offsets],
-                )
-            ]
-    return pieces
-
-
-def lay_kernel(dims, rows, plan, *refs):
-    ins, out, stage, taken, put = refs[: len(plan)], *refs[len(plan) :]
-    here = coords(lax.axis_index("seq"), dims)
-    loads, stores = [], []
-    for ref, (column, offsets) in zip(ins, plan):
-        for b, offset in enumerate(offsets):
-            there = sum(
-                lax.rem(c + o, d) * st for c, o, d, st in zip(here, offset, dims, strides(dims))
-            )
-            place = (pl.ds(pl.multiple_of(there * rows, rows), rows), pl.ds(column, ref.shape[2]))
-            k = len(loads)
-            loads.append(pltpu.make_async_copy(ref.at[b], stage.at[place], taken.at[k]))
-            stores.append(pltpu.make_async_copy(stage.at[place], out.at[place], put.at[k]))
-    for load in loads:
-        load.start()
-    for load, store in zip(loads, stores):
-        load.wait()
-        store.start()
-    for store in stores:
-        store.wait()
-
-
-def lay_blocks(pieces, dims):
-    blocks = jnp.concatenate([p for p, _ in pieces], axis=0)
-    known = [coords_place(o, dims) for _, offsets in pieces for o in offsets]
-    slot_of = jnp.asarray(np.argsort(np.array(known)), jnp.int32)
-    here = coords(lax.axis_index("seq"), dims)
-    there = coords(jnp.arange(math.prod(dims), dtype=jnp.int32), dims)
-    offset = [lax.rem(t - h + d, d) for t, h, d in zip(there, here, dims)]
-    return blocks[slot_of[coords_place(offset, dims)]].reshape(-1, blocks.shape[2])
-
-
-def coords_place(offset, dims):
-    return sum(o * st for o, st in zip(offset, strides(dims)))
-
-
-def lay_out(parts, dims):
-    plan, arrays, column = [], [], 0
-    for pieces in parts:
-        for piece, offsets in pieces:
-            plan.append((column, offsets))
-            arrays.append(piece)
-        column += pieces[0][0].shape[2]
-    rows = arrays[0].shape[1]
-    if rows % (2 * 8):
-        return jnp.concatenate([lay_blocks(pieces, dims) for pieces in parts], axis=1)
-    count = sum(len(offsets) for _, offsets in plan)
-    size = math.prod(dims) * rows * column * arrays[0].dtype.itemsize
-    return pl.pallas_call(
-        functools.partial(lay_kernel, dims, rows, plan),
-        in_specs=[pl.BlockSpec(memory_space=pl.ANY)] * len(arrays),
-        out_specs=pl.BlockSpec(memory_space=pl.ANY),
-        out_shape=jax.ShapeDtypeStruct((math.prod(dims) * rows, column), arrays[0].dtype),
-        scratch_shapes=[
-            pltpu.VMEM((math.prod(dims) * rows, column), arrays[0].dtype),
-            pltpu.SemaphoreType.DMA((count,)),
-            pltpu.SemaphoreType.DMA((count,)),
-        ],
-        compiler_params=pltpu.CompilerParams(vmem_limit_bytes=VMEM_BYTES),
-        cost_estimate=pl.CostEstimate(flops=0, bytes_accessed=2 * size, transcendentals=0),
-    )(*arrays)
-
-
-def gather_rows(shard, orders, dims):
-    total, used, parts = sum(share for _, share in orders), 0, []
-    columns, done = shard.shape[1], 0
-    for order, share in orders:
-        done += share
-        end = columns if done == total else columns * done // total // LANES * LANES
-        parts.append(gather_pieces(shard[:, used:end], order, dims))
-        used = end
-    return lay_out(parts, dims)
-
-
-def scatter_part(grad, order, dims):
-    rows = grad.shape[0] // math.prod(dims)
-    here = coords(lax.axis_index("seq"), dims)
-    x = grad.reshape(dims + (rows, grad.shape[1]))
-    for axis in order:
-        total = lax.dynamic_index_in_dim(x, here[axis], axis).astype(f32)
-        for shift in range(1, dims[axis]):
-            to = lax.rem(here[axis] + shift, dims[axis])
-            total = total + along(
-                lax.dynamic_index_in_dim(x, to, axis), dims, axis, shift
-            ).astype(f32)
-        x = total.astype(grad.dtype)
-    return total.reshape(rows, grad.shape[1])
-
-
-def scatter_rows(grad, orders, dims):
-    total, used, parts = sum(share for _, share in orders), 0, []
-    columns, done = grad.shape[1], 0
-    for order, share in orders:
-        done += share
-        end = columns if done == total else columns * done // total // LANES * LANES
-        parts.append(scatter_part(grad[:, used:end], order[::-1], dims))
-        used = end
-    return parts[0] if len(parts) == 1 else jnp.concatenate(parts, axis=1)
 
 
 def other_core(x):
@@ -698,21 +860,17 @@
     place = me * rows
     tables = feature_tables(half // HDIM)
     qk = w_query.shape[1]
-    ff = w_gate.shape[1]
-    zyx, zxy, xzy, yzx = (0, 1, 2), (0, 2, 1), (2, 0, 1), (1, 0, 2)
 
     small = jnp.concatenate([norm_gains, conv_filter], axis=0).T
     small = jnp.pad(small, ((0, 0), (0, LANES - small.shape[1])))
     pack_in = jnp.concatenate([w_value, w_wquery, w_wkey, w_conv_gate, w_query, w_key], axis=1)
-    pack_ff = jnp.concatenate([w_gate, w_up], axis=1)
-    wide = [(zyx, 1), (zxy, 1)]
-    narrow = [(xzy, 10), (yzx, 9)]
-    small_all = gather_rows(small, [(zyx, 1)], dims)
-    full_in = gather_rows(pack_in, wide, dims)
-    full_conv = gather_rows(w_conv_in, [(xzy, 1)], dims)
-    full_out = gather_rows(w_out.T, [(yzx, 1)], dims)
-    full_ff = gather_rows(pack_ff, wide, dims)
-    full_down = gather_rows(w_down.T, narrow, dims)
+    shards = (small, pack_in, w_conv_in, w_out.T, w_gate)
+    plan = chunk_plan([s.shape[1] for s in shards], FIRST)
+    fulls, later = gather_all(shards, (w_up, w_down.T), plan, dims, 3, 1)
+    small_all, full_in, full_conv, full_out, full_gate = [
+        full.reshape(-1, full.shape[-1]) for full in fulls
+    ]
+    full_up, full_down = [lax.all_gather(s, "seq", axis=0, tiled=True) for s in later]
     vectors = small_all[:, : norm_gains.shape[0] + KCONV].astype(f32).T
     gain1, gain2 = vectors[0:1], vectors[1:2]
     taps = vectors[2:]
@@ -783,13 +941,13 @@
 
     r2 = rsq(resid)
     h2 = (resid * r2 * gain2).astype(bf16)
-    gate_up = mul(h2, full_ff).astype(bf16)
-    gate, up = gate_up[:, :ff].astype(f32), gate_up[:, ff:].astype(f32)
+    gate = mul(h2, full_gate).astype(bf16).astype(f32)
+    up = mul(h2, full_up).astype(bf16).astype(f32)
     sig = 1.0 / (1.0 + jnp.exp(-gate))
     hidden = (gate * sig * up).astype(bf16)
     flat_cot = cot_low.reshape(micros * rows, width)
     grad_down = t_mul(flat_cot, hidden).astype(bf16)
-    sum_down = scatter_rows(grad_down, narrow, dims)
+    sum_down = lax.psum_scatter(grad_down, "seq", scatter_dimension=0, tiled=True).astype(f32)
     ffn = mul_t(hidden, full_down).astype(bf16)
 
     def pick(a, which):
@@ -802,16 +960,15 @@
     d_hidden = mul(flat_cot, full_down)
     d_gate = (d_hidden * up * (sig * (1.0 + gate * (1.0 - sig)))).astype(bf16)
     d_up = (d_hidden * (gate * sig)).astype(bf16)
-    d_ff = jnp.concatenate([d_gate, d_up], axis=1)
-    grad_ff = t_mul(h2, d_ff).astype(bf16)
-    sum_ff = scatter_rows(grad_ff, wide, dims)
-    d_h2 = core_sum(mul_t(d_ff, full_ff))
+    grad_gate = t_mul(h2, d_gate).astype(bf16)
+    grad_up = t_mul(h2, d_up).astype(bf16)
+    sum_gate = lax.psum_scatter(grad_gate, "seq", scatter_dimension=0, tiled=True).astype(f32)
+    d_h2 = core_sum(mul_t(d_gate, full_gate) + mul_t(d_up, full_up))
     d_resid, d_gain2 = norm_back(resid, r2, gain2, d_h2)
     d_resid = flat_cot.astype(f32) + d_resid
     d_resid_low = d_resid.astype(bf16)
 
     grad_out = t_mul(d_resid_low, flat_mixed).astype(bf16)
-    sum_out = scatter_rows(grad_out, [(yzx, 1)], dims)
     d_mixed = mul(d_resid_low, full_out).astype(bf16).reshape(micros, rows, half)
     d_prefix = prefix_gradient(ic, proj, half, d_mixed, linear, rden, tables)
     d_own = carry_over(d_prefix, starts, rows, dims, True)
@@ -822,7 +979,6 @@
     back_v = shifted(back_v, -1)
     flat_dci = dci.reshape(micros * rows, half)
     grad_conv = t_mul(flat_conv, flat_dci).astype(bf16)
-    sum_conv = scatter_rows(grad_conv, [(xzy, 1)], dims)
     d_conv = mul_t(flat_dci, full_conv).reshape(micros, rows, width)
     d_h1 = taps[0] * d_conv
     d_taps = [jnp.sum(d_conv * h1f, axis=(0, 1))]
@@ -839,7 +995,6 @@
         ic, proj, half, d_own, tables, dk, dv, dwk, dwq, dcg, dq, back_k, back_v
     ).reshape(micros * rows, -1)
     grad_in = t_mul(flat_h1, d_proj).astype(bf16)
-    sum_in = scatter_rows(grad_in, wide, dims)
     d_h1 = core_sum(d_h1.reshape(micros * rows, width) + mul_t(d_proj, full_in))
     d_x, d_gain1 = norm_back(
         x.reshape(micros * rows, width), r1.reshape(micros * rows, 1), gain1, d_h1
@@ -850,7 +1005,16 @@
     d_taps = d_taps + other_core(d_taps)
     d_small = jnp.concatenate([d_gain1[None], d_gain2[None], d_taps], axis=0).T
     d_small = jnp.pad(d_small, ((0, 0), (0, LANES - d_small.shape[1])))
-    sum_small = scatter_rows(d_small, [(zyx, 1)], dims).T
+    grads = [
+        g.astype(bf16).reshape(dims + (-1, g.shape[1]))
+        for g in (grad_up, grad_out, grad_conv, grad_in, d_small)
+    ]
+    plan = [
+        (w, first, last, order[::-1])
+        for w, first, last, order in chunk_plan([g.shape[4] for g in grads], LAST)
+    ]
+    sum_up, sum_out, sum_conv, sum_in, sum_small = scatter_all(grads, plan, dims, 3, 2)
+    sum_small = sum_small.T
     gains_count = norm_gains.shape[0]
     return (
         output,
@@ -865,8 +1029,8 @@
         sum_conv,
         sum_in[:, 3 * half : 4 * half],
         sum_out.T,
-        sum_ff[:, :ff],
-        sum_ff[:, ff:],
+        sum_gate,
+        sum_up,
         sum_down.T,
     )
 

time: 1830 us -> 1340 us (0.73)
  waiting for transfers between devices: 819 us -> 248 us
  Pallas kernels: 208 us -> 675 us
  starting transfers between devices: 310 us -> 33 us
  other arithmetic: 139 us -> 72.4 us
  local copies, waits for them, and re-layouts: 86.8 us -> 43.9 us
    ppermute x117 -> x10, waiting for transfers between devices: 819 us -> 244 us  [along(): return lax.ppermute(x, 'seq', ring_pairs(dims, axis, shift))]
    pallas_call x6 -> x2, Pallas kernels: 39 us -> 508 us  [the longest x1 255 us: scatter_all(): pl.pallas_call(functools.partial(scatter_kernel, dims, plan, depth, count...]
    ppermute x117 -> x10, starting transfers between devices: 295 us -> 19.9 us  [along(): return lax.ppermute(x, 'seq', ring_pairs(dims, axis, shift))]
    convert_element_type x16 -> x2, other arithmetic: 34.4 us -> 2.77 us  [the longest x1 2.1 us: per_device(): lax.psum_scatter(grad_gate, 'seq', scatter_dimension=0, tiled=True)]
    dynamic_slice x27 -> x0, local copies, waits for them, and re-layouts: 23.8 us -> none  [scatter_part(): lax.dynamic_index_in_dim(x, to, axis)]
    dot_general x5 -> x6, matrix products: 104 us -> 90.1 us  [mul_t(): lax.dot_general(a, b, (((1,), (1,)), ((), ())), preferred_element_type=f32)]
    dot_general x5 -> x6, matrix products: 72.9 us -> 70.4 us  [mul(): lax.dot_general(a, b, (((1,), (0,)), ((), ())), preferred_element_type=f32)]
    dot_general x5 -> x6, matrix products: 75.4 us -> 77.6 us  [t_mul(): lax.dot_general(a, b, (((0,), (0,)), ((), ())), preferred_element_type=f32)]
  transfers between devices with their start and end apart: 130 -> 27, of which waited for: 51 -> 9; matrix products, arithmetic and copies ran while one was open for 17% -> 25% of each run, Pallas kernels for 11% -> 32%
where the time goes in v2:
time: 1340 us; the launch traced here: 1330 us
  Pallas kernels  675 us (50%)
  waiting for transfers between devices  248 us (19%)
  matrix products  238 us (18%)
  other arithmetic  72.4 us (5%)
  local copies, waits for them, and re-layouts  43.9 us (3%)
  starting transfers between devices  33 us (2%)
  between operations  15.8 us (1%)
    pallas_call x1, Pallas kernels, scatter_all(): pl.pallas_call(functools.partial(scatter_kernel, dims, plan, depth, count...  255 us
    pallas_call x1, Pallas kernels, gather_all(): pl.pallas_call(functools.partial(gather_kernel, dims, plan, depth, count,...  254 us
    ppermute x10, waiting for transfers between devices, along(): return lax.ppermute(x, 'seq', ring_pairs(dims, axis, shift))  244 us
    pallas_call x5, Pallas kernels, call(): pl.pallas_call(kernel, grid=(micros,), in_specs=[spec for _, spec in ins]...  167 us
    dot_general x6, matrix products, mul_t(): lax.dot_general(a, b, (((1,), (1,)), ((), ())), preferred_element_type=f32)  90.1 us
    dot_general x6, matrix products, t_mul(): lax.dot_general(a, b, (((0,), (0,)), ((), ())), preferred_element_type=f32)  77.6 us
    dot_general x6, matrix products, mul(): lax.dot_general(a, b, (((1,), (0,)), ((), ())), preferred_element_type=f32)  70.4 us
  transfers between devices with their start and end apart: 27, of which 9 were waited for; matrix products, arithmetic and copies ran while one was open for 25% of the time, Pallas kernels for 32%

profile of v2, /device:TPU:0, one launch (start us, length us, event | category | flops | bytes accessed | tf_op | source)
XLA Modules:
  0.0 1327.0 jit_solution(12882014171494435110)
XLA Ops:
  15.1 253.6 %shard_map.307 = (bf16[4,2,2,112,128]{4,3,2,1,0:T(8,128)(2,1)}, bf16[4,2,2,112,3840]{4,3,2,1,0:T(8,128)(2,1)}, bf16[4,2,2,112,896]{4,3,2,1,0:T(8,128)(2,1)}, bf1...) custom-call(bf16[112,128]{1,0:T(8,128)(2,1)} %pad.64.refs_0_, ...), custom_call_target="tpu_custom_call" | custom-call | bytes 293601280 | tf_op jit(solution)/shard_map/pallas_call | solution.py:589
  290.4 16.7 %convolution_convert_fusion.3 = bf16[1024,3840]{1,0:T(8,128)(2,1)} fusion(bf16[1792,3840]{1,0:T(8,128)(2,1)S(1)} %bitcast.206, f32[1792]{0:T(1024)S(1)} %get-tuple-element.134, f32[1024]{0:T(1024)S(1)} %bitcast.189, bf16[1024,896]{1,0:T(8,128)(2,1)S(1)} %bitcast.155, bf16[1024,896]{1,0:T(8,128)(2,1)S(1)} %bitcast.159), kind=kOutput, calls=%fused_computation.22 | convolution fusion | flops 14109638656 | bytes 25308160 | tf_op jit(solution)/shard_map/dot_general | solution.py:31
  307.1 8.7 shard_map.308
  340.6 30.6 %collective-permute-done.5 = bf16[2,8,160,128]{3,2,1,0:T(8,128)(2,1)S(1)} collective-permute-done((bf16[2,8,160,128]{3,2,1,0:T(8,128)(2,1)S(1)}, bf16[2,8,160,128]{3,2,1,0:T(8,128)(2,1)S(1)}, u32[]{:S(2)}, u32[]{:S(2)}) %collective-permute-start.5) | collective-permute-done | bytes 655392 | tf_op jit(solution)/shard_map/ppermute | solution.py:746
  371.5 7.2 collective-permute-start.8
  385.8 23.1 %collective-permute-done.8 = bf16[2,8,160,128]{3,2,1,0:T(8,128)(2,1)S(1)} collective-permute-done((bf16[2,8,160,128]{3,2,1,0:T(8,128)(2,1)S(1)}, bf16[2,8,160,128]{3,2,1,0:T(8,128)(2,1)S(1)}, u32[]{:S(2)}, u32[]{:S(2)}) %collective-permute-start.8) | collective-permute-done | bytes 655392 | tf_op jit(solution)/shard_map/ppermute | solution.py:746
  408.9 48.6 %collective-permute-done.7 = bf16[2,8,160,128]{3,2,1,0:T(8,128)(2,1)S(1)} collective-permute-done((bf16[2,8,160,128]{3,2,1,0:T(8,128)(2,1)S(1)}, bf16[2,8,160,128]{3,2,1,0:T(8,128)(2,1)S(1)}, u32[]{:S(2)}, u32[]{:S(2)}) %collective-permute-start.7) | collective-permute-done | bytes 655392 | tf_op jit(solution)/shard_map/ppermute | solution.py:746
  459.8 42.6 %shard_map.309 = (bf16[2,512,896]{2,1,0:T(8,128)(2,1)}, bf16[2,512,896]{2,1,0:T(8,128)(2,1)}, f32[2,512,128]{2,1,0:T(8,128)}) custom-call(s32[2,512,8]{2,1,0:T(8,128)} %copy.74.ic, s32[2,8,640]{2,1,0:T(8,128)} %pad_add_fusion.ir, bf16[2,512,3840]{2,1,0:T(8,128)(2,1)} %bitcast.140, bf16[2,512,3840]{2,1,0:T(8,128)(2,1)} %bitcast.141, ...), custom_call_target="tpu_custom_call" | custom-call | flops 10000000000 | bytes 12582912 | tf_op jit(solution)/shard_map/pallas_call | solution.py:330
  502.4 6.6 convolution_convert_fusion.7
  523.2 11.3 convolution_convert_fusion.5
  534.6 13.4 %convolution_convert_fusion.4 = bf16[1024,2432]{1,0:T(8,128)(2,1)S(1)} fusion(bf16[1024,1792]{1,0:T(8,128)(2,1)} %copy-done.18, bf16[1792,2432]{1,0:T(8,128)(2,1)} %all-gather.3.cloned.1.call-done), kind=kOutput, calls=%fused_computation.52 | convolution fusion | flops 8927969280 | bytes 17367040 | tf_op jit(solution)/shard_map/dot_general | solution.py:31
  550.4 12.9 convolution_convert_fusion
  569.1 16.9 %convolution_convert_fusion.6 = bf16[1024,1792]{1,0:T(8,128)(2,1)S(1)} fusion(bf16[1792,2432]{1,0:T(8,128)(2,1)} %all-gather.5.cloned.1.call-done, bf16[1024,2432]{1,0:T(8,128)(2,1)} %copy-done.73, bf16[1024,2432]{1,0:T(8,128)(2,1)} %convolution_convert_fusion.5), kind=kOutput, calls=%fused_computation.54 | convolution fusion | flops 8947236864 | bytes 22347776 | tf_op jit(solution)/shard_map/dot_general | solution.py:35
  587.7 18.8 %multiply_convert_fusion = (bf16[1024,2432]{1,0:T(8,128)(2,1)}, bf16[1024,2432]{1,0:T(8,128)(2,1)}) fusion(bf16[1024,2432]{1,0:T(8,128)(2,1)} %convolution_convert_fusion.5, bf16[1024,2432]{1,0:T(8,128)(2,1)} %copy-done.73, bf16[1024,1792]{1,0:T(8,128)(2,1)S(1)} %bitcast.168, bf16[1792,2432]{1,0:T(8,128)(2,1)} %all-gather.5.cloned.1.call-done), kind=kOutput, calls=%fused_computation.17 | convolution fusion | flops 8962834432 | bytes 32309248 | tf_op jit(solution)/shard_map/dot_general | solution.py:31
  606.5 16.2 %fusion.63 = f32[1024,1792]{1,0:T(8,128)} fusion(bf16[1024,2432]{1,0:T(8,128)(2,1)} %get-tuple-element.172, bf16[1792,2432]{1,0:T(8,128)(2,1)} %bitcast.207), kind=kOutput, calls=%fused_computation.290 | convolution fusion | flops 8925478912 | bytes 21037056 | tf_op jit(solution)/shard_map/dot_general | solution.py:35
  622.7 15.7 %add_convert_fusion = bf16[1024,1792]{1,0:T(8,128)(2,1)} fusion(f32[1024,1792]{1,0:T(8,128)} %fusion.63, bf16[1024,2432]{1,0:T(8,128)(2,1)S(1)} %copy-done.74, bf16[1792,2432]{1,0:T(8,128)(2,1)} %all-gather.3.cloned.1.call-done), kind=kOutput, calls=%fused_computation.44 | convolution fusion | flops 8929148928 | bytes 24707072 | tf_op jit(solution)/shard_map/dot_general | solution.py:35
  638.6 15.0 %convolution_convert_fusion.1 = bf16[1792,2432]{1,0:T(8,128)(2,1)} fusion(bf16[1024,1792]{1,0:T(8,128)(2,1)S(1)} %copy-done.19, bf16[1024,2432]{1,0:T(8,128)(2,1)} %get-tuple-element.172), kind=kOutput, calls=%fused_computation.7 | convolution fusion | flops 8929837056 | bytes 17367040 | tf_op jit(solution)/shard_map/dot_general | solution.py:39
  653.7 15.1 %convolution_convert_fusion.2 = bf16[1792,2432]{1,0:T(8,128)(2,1)} fusion(bf16[1024,1792]{1,0:T(8,128)(2,1)} %copy-done.18, bf16[1024,2432]{1,0:T(8,128)(2,1)} %get-tuple-element.171), kind=kOutput, calls=%fused_computation.8 | convolution fusion | flops 8929837056 | bytes 17367040 | tf_op jit(solution)/shard_map/dot_general | solution.py:39
  687.4 87.4 %shard_map.310 = (bf16[2,512,128]{2,1,0:T(8,128)(2,1)}, f32[2,512,128]{2,1,0:T(8,128)}, f32[2,512,896]{2,1,0:T(8,128)}, bf16[2,512,896]{2,1,0:T(8,128)(2,1)}, f3...) custom-call(s32[2,512,8]{2,1,0:T(8,128)} %copy.74.ic, ...), custom_call_target="tpu_custom_call" | custom-call | flops 20000000000 | bytes 42270720 | tf_op jit(solution)/shard_map/pallas_call | solution.py:330
  774.8 12.1 multiply_reduce_fusion.1
  790.3 14.0 %shard_map.311 = bf16[2,8,160,128]{3,2,1,0:T(8,128)(2,1)} custom-call(s32[2,512,8]{2,1,0:T(8,128)} %copy.74.ic, bf16[2,512,3840]{2,1,0:T(8,128)(2,1)} %bitcast.150, bf16[2,512,896]{2,1,0:T(8,128)(2,1)} %bitcast.178, bf16[2,512,896]{2,1,0:T(8,128)(2,1)} %get-tuple-element.47.linear, f32[2,512,128]{2,1,0:T(8,128)} %get-tuple-element.48.rden, ...), custom_call_target="tpu_custom_call" | custom-call | flops 1000000000 | bytes 1966080 | tf_op jit(solution)/shard_map/pallas_call | solution.py:330
  813.4 44.2 %collective-permute-done.14 = bf16[2,8,160,128]{3,2,1,0:T(8,128)(2,1)S(1)} collective-permute-done((bf16[2,8,160,128]{3,2,1,0:T(8,128)(2,1)}, bf16[2,8,160,128]{3,2,1,0:T(8,128)(2,1)S(1)}, u32[]{:S(2)}, u32[]{:S(2)}) %collective-permute-start.14) | collective-permute-done | bytes 655392 | tf_op jit(solution)/shard_map/ppermute | solution.py:746
  863.6 23.0 %collective-permute-done.15 = bf16[2,8,160,128]{3,2,1,0:T(8,128)(2,1)S(1)} collective-permute-done((bf16[2,8,160,128]{3,2,1,0:T(8,128)(2,1)S(1)}, bf16[2,8,160,128]{3,2,1,0:T(8,128)(2,1)S(1)}, u32[]{:S(2)}, u32[]{:S(2)}) %collective-permute-start.15) | collective-permute-done | bytes 655392 | tf_op jit(solution)/shard_map/ppermute | solution.py:746
  899.2 19.7 %collective-permute-done.18 = bf16[2,8,160,128]{3,2,1,0:T(8,128)(2,1)S(1)} collective-permute-done((bf16[2,8,160,128]{3,2,1,0:T(8,128)(2,1)S(1)}, bf16[2,8,160,128]{3,2,1,0:T(8,128)(2,1)S(1)}, u32[]{:S(2)}, u32[]{:S(2)}) %collective-permute-start.18) | collective-permute-done | bytes 655392 | tf_op jit(solution)/shard_map/ppermute | solution.py:746
  918.9 50.0 %collective-permute-done.17 = bf16[2,8,160,128]{3,2,1,0:T(8,128)(2,1)S(1)} collective-permute-done((bf16[2,8,160,128]{3,2,1,0:T(8,128)(2,1)S(1)}, bf16[2,8,160,128]{3,2,1,0:T(8,128)(2,1)S(1)}, u32[]{:S(2)}, u32[]{:S(2)}) %collective-permute-start.17) | collective-permute-done | bytes 655392 | tf_op jit(solution)/shard_map/ppermute | solution.py:746
  971.2 14.4 %shard_map.312 = bf16[2,512,3840]{2,1,0:T(8,128)(2,1)} custom-call(s32[2,512,8]{2,1,0:T(8,128)} %copy.74.ic, bf16[2,512,3840]{2,1,0:T(8,128)(2,1)} %bitcast.151, bf16[2,512,3840]{2,1,0:T(8,128)(2,1)} %bitcast.152, bf16[2,8,160,128]{3,2,1,0:T(8,128)(2,1)} %fusion.40.d_own, bf16[8,128,160]{2,1,0:T(8,128)(2,1)} %constant.304.clone.left, ...), custom_call_target="tpu_custom_call" | custom-call | flops 2000000000 | bytes 23592960 | tf_op jit(solution)/shard_map/pallas_call | solution.py:330
  985.7 22.6 %fusion.15 = bf16[1024,1792]{1,0:T(8,128)(2,1)} fusion(f32[2,512,1792]{2,1,0:T(8,128)} %convert_add_fusion.1, bf16[1024,3840]{1,0:T(8,128)(2,1)} %bitcast.171, bf16[1792,3840]{1,0:T(8,128)(2,1)} %bitcast.205), kind=kOutput, calls=%fused_computation.31 | convolution fusion | flops 14096531456 | bytes 32636928 | tf_op jit(solution)/shard_map/dot_general | solution.py:35
  1008.3 7.6 bitcast_convert_fusion.1
  1016.0 21.5 %bitcast_convert_fusion = bf16[1792,3840]{1,0:T(8,128)(2,1)} fusion(bf16[2,512,1792]{2,1,0:T(8,128)(2,1)S(1)} %copy-done.9, bf16[2,512,3840]{2,1,0:T(8,128)(2,1)} %shard_map.312), kind=kOutput, calls=%fused_computation | convolution fusion | flops 14099742720 | bytes 25296896 | tf_op jit(solution)/shard_map/dot_general | solution.py:39
  1037.5 6.6 multiply_reduce_fusion.3
  1045.4 254.5 %shard_map.313 = (f32[112,2432]{1,0:T(8,128)}, f32[112,896]{1,0:T(8,128)}, f32[112,896]{1,0:T(8,128)}, f32[112,3840]{1,0:T(8,128)}, f32[112,128]{1,0:T(8,128)}) custom-call(bf16[4,2,2,112,2432]{4,3,2,1,0:T(8,128)(2,1)} %bitcast.170, bf16[4,2,2,112,896]{4,3,2,1,0:T(8,128)(2,1)} %bitcast.173, bf16[4,2,2,112,896]{4,3,2,1,0:T(8,128)(2,1)} %bitcast.174, ...), custom_call_target="tpu_custom_call" | custom-call | bytes 293601280 | tf_op jit(solution)/shard_map/pallas_call | solution.py:717
  1306.9 6.3 fusion.17
  (366 shorter events, 154.1 us)
Async XLA Ops:
  7.2 261.7 %copy-start.23 = (bf16[2,512,896]{2,1,0:T(8,128)(2,1)S(1)}, bf16[2,512,896]{2,1,0:T(8,128)(2,1)}, u32[]{:S(2)}) copy-start(bf16[2,512,896]{2,1,0:T(8,128)(2,1)} %param.21) | copy-start | bytes 5505028
  7.2 262.3 %copy-start.64 = (s32[2,4]{1,0:T(2,128)S(1)}, s32[2,4]{1,0:T(2,128)}, u32[]{:S(2)}) copy-start(s32[2,4]{1,0:T(2,128)} %param.22) | copy-start | bytes 100
  7.2 262.4 %copy-start.65 = (s32[2,4]{1,0:T(2,128)S(1)}, s32[2,4]{1,0:T(2,128)}, u32[]{:S(2)}) copy-start(s32[2,4]{1,0:T(2,128)} %param.23) | copy-start | bytes 100
  7.2 527.4 %all-gather.3.cloned.1.call-start = ((), (), s32[]{:S(2)}) async-start(), calls=%async_computation.2 | async-start | bytes 9261056 | tf_op jit(solution)/shard_map/all_gather | solution.py:873
  268.7 300.4 %all-gather.5.cloned.1.call-start = ((), (), s32[]{:S(2)}) async-start(), calls=%async_computation.3 | async-start | bytes 9261056 | tf_op jit(solution)/shard_map/all_gather | solution.py:873
  268.8 11.6 collective-permute-start
  268.8 11.5 collective-permute-start.11
  269.5 1043.8 %reduce-scatter.5.cloned.1.call-start = ((), (), s32[]{:S(2)}) async-start(), calls=%async_computation.5 | async-start | bytes 9261056 | tf_op jit(solution)/shard_map/reduce_scatter | solution.py:950
  280.3 283.1 %copy-start.34 = (f32[1792]{0:T(1024)}, f32[1792]{0:T(1024)S(1)}, u32[]{:S(2)}) copy-start(f32[1792]{0:T(1024)S(1)} %get-tuple-element.134) | copy-start | bytes 21508
  286.5 277.7 %copy-start.1 = (bf16[2,512,896]{2,1,0:T(8,128)(2,1)}, bf16[2,512,896]{2,1,0:T(8,128)(2,1)S(1)}, u32[]{:S(2)}) copy-start(bf16[2,512,896]{2,1,0:T(8,128)(2,1)S(1)} %get-tuple-element.217) | copy-start | bytes 5505028
  315.8 18.4 %collective-permute-start.4 = (bf16[2,8,160,128]{3,2,1,0:T(8,128)(2,1)}, bf16[2,8,160,128]{3,2,1,0:T(8,128)(2,1)S(1)}, u32[]{:S(2)}, u32[]{:S(2)}) collective-permute-start(bf16[2,8,160,128]{3,2,1,0:T(8,128)(2,1)} %shard_map.308), channel_id=1, source_target_pairs={{0,2},{2,0},{4,6},{6,4},{8,10},{10,8},{12,14},{14,12},{16,18},{18,... | collective-permute-start | bytes 1966088 | tf_op jit(solution)/shard_map/ppermute | solution.py:746
  320.2 16.6 %collective-permute-start.1 = (bf16[2,2,1792]{2,1,0:T(2,128)(2,1)S(1)}, bf16[2,2,1792]{2,1,0:T(2,128)(2,1)S(1)}, u32[]{:S(2)}, u32[]{:S(2)}) collective-permute-start(bf16[2,2,1792]{2,1,0:T(2,128)(2,1)S(1)} %slice.165), channel_id=1, source_target_pairs={{0,2},{2,4},{4,6},{6,8},{8,10},{10,12},{12,14},{14,16},{16,18},{18... | collective-permute-start | bytes 43016 | tf_op jit(solution)/shard_map/ppermute | solution.py:766
  323.3 135.8 %collective-permute-start.3 = (bf16[2,64,896]{2,1,0:T(8,128)(2,1)S(1)}, bf16[2,64,896]{2,1,0:T(8,128)(2,1)S(1)}, u32[]{:S(2)}, u32[]{:S(2)}) collective-permute-start(bf16[2,64,896]{2,1,0:T(8,128)(2,1)S(1)} %get-tuple-element.173), channel_id=1, source_target_pairs={{0,2},{2,4},{4,6},{6,8},{8,10},{10,12},{12,14},{14,16},{16,18},{18... | collective-permute-start | bytes 688136 | tf_op jit(solution)/shard_map/ppermute | solution.py:766
  326.7 132.4 %collective-permute-start.2 = (bf16[2,64,896]{2,1,0:T(8,128)(2,1)S(1)}, bf16[2,64,896]{2,1,0:T(8,128)(2,1)S(1)}, u32[]{:S(2)}, u32[]{:S(2)}) collective-permute-start(bf16[2,64,896]{2,1,0:T(8,128)(2,1)S(1)} %get-tuple-element.174), channel_id=1, source_target_pairs={{0,2},{2,4},{4,6},{6,8},{8,10},{10,12},{12,14},{14,16},{16,18},{18... | collective-permute-start | bytes 688136 | tf_op jit(solution)/shard_map/ppermute | solution.py:766
  334.6 36.6 %collective-permute-start.5 = (bf16[2,8,160,128]{3,2,1,0:T(8,128)(2,1)S(1)}, bf16[2,8,160,128]{3,2,1,0:T(8,128)(2,1)S(1)}, u32[]{:S(2)}, u32[]{:S(2)}) collective-permute-start(bf16[2,8,160,128]{3,2,1,0:T(8,128)(2,1)S(1)} %fusion.33), channel_id=1, source_target_pairs={{0,4},{2,6},{4,0},{6,2},{8,12},{10,14},{12,8},{14,10},{16,20},{18,... | collective-permute-start | bytes 1966088 | tf_op jit(solution)/shard_map/ppermute | solution.py:746
  371.5 37.4 %collective-permute-start.8 = (bf16[2,8,160,128]{3,2,1,0:T(8,128)(2,1)S(1)}, bf16[2,8,160,128]{3,2,1,0:T(8,128)(2,1)S(1)}, u32[]{:S(2)}, u32[]{:S(2)}) collective-permute-start(bf16[2,8,160,128]{3,2,1,0:T(8,128)(2,1)S(1)} %fusion.35), channel_id=1, source_target_pairs={{0,24},{2,26},{4,28},{6,30},{8,0},{10,2},{12,4},{14,6},{16,8},{18,... | collective-permute-start | bytes 1966088 | tf_op jit(solution)/shard_map/ppermute | solution.py:746
  378.7 78.8 %collective-permute-start.7 = (bf16[2,8,160,128]{3,2,1,0:T(8,128)(2,1)S(1)}, bf16[2,8,160,128]{3,2,1,0:T(8,128)(2,1)S(1)}, u32[]{:S(2)}, u32[]{:S(2)}) collective-permute-start(bf16[2,8,160,128]{3,2,1,0:T(8,128)(2,1)S(1)} %fusion.35), channel_id=1, source_target_pairs={{0,16},{2,18},{4,20},{6,22},{8,24},{10,26},{12,28},{14,30},{16,0},... | collective-permute-start | bytes 1966088 | tf_op jit(solution)/shard_map/ppermute | solution.py:746
  380.8 76.8 %collective-permute-start.6 = (bf16[2,8,160,128]{3,2,1,0:T(8,128)(2,1)S(1)}, bf16[2,8,160,128]{3,2,1,0:T(8,128)(2,1)S(1)}, u32[]{:S(2)}, u32[]{:S(2)}) collective-permute-start(bf16[2,8,160,128]{3,2,1,0:T(8,128)(2,1)S(1)} %fusion.35), channel_id=1, source_target_pairs={{0,8},{2,10},{4,12},{6,14},{8,16},{10,18},{12,20},{14,22},{16,24},... | collective-permute-start | bytes 1966088 | tf_op jit(solution)/shard_map/ppermute | solution.py:746
  509.1 6.5 collective-permute-start.9
  563.4 752.0 %reduce-scatter.3.cloned.1.call-start = ((), (), s32[]{:S(2)}) async-start(), calls=%async_computation.4 | async-start | bytes 9261056 | tf_op jit(solution)/shard_map/reduce_scatter | solution.py:965
  587.6 81.2 %collective-permute-start.10 = (bf16[1024,896]{1,0:T(8,128)(2,1)}, bf16[1024,896]{1,0:T(8,128)(2,1)}, u32[]{:S(2)}, u32[]{:S(2)}) collective-permute-start(bf16[1024,896]{1,0:T(8,128)(2,1)} %constant_dynamic-slice_fusion.7), channel_id=1, source_target_pairs={{0,1},{1,0},{2,3},{3,2},{4,5},{5,4},{6,7},{7,6},{8,9},{9,8},{10,11... | collective-permute-start | bytes 5505032 | tf_op jit(solution)/shard_map/ppermute | solution.py:750
  638.4 33.9 %collective-permute-start.12 = (bf16[1024,1792]{1,0:T(8,128)(2,1)}, bf16[1024,1792]{1,0:T(8,128)(2,1)}, u32[]{:S(2)}, u32[]{:S(2)}) collective-permute-start(bf16[1024,1792]{1,0:T(8,128)(2,1)} %add_convert_fusion), channel_id=1, source_target_pairs={{0,1},{1,0},{2,3},{3,2},{4,5},{5,4},{6,7},{7,6},{8,9},{9,8},{10,11... | collective-permute-start | bytes 11010056 | tf_op jit(solution)/shard_map/ppermute | solution.py:750
  804.4 53.2 %collective-permute-start.14 = (bf16[2,8,160,128]{3,2,1,0:T(8,128)(2,1)}, bf16[2,8,160,128]{3,2,1,0:T(8,128)(2,1)S(1)}, u32[]{:S(2)}, u32[]{:S(2)}) collective-permute-start(bf16[2,8,160,128]{3,2,1,0:T(8,128)(2,1)} %shard_map.311), channel_id=1, source_target_pairs={{0,2},{2,0},{4,6},{6,4},{8,10},{10,8},{12,14},{14,12},{16,18},{18,... | collective-permute-start | bytes 1966088 | tf_op jit(solution)/shard_map/ppermute | solution.py:746
  804.4 166.1 %collective-permute-start.19 = (bf16[2,64,896]{2,1,0:T(8,128)(2,1)}, bf16[2,64,896]{2,1,0:T(8,128)(2,1)S(1)}, u32[]{:S(2)}, u32[]{:S(2)}) collective-permute-start(bf16[2,64,896]{2,1,0:T(8,128)(2,1)} %get-tuple-element.56), channel_id=1, source_target_pairs={{2,0},{4,2},{6,4},{8,6},{10,8},{12,10},{14,12},{16,14},{18,16},{20... | collective-permute-start | bytes 688136 | tf_op jit(solution)/shard_map/ppermute | solution.py:766
  805.7 164.8 %collective-permute-start.20 = (bf16[2,64,896]{2,1,0:T(8,128)(2,1)S(1)}, bf16[2,64,896]{2,1,0:T(8,128)(2,1)S(1)}, u32[]{:S(2)}, u32[]{:S(2)}) collective-permute-start(bf16[2,64,896]{2,1,0:T(8,128)(2,1)S(1)} %copy-done.70), channel_id=1, source_target_pairs={{2,0},{4,2},{6,4},{8,6},{10,8},{12,10},{14,12},{16,14},{18,16},{20... | collective-permute-start | bytes 688136 | tf_op jit(solution)/shard_map/ppermute | solution.py:766
  812.1 79.2 %collective-permute-start.13 = (bf16[2,2,1792]{2,1,0:T(2,128)(2,1)S(1)}, bf16[2,2,1792]{2,1,0:T(2,128)(2,1)S(1)}, u32[]{:S(2)}, u32[]{:S(2)}) collective-permute-start(bf16[2,2,1792]{2,1,0:T(2,128)(2,1)S(1)} %fusion.45), channel_id=1, source_target_pairs={{2,0},{4,2},{6,4},{8,6},{10,8},{12,10},{14,12},{16,14},{18,16},{20... | collective-permute-start | bytes 43016 | tf_op jit(solution)/shard_map/ppermute | solution.py:766
  858.0 28.6 %collective-permute-start.15 = (bf16[2,8,160,128]{3,2,1,0:T(8,128)(2,1)S(1)}, bf16[2,8,160,128]{3,2,1,0:T(8,128)(2,1)S(1)}, u32[]{:S(2)}, u32[]{:S(2)}) collective-permute-start(bf16[2,8,160,128]{3,2,1,0:T(8,128)(2,1)S(1)} %fusion.42), channel_id=1, source_target_pairs={{0,4},{2,6},{4,0},{6,2},{8,12},{10,14},{12,8},{14,10},{16,20},{18,... | collective-permute-start | bytes 1966088 | tf_op jit(solution)/shard_map/ppermute | solution.py:746
  886.9 31.9 %collective-permute-start.18 = (bf16[2,8,160,128]{3,2,1,0:T(8,128)(2,1)S(1)}, bf16[2,8,160,128]{3,2,1,0:T(8,128)(2,1)S(1)}, u32[]{:S(2)}, u32[]{:S(2)}) collective-permute-start(bf16[2,8,160,128]{3,2,1,0:T(8,128)(2,1)S(1)} %fusion.44), channel_id=1, source_target_pairs={{0,24},{2,26},{4,28},{6,30},{8,0},{10,2},{12,4},{14,6},{16,8},{18,... | collective-permute-start | bytes 1966088 | tf_op jit(solution)/shard_map/ppermute | solution.py:746
  887.2 81.7 %collective-permute-start.17 = (bf16[2,8,160,128]{3,2,1,0:T(8,128)(2,1)S(1)}, bf16[2,8,160,128]{3,2,1,0:T(8,128)(2,1)S(1)}, u32[]{:S(2)}, u32[]{:S(2)}) collective-permute-start(bf16[2,8,160,128]{3,2,1,0:T(8,128)(2,1)S(1)} %fusion.44), channel_id=1, source_target_pairs={{0,16},{2,18},{4,20},{6,22},{8,24},{10,26},{12,28},{14,30},{16,0},... | collective-permute-start | bytes 1966088 | tf_op jit(solution)/shard_map/ppermute | solution.py:746
  891.3 77.6 %collective-permute-start.16 = (bf16[2,8,160,128]{3,2,1,0:T(8,128)(2,1)S(1)}, bf16[2,8,160,128]{3,2,1,0:T(8,128)(2,1)S(1)}, u32[]{:S(2)}, u32[]{:S(2)}) collective-permute-start(bf16[2,8,160,128]{3,2,1,0:T(8,128)(2,1)S(1)} %fusion.44), channel_id=1, source_target_pairs={{0,8},{2,10},{4,12},{6,14},{8,16},{10,18},{12,20},{14,22},{16,24},... | collective-permute-start | bytes 1966088 | tf_op jit(solution)/shard_map/ppermute | solution.py:746
  918.9 97.0 %collective-permute-start.22 = (f32[3,1792]{1,0:T(4,128)S(1)}, f32[3,1792]{1,0:T(4,128)S(1)}, u32[]{:S(2)}, u32[]{:S(2)}) collective-permute-start(f32[3,1792]{1,0:T(4,128)S(1)} %pad_maximum_fusion.4), channel_id=1, source_target_pairs={{0,1},{1,0},{2,3},{3,2},{4,5},{5,4},{6,7},{7,6},{8,9},{9,8},{10,11... | collective-permute-start | bytes 64520 | tf_op jit(solution)/shard_map/ppermute | solution.py:750
  1008.3 29.2 %collective-permute-start.21 = (bf16[1024,1792]{1,0:T(8,128)(2,1)}, bf16[1024,1792]{1,0:T(8,128)(2,1)}, u32[]{:S(2)}, u32[]{:S(2)}) collective-permute-start(bf16[1024,1792]{1,0:T(8,128)(2,1)} %fusion.15), channel_id=1, source_target_pairs={{0,1},{1,0},{2,3},{3,2},{4,5},{5,4},{6,7},{7,6},{8,9},{9,8},{10,11... | collective-permute-start | bytes 11010056 | tf_op jit(solution)/shard_map/ppermute | solution.py:750
  (79 other events, 2826.7 us)
Sparse Core Ops, SparseCore 0:
  268.8 177.2 all-gather.2
  448.9 112.3 all-gather.4
  563.6 185.0 reduce-scatter.4
  750.8 214.5 reduce-scatter.2

commit v3 on v2

--- a/solution.py
+++ b/solution.py
@@ -24,7 +24,7 @@
 
 ZYX, ZXY, XZY, YZX, XYZ, YXZ = (0, 1, 2), (0, 2, 1), (2, 0, 1), (1, 0, 2), (2, 1, 0), (1, 2, 0)
 FIRST = [(ZXY, 4), (ZXY, 5), (ZYX, 3), (ZXY, 4), (YZX, 3), (ZYX, 3), (ZXY, 5), (ZYX, 5), (YXZ, 4), (XZY, 5), (ZYX, 4)]
-LAST = [(XZY, 5), (ZXY, 5), (YXZ, 3), (ZYX, 7), (YZX, 3), (ZYX, 3), (ZXY, 4), (ZYX, 3)]
+LAST = [(ZYX, 3), (YXZ, 2), (ZXY, 4), (XZY, 2), (ZYX, 4), (ZYX, 1)]
 
 
 def mul(a, b):
@@ -80,16 +80,16 @@
     return a, b, (a * b * consts[2:3]).astype(bf16)
 
 
-def own_kernel(ic, qk, v, left, right, consts, state):
-    heads = v.shape[2] // HDIM
-    width = qk.shape[2] // 2
-    keys = qk[0, :, width:]
+def own_kernel(ic, kv, left, right, consts, state):
+    half, width = split_kv(kv)
+    heads = half // HDIM
+    keys = kv[0, :, half + width :]
     last = ic[0, :, 2:3].astype(f32)
     table = consts[...]
     for h in range(heads):
         _, _, phi = features(keys, left[h], right[h], table)
         phi = (phi.astype(f32) * last).astype(bf16)
-        state[0, h] = t_mul(phi, with_one(v[0, :, head_cols(h)])).astype(bf16)
+        state[0, h] = t_mul(phi, with_one(kv[0, :, head_cols(h)])).astype(bf16)
 
 
 def linear_mask(ic, ir, t):
@@ -130,50 +130,61 @@
     return jnp.where(lane // FDIM == h, rows.astype(f32), 0.0).astype(bf16)
 
 
-def mix_kernel(
-    ic, ir, qk, v, wq, wk, cg, ci, wkp, vp, prefix, left, right, consts,
-    mixed, linear, rden, lmask, wmask, kext, vext,
-):
-    heads = v.shape[2] // HDIM
-    rows = v.shape[1]
-    tiles = rows // TILE
-    width = qk.shape[2] // 2
-    fill_masks(ic, ir, lmask, wmask, tiles)
-    queries = qk[0, :, :width]
-    keys = qk[0, :, width:]
-    carried = ic[0, :, 1:2].astype(f32)
-    table = consts[...]
-    lane = lax.broadcasted_iota(jnp.int32, (rows, LANES), 1)
-    inverse = jnp.zeros((rows, LANES), f32)
+def window_kernel(ic, ir, kv, wq, wk, cg, ci, wkp, vp, *rest):
+    part, wmask, kext, vext = rest[-4:]
+    half, _ = split_kv(kv)
+    rows = kv.shape[1]
+    for t in range(rows // TILE):
+        wmask[t * TILE : (t + 1) * TILE, :] = jnp.where(window_mask(ic, ir, t), 0.0, -1e30)
     kext[0:WIN, :] = wkp[0]
     kext[WIN:, :] = wk[0]
     vext[0:WIN, :] = vp[0]
-    vext[WIN:, :] = v[0]
-    for h in range(heads):
+    vext[WIN:, :] = kv[0, :, :half]
+    for h in range(half // HDIM):
         hc = head_cols(h)
-        vh = with_one(vext[:, hc])
+        vh = vext[:, hc]
         kh = kext[:, hc]
+        for t in range(rows // TILE):
+            r = slice(t * TILE, (t + 1) * TILE)
+            e = slice(t * TILE, t * TILE + TILE + WIN)
+            probs = window_probs(wq[0, r, hc], kh[e], wmask[r, :])
+            conv = ci[0, r, hc].astype(f32) * cg[0, r, hc].astype(f32)
+            part[0, r, hc] = mul(probs.astype(bf16), vh[e]) + conv
+
+
+def linear_kernel(ic, ir, kv, part, prefix, left, right, consts, mixed, linear, rden, lmask):
+    half, width = split_kv(kv)
+    rows = kv.shape[1]
+    for t in range(rows // TILE):
+        lmask[t * TILE : (t + 1) * TILE, 0 : TILE * (t + 1)] = jnp.where(
+            linear_mask(ic, ir, t), 1.0, 0.0
+        )
+    queries = kv[0, :, half : half + width]
+    keys = kv[0, :, half + width :]
+    carried = ic[0, :, 1:2].astype(f32)
+    table = consts[...]
+    lane = lax.broadcasted_iota(jnp.int32, (TILE, LANES), 1)
+    for h in range(half // HDIM):
+        hc = head_cols(h)
+        vh = with_one(kv[0, :, hc])
         qh = head_rows(queries, h)
         _, _, phi = features(queries, left[h], right[h], table)
         phi = (phi.astype(f32) * (carried * table[3:4])).astype(bf16)
-        for t in range(tiles):
+        for t in range(rows // TILE):
             r = slice(t * TILE, (t + 1) * TILE)
             n = TILE * (t + 1)
             a = 0.25 * mul_t(qh[r], keys[0:n])
             weight = ((1.0 + a + 0.5 * (a * a)) * lmask[r, 0:n]).astype(bf16)
-            numer = mul(weight, vh[WIN : WIN + n]) + mul(phi[r], prefix[0, h])
+            numer = mul(weight, vh[0:n]) + mul(phi[r], prefix[0, h])
             inv = 1.0 / numer[:, HDIM : HDIM + 1]
-            inverse_t = jnp.where(lane[r] == h, inv, 0.0)
             lin = (numer * inv)[:, :HDIM]
-            probs = window_probs(wq[0, r, hc], kh[r.start : r.start + TILE + WIN], wmask[r, :])
-            win = mul(probs.astype(bf16), vh[r.start : r.start + TILE + WIN])[:, :HDIM]
-            conv = ci[0, r, hc].astype(f32) * cg[0, r, hc].astype(f32)
-            mixed[0, r, hc] = (lin + win + conv).astype(bf16)
+            mixed[0, r, hc] = (lin + part[0, r, hc]).astype(bf16)
             linear[0, r, hc] = lin.astype(bf16)
+            inverse = jnp.where(lane == h, inv, 0.0)
             if h == 0:
-                rden[0, r, :] = inverse_t
+                rden[0, r, :] = inverse
             else:
-                rden[0, r, :] += inverse_t
+                rden[0, r, :] += inverse
 
 
 def d_numer(dm, linear, rden, h, r):
@@ -192,11 +203,11 @@
     return jnp.concatenate([dn, extra], axis=1).astype(bf16)
 
 
-def prefix_grad_kernel(ic, qk, dm, linear, rden, left, right, consts, d_prefix):
-    heads = dm.shape[2] // HDIM
+def prefix_grad_kernel(ic, kv, dm, linear, rden, left, right, consts, d_prefix):
+    half, width = split_kv(kv)
+    heads = half // HDIM
     rows = dm.shape[1]
-    width = qk.shape[2] // 2
-    queries = qk[0, :, :width]
+    queries = kv[0, :, half : half + width]
     carried = ic[0, :, 1:2].astype(f32)
     table = consts[...]
     for h in range(heads):
@@ -207,26 +218,22 @@
 
 
 def mix_grad_kernel(
-    ic, ir, qk, v, wq, wk, cg, ci, wkp, vp, prefix, left, right, consts, dm, linear, rden,
-    dq, dk, dv, dwq, dwk, dcg, dci, dwkp, dvp, lmask, wmask, kext, vext, dqs, dks, dvs, dwks,
+    ic, ir, kv, wq, wk, wkp, vp, prefix, left, right, consts, dm, linear, rden, *rest
 ):
-    heads = v.shape[2] // HDIM
-    rows = v.shape[1]
+    dq, dk, dv, dwq, dwk, dwkp, dvp, lmask, wmask, kext, vext, dqs, dks, dvs, dwks = rest[-15:]
+    half, width = split_kv(kv)
+    heads = half // HDIM
+    rows = kv.shape[1]
     tiles = rows // TILE
-    width = qk.shape[2] // 2
     fill_masks(ic, ir, lmask, wmask, tiles)
-    queries = qk[0, :, :width]
-    keys = qk[0, :, width:]
+    queries = kv[0, :, half : half + width]
+    keys = kv[0, :, half + width :]
     carried = ic[0, :, 1:2].astype(f32)
     table = consts[...]
     kext[0:WIN, :] = wkp[0]
     kext[WIN:, :] = wk[0]
     vext[0:WIN, :] = vp[0]
-    vext[WIN:, :] = v[0]
-    grad_rows = dm[0].astype(f32)
-    dci[0] = (grad_rows * cg[0].astype(f32)).astype(bf16)
-    dcg[0] = (grad_rows * ci[0].astype(f32)).astype(bf16)
-    lane_q = lax.broadcasted_iota(jnp.int32, (TILE, width), 1)
+    vext[WIN:, :] = kv[0, :, :half]
     lane_f = lax.broadcasted_iota(jnp.int32, (PHI, LANES), 1)
     dqs[...] = jnp.zeros_like(dqs)
     dks[...] = jnp.zeros_like(dks)
@@ -280,13 +287,12 @@
 
 
 def finish_kernel(
-    ic, qk, v, d_own, left, right, consts, dk, dv, dwk, dwq, dcg, dq, back_k, back_v, out
+    ic, kv, d_own, left, right, consts, dk, dv, dwk, dwq, dcg, dq, back_k, back_v, d_kv, d_rest
 ):
-    heads = v.shape[2] // HDIM
-    rows = v.shape[1]
-    half = v.shape[2]
-    width = qk.shape[2] // 2
-    keys = qk[0, :, width:]
+    half, width = split_kv(kv)
+    heads = half // HDIM
+    rows = kv.shape[1]
+    keys = kv[0, :, half + width :]
     last = ic[0, :, 2:3].astype(f32)
     table = consts[...]
     d_keys = dk[0]
@@ -296,22 +302,22 @@
         fa, fb, phi = features(keys, left[h], right[h], table)
         phi = (phi.astype(f32) * last).astype(bf16)
         part = dv[0, :, hc] + mul(phi, grad)[:, :HDIM]
-        out[0, 0 : rows - WIN, hc] = part[0 : rows - WIN].astype(bf16)
-        out[0, rows - WIN :, hc] = (part[rows - WIN :] + back_v[0, :, hc].astype(f32)).astype(bf16)
-        g = mul_t(with_one(v[0, :, hc]), grad) * (last * table[2:3])
+        d_kv[0, 0 : rows - WIN, hc] = part[0 : rows - WIN].astype(bf16)
+        d_kv[0, rows - WIN :, hc] = (part[rows - WIN :] + back_v[0, :, hc].astype(f32)).astype(bf16)
+        g = mul_t(with_one(kv[0, :, hc]), grad) * (last * table[2:3])
         d_keys = (
             d_keys
             + mul_t((g * fb).astype(bf16), left[h])
             + mul_t((g * fa).astype(bf16), right[h])
         )
-    out[0, :, half : 2 * half] = dwq[0]
-    out[0, 0 : rows - WIN, 2 * half : 3 * half] = dwk[0, 0 : rows - WIN].astype(bf16)
-    out[0, rows - WIN :, 2 * half : 3 * half] = (
+    d_kv[0, :, half : half + width] = dq[0]
+    d_kv[0, :, half + width :] = d_keys.astype(bf16)
+    d_rest[0, :, 0:half] = dwq[0]
+    d_rest[0, 0 : rows - WIN, half : 2 * half] = dwk[0, 0 : rows - WIN].astype(bf16)
+    d_rest[0, rows - WIN :, half : 2 * half] = (
         dwk[0, rows - WIN :] + back_k[0].astype(f32)
     ).astype(bf16)
-    out[0, :, 3 * half : 4 * half] = dcg[0]
-    out[0, :, 4 * half : 4 * half + width] = dq[0]
-    out[0, :, 4 * half + width :] = d_keys.astype(bf16)
+    d_rest[0, :, 2 * half :] = dcg[0]
 
 
 def micro_spec(array, block=None, at=0):
@@ -347,67 +353,78 @@
     return jax.ShapeDtypeStruct(shape, dtype)
 
 
-def projected(proj, half):
-    width = proj.shape[2] - 4 * half
-    return [(proj, micro_spec(proj, half, i)) for i in range(4)] + [
-        (proj, micro_spec(proj, width, 4 * half // width))
+def parts_of(proj, half):
+    return [(proj, micro_spec(proj, half, i)) for i in range(proj.shape[2] // half)]
+
+
+def split_kv(kv):
+    width = (kv.shape[2] - kv.shape[2] // (HDIM + 2 * FDIM) * HDIM) // 2
+    half = kv.shape[2] - 2 * width
+    return half, width
+
+
+def micro_ins(*arrays):
+    return [(a, micro_spec(a)) for a in arrays]
+
+
+def table_ins(tables):
+    return [(t, whole_spec(t)) for t in tables]
+
+
+def awaited(arrays):
+    return [(a, pl.BlockSpec(memory_space=pl.ANY)) for a in arrays]
+
+
+def own_states(ic, kv, tables):
+    micros = kv.shape[0]
+    heads = split_kv(kv)[0] // HDIM
+    ins = micro_ins(ic, kv) + table_ins(tables)
+    return call(own_kernel, micros, ins, [struct(micros, heads, PHI, LANES)], [], 10**9)[0]
+
+
+def window_forward(ic, ir, kv, rest, conv_in, tail_k, tail_v, after):
+    micros, rows, _ = kv.shape
+    half = split_kv(kv)[0]
+    ins = micro_ins(ic, ir, kv) + parts_of(rest, half) + micro_ins(conv_in, tail_k, tail_v)
+    scratch = [
+        pltpu.VMEM((rows, TILE + WIN), f32),
+        pltpu.VMEM((rows + WIN, half), bf16),
+        pltpu.VMEM((rows + WIN, half), bf16),
     ]
-
-
-def own_states(ic, proj, half, tables):
-    micros = proj.shape[0]
-    heads = half // HDIM
-    v, _, _, _, qk = projected(proj, half)
-    ins = [(ic, micro_spec(ic)), qk, v] + [(t, whole_spec(t)) for t in tables]
-    return call(own_kernel, micros, ins, [struct(micros, heads, PHI, LANES)], [], 10**9)[0]
-
-
-def mix_forward(ic, ir, proj, half, conv_in, tail_k, tail_v, prefix, tables):
-    micros, rows, _ = proj.shape
-    v, wq, wk, cg, qk = projected(proj, half)
-    rest = [(a, micro_spec(a)) for a in (conv_in, tail_k, tail_v, prefix)]
-    ins = (
-        [(ic, micro_spec(ic)), (ir, micro_spec(ir)), qk, v, wq, wk, cg]
-        + rest
-        + [(t, whole_spec(t)) for t in tables]
-    )
+    outs = [struct(micros, rows, half, dtype=f32)]
+    return call(window_kernel, micros, ins + awaited(after), outs, scratch, 3 * 10**10)[0]
+
+
+def linear_forward(ic, ir, kv, part, prefix, tables):
+    micros, rows, _ = kv.shape
+    half = split_kv(kv)[0]
+    ins = micro_ins(ic, ir, kv, part, prefix) + table_ins(tables)
     outs = [
         struct(micros, rows, half),
         struct(micros, rows, half),
         struct(micros, rows, LANES, dtype=f32),
     ]
-    scratch = [
-        pltpu.VMEM((rows, rows), f32),
-        pltpu.VMEM((rows, TILE + WIN), f32),
-        pltpu.VMEM((rows + WIN, half), bf16),
-        pltpu.VMEM((rows + WIN, half), bf16),
-    ]
-    return call(mix_kernel, micros, ins, outs, scratch, 10**10)
-
-
-def prefix_gradient(ic, proj, half, dm, linear, rden, tables):
-    micros = proj.shape[0]
-    heads = half // HDIM
-    qk = projected(proj, half)[4]
+    return call(linear_kernel, micros, ins, outs, [pltpu.VMEM((rows, rows), f32)], 2 * 10**10)
+
+
+def prefix_gradient(ic, kv, dm, linear, rden, tables):
+    micros = kv.shape[0]
+    heads = split_kv(kv)[0] // HDIM
+    ins = micro_ins(ic, kv, dm, linear, rden) + table_ins(tables)
+    outs = [struct(micros, heads, PHI, LANES)]
+    return call(prefix_grad_kernel, micros, ins, outs, [], 10**9)[0]
+
+
+def mix_backward(ic, ir, kv, rest, tail_k, tail_v, prefix, tables, dm, linear, rden, after):
+    micros, rows, _ = kv.shape
+    half, width = split_kv(kv)
     ins = (
-        [(ic, micro_spec(ic)), qk]
-        + [(a, micro_spec(a)) for a in (dm, linear, rden)]
-        + [(t, whole_spec(t)) for t in tables]
-    )
-    return call(
-        prefix_grad_kernel, micros, ins, [struct(micros, heads, PHI, LANES)], [], 10**9
-    )[0]
-
-
-def mix_backward(ic, ir, proj, half, conv_in, tail_k, tail_v, prefix, tables, dm, linear, rden):
-    micros, rows, _ = proj.shape
-    width = (proj.shape[2] - 4 * half) // 2
-    v, wq, wk, cg, qk = projected(proj, half)
-    ins = (
-        [(ic, micro_spec(ic)), (ir, micro_spec(ir)), qk, v, wq, wk, cg]
-        + [(a, micro_spec(a)) for a in (conv_in, tail_k, tail_v, prefix)]
-        + [(t, whole_spec(t)) for t in tables]
-        + [(a, micro_spec(a)) for a in (dm, linear, rden)]
+        micro_ins(ic, ir, kv)
+        + parts_of(rest, half)[:2]
+        + micro_ins(tail_k, tail_v, prefix)
+        + table_ins(tables)
+        + micro_ins(dm, linear, rden)
+        + awaited(after)
     )
     outs = [
         struct(micros, rows, width),
@@ -415,8 +432,6 @@
         struct(micros, rows, half, dtype=f32),
         struct(micros, rows, half),
         struct(micros, rows, half, dtype=f32),
-        struct(micros, rows, half),
-        struct(micros, rows, half),
         struct(micros, WIN, half),
         struct(micros, WIN, half),
     ]
@@ -430,18 +445,17 @@
         pltpu.VMEM((rows + WIN, HDIM), f32),
         pltpu.VMEM((rows + WIN, HDIM), f32),
     ]
-    return call(mix_grad_kernel, micros, ins, outs, scratch, 2 * 10**10)
-
-
-def finish_gradients(ic, proj, half, d_own, tables, dk, dv, dwk, dwq, dcg, dq, back_k, back_v):
-    micros = proj.shape[0]
-    v, _, _, _, qk = projected(proj, half)
+    return call(mix_grad_kernel, micros, ins, outs, scratch, 8 * 10**10)
+
+
+def finish_gradients(ic, kv, rest, d_own, tables, dk, dv, dwk, dwq, dcg, dq, back_k, back_v):
     ins = (
-        [(ic, micro_spec(ic)), qk, v, (d_own, micro_spec(d_own))]
-        + [(t, whole_spec(t)) for t in tables]
-        + [(a, micro_spec(a)) for a in (dk, dv, dwk, dwq, dcg, dq, back_k, back_v)]
+        micro_ins(ic, kv, d_own)
+        + table_ins(tables)
+        + micro_ins(dk, dv, dwk, dwq, dcg, dq, back_k, back_v)
     )
-    return call(finish_kernel, micros, ins, [struct(*proj.shape)], [], 2 * 10**9)[0]
+    outs = [struct(*kv.shape), struct(*rest.shape)]
+    return call(finish_kernel, kv.shape[0], ins, outs, [], 2 * 10**9)
 
 
 def cut_axis(size):
@@ -605,9 +619,16 @@
     return made[:count], made[count:]
 
 
-def scatter_kernel(dims, plan, depth, count, *refs):
-    grads, outs = refs[:count], refs[count : 2 * count]
-    rest = refs[2 * count :]
+def scatter_kernel(dims, plan, depth, cuts, *refs):
+    count, made = len(cuts), sum(len(c) for c in cuts)
+    grads, rest = refs[:count], refs[-(made + 4 * len(plan) + 3) :]
+    outs, rest = list(rest[:made]), rest[made:]
+    pieces = []
+    for w, widths in enumerate(cuts):
+        at = 0
+        for width in widths:
+            pieces.append((w, at, at + width, outs[len(pieces)]))
+            at += width
     n = len(plan)
     landed, sums = rest[: 3 * n], rest[3 * n : 4 * n]
     own_sem, send, recv = rest[4 * n :]
@@ -687,7 +708,10 @@
             if phase < 2:
                 sums[k][at] = total.astype(bf16)
             else:
-                outs[w][:, c0:c1] = total
+                for owner, first, last, out in pieces:
+                    low, high = max(first, c0), min(last, c1)
+                    if owner == w and low < high:
+                        out[:, low - first : high - first] = total[:, low - c0 : high - c0]
             return carry
 
         if size == 1:
@@ -702,8 +726,7 @@
             copy.wait_send()
 
 
-def scatter_all(grads, plan, dims, depth, collective_id):
-    count = len(grads)
+def scatter_all(grads, cuts, after, plan, dims, depth, collective_id):
     sems = len(plan) * sum(d - 1 for d in dims)
     rows = grads[0].shape[3]
     landed, sums = [], []
@@ -715,10 +738,10 @@
         sums.append(pltpu.VMEM(keep + (rows, c1 - c0), bf16))
     size = 2 * math.prod(dims) * sum(g.shape[3] * g.shape[4] for g in grads)
     return pl.pallas_call(
-        functools.partial(scatter_kernel, dims, plan, depth, count),
-        in_specs=[pl.BlockSpec(memory_space=pl.ANY)] * count,
-        out_specs=[pl.BlockSpec(memory_space=pltpu.VMEM)] * count,
-        out_shape=[jax.ShapeDtypeStruct(g.shape[3:], f32) for g in grads],
+        functools.partial(scatter_kernel, dims, plan, depth, cuts),
+        in_specs=[pl.BlockSpec(memory_space=pl.ANY)] * (len(grads) + len(after)),
+        out_specs=[pl.BlockSpec(memory_space=pltpu.VMEM)] * sum(len(c) for c in cuts),
+        out_shape=[jax.ShapeDtypeStruct((rows, width), f32) for c in cuts for width in c],
         scratch_shapes=landed
         + sums
         + [
@@ -730,7 +753,7 @@
             collective_id=collective_id, has_side_effects=True, vmem_limit_bytes=VMEM_BYTES
         ),
         cost_estimate=pl.CostEstimate(flops=0, bytes_accessed=10 * size, transcendentals=0),
-    )(*grads)
+    )(*grads, *after)
 
 
 def ring_pairs(dims, axis, shift):
@@ -781,6 +804,19 @@
     return slot, start, positions - start < length
 
 
+def gather_heads(part, dims, axis):
+    size = dims[axis]
+    c = coords(lax.axis_index("seq"), dims)[axis]
+    pieces = [part] + [along(part, dims, axis, shift) for shift in range(1, size)]
+    ordered = []
+    for place in range(size):
+        piece = pieces[0]
+        for shift in range(1, size):
+            piece = jnp.where(lax.rem(c + size - shift, size) == place, pieces[shift], piece)
+        ordered.append(piece)
+    return jnp.concatenate(ordered, axis=1)
+
+
 def carry_over(own, starts, rows, dims, backward):
     me = lax.axis_index("seq")
     here = coords(me, dims)
@@ -792,10 +828,23 @@
     def weigh(flag, x):
         return jnp.where(flag[:, None, None, None], x.astype(f32), 0.0)
 
-    result = None
+    result, totals = None, []
     total = own
+    plane = dims[1] * dims[2]
     for axis in (2, 1, 0):
         size, stride = dims[axis], strides(dims)[axis]
+        if axis == 0 and not backward and size > 1 and own.shape[1] % plane == 0:
+            share = own.shape[1] // plane
+            mine = lax.dynamic_slice_in_dim(total, lax.rem(me, plane) * share, share, 1)
+            near = None
+            for shift in range(1, size):
+                j = lax.rem(here[0] + size - shift, size)
+                flag = (j < here[0]) & unbroken((j + 1) * plane, here[0] * plane - 1)
+                part = weigh(flag, along(mine, dims, 0, shift))
+                near = part if near is None else near + part
+            near = gather_heads(gather_heads(near.astype(own.dtype), dims, 2), dims, 1)
+            result = result + weigh(unbroken(here[0] * plane, me - 1), near)
+            continue
         base = me // (stride * size) * (stride * size)
         c = here[axis]
         if size == 1:
@@ -818,7 +867,8 @@
             result = part if result is None else result + part
             added = added + weigh(gap(j), got)
         total = added.astype(own.dtype)
-    return result.astype(own.dtype)
+        totals.append(total)
+    return result.astype(own.dtype), totals
 
 
 def rsq(v):
@@ -863,11 +913,12 @@
 
     small = jnp.concatenate([norm_gains, conv_filter], axis=0).T
     small = jnp.pad(small, ((0, 0), (0, LANES - small.shape[1])))
-    pack_in = jnp.concatenate([w_value, w_wquery, w_wkey, w_conv_gate, w_query, w_key], axis=1)
-    shards = (small, pack_in, w_conv_in, w_out.T, w_gate)
+    pack_kv = jnp.concatenate([w_value, w_query, w_key], axis=1)
+    pack_rest = jnp.concatenate([w_wquery, w_wkey, w_conv_gate], axis=1)
+    shards = (small, pack_kv, pack_rest, w_conv_in, w_out.T, w_gate)
     plan = chunk_plan([s.shape[1] for s in shards], FIRST)
     fulls, later = gather_all(shards, (w_up, w_down.T), plan, dims, 3, 1)
-    small_all, full_in, full_conv, full_out, full_gate = [
+    small_all, full_kv, full_rest, full_conv, full_out, full_gate = [
         full.reshape(-1, full.shape[-1]) for full in fulls
     ]
     full_up, full_down = [lax.all_gather(s, "seq", axis=0, tiled=True) for s in later]
@@ -913,12 +964,12 @@
     width = h1.shape[2]
     h1_prev = shifted(h1[:, rows - (KCONV - 1) :], 1)
     flat_h1 = h1.reshape(micros * rows, width)
-    proj = mul(flat_h1, full_in).astype(bf16).reshape(micros, rows, -1)
-
-    tail_v = shifted(proj[:, rows - WIN :, :half], 1)
-    tail_k = shifted(proj[:, rows - WIN :, 2 * half : 3 * half], 1)
-    own = own_states(ic, proj, half, tables)
-    prefix = carry_over(own, starts, rows, dims, False)
+    kv = mul(flat_h1, full_kv).astype(bf16).reshape(micros, rows, -1)
+    own = own_states(ic, kv, tables)
+    prefix, totals = carry_over(own, starts, rows, dims, False)
+    rest = mul(flat_h1, full_rest).astype(bf16).reshape(micros, rows, -1)
+    tail_v = shifted(kv[:, rows - WIN :, :half], 1)
+    tail_k = shifted(rest[:, rows - WIN :, half : 2 * half], 1)
 
     stacked = jnp.concatenate([h1_prev, h1], axis=1)
     h1f = h1.astype(f32)
@@ -933,9 +984,8 @@
     flat_conv = conv.reshape(micros * rows, width)
     conv_in = mul(flat_conv, full_conv).astype(bf16).reshape(micros, rows, half)
 
-    mixed, linear, rden = mix_forward(
-        ic, ir, proj, half, conv_in, tail_k, tail_v, prefix, tables
-    )
+    part = window_forward(ic, ir, kv, rest, conv_in, tail_k, tail_v, (totals[1],))
+    mixed, linear, rden = linear_forward(ic, ir, kv, part, prefix, tables)
     flat_mixed = mixed.reshape(micros * rows, half)
     resid = x.reshape(micros * rows, width) + core_sum(mul_t(flat_mixed, full_out))
 
@@ -970,16 +1020,21 @@
 
     grad_out = t_mul(d_resid_low, flat_mixed).astype(bf16)
     d_mixed = mul(d_resid_low, full_out).astype(bf16).reshape(micros, rows, half)
-    d_prefix = prefix_gradient(ic, proj, half, d_mixed, linear, rden, tables)
-    d_own = carry_over(d_prefix, starts, rows, dims, True)
-    dq, dk, dv, dwq, dwk, dcg, dci, back_k, back_v = mix_backward(
-        ic, ir, proj, half, conv_in, tail_k, tail_v, prefix, tables, d_mixed, linear, rden
+    d_prefix = prefix_gradient(ic, kv, d_mixed, linear, rden, tables)
+    d_own, totals = carry_over(d_prefix, starts, rows, dims, True)
+    gate_rows = rest[:, :, 2 * half :].astype(f32)
+    dm = d_mixed.astype(f32)
+    dci = (dm * gate_rows).astype(bf16)
+    dcg = (dm * conv_in.astype(f32)).astype(bf16)
+    flat_dci = dci.reshape(micros * rows, half)
+    grad_conv = t_mul(flat_conv, flat_dci).astype(bf16)
+    d_conv = mul_t(flat_dci, full_conv).reshape(micros, rows, width)
+    dq, dk, dv, dwq, dwk, back_k, back_v = mix_backward(
+        ic, ir, kv, rest, tail_k, tail_v, prefix, tables, d_mixed, linear, rden,
+        (totals[1], d_conv, grad_conv, grad_out),
     )
     back_k = shifted(back_k, -1)
     back_v = shifted(back_v, -1)
-    flat_dci = dci.reshape(micros * rows, half)
-    grad_conv = t_mul(flat_conv, flat_dci).astype(bf16)
-    d_conv = mul_t(flat_dci, full_conv).reshape(micros, rows, width)
     d_h1 = taps[0] * d_conv
     d_taps = [jnp.sum(d_conv * h1f, axis=(0, 1))]
     before = jnp.zeros((micros, KCONV - 1, width), f32)
@@ -991,11 +1046,16 @@
         before = before + jnp.pad(moved[:, :s], ((0, 0), (KCONV - 1 - s, 0), (0, 0)))
     returned = shifted(before.astype(bf16), -1).astype(f32)
     d_h1 = d_h1 + jnp.pad(returned, ((0, 0), (rows - (KCONV - 1), 0), (0, 0)))
-    d_proj = finish_gradients(
-        ic, proj, half, d_own, tables, dk, dv, dwk, dwq, dcg, dq, back_k, back_v
-    ).reshape(micros * rows, -1)
-    grad_in = t_mul(flat_h1, d_proj).astype(bf16)
-    d_h1 = core_sum(d_h1.reshape(micros * rows, width) + mul_t(d_proj, full_in))
+    d_kv, d_rest = [
+        d.reshape(micros * rows, -1)
+        for d in finish_gradients(
+            ic, kv, rest, d_own, tables, dk, dv, dwk, dwq, dcg, dq, back_k, back_v
+        )
+    ]
+    grad_kv = t_mul(flat_h1, d_kv).astype(bf16)
+    grad_rest = t_mul(flat_h1, d_rest).astype(bf16)
+    d_h1 = d_h1.reshape(micros * rows, width) + mul_t(d_kv, full_kv) + mul_t(d_rest, full_rest)
+    d_h1 = core_sum(d_h1)
     d_x, d_gain1 = norm_back(
         x.reshape(micros * rows, width), r1.reshape(micros * rows, 1), gain1, d_h1
     )
@@ -1007,13 +1067,17 @@
     d_small = jnp.pad(d_small, ((0, 0), (0, LANES - d_small.shape[1])))
     grads = [
         g.astype(bf16).reshape(dims + (-1, g.shape[1]))
-        for g in (grad_up, grad_out, grad_conv, grad_in, d_small)
+        for g in (grad_up, grad_out, grad_conv, grad_rest, grad_kv, d_small)
     ]
+    cuts = [[g.shape[4]] for g in grads]
+    cuts[3], cuts[4] = [half] * 3, [half, qk, qk]
     plan = [
         (w, first, last, order[::-1])
         for w, first, last, order in chunk_plan([g.shape[4] for g in grads], LAST)
     ]
-    sum_up, sum_out, sum_conv, sum_in, sum_small = scatter_all(grads, plan, dims, 3, 2)
+    sum_up, sum_out, sum_conv, s_wq, s_wk, s_cg, s_v, s_q, s_k, sum_small = scatter_all(
+        grads, cuts, (sum_gate, sum_down), plan, dims, 2, 2
+    )
     sum_small = sum_small.T
     gains_count = norm_gains.shape[0]
     return (
@@ -1021,13 +1085,13 @@
         grad_input,
         sum_small[:gains_count],
         sum_small[gains_count : gains_count + KCONV],
-        sum_in[:, 4 * half : 4 * half + qk],
-        sum_in[:, 4 * half + qk :],
-        sum_in[:, :half],
-        sum_in[:, half : 2 * half],
-        sum_in[:, 2 * half : 3 * half],
+        s_q,
+        s_k,
+        s_v,
+        s_wq,
+        s_wk,
         sum_conv,
-        sum_in[:, 3 * half : 4 * half],
+        s_cg,
         sum_out.T,
         sum_gate,
         sum_up,

time: 1340 us -> 1240 us (0.925)
  waiting for transfers between devices: 248 us -> 132 us
    ppermute x10 -> x12, waiting for transfers between devices: 244 us -> 91.9 us  [along(): return lax.ppermute(x, 'seq', ring_pairs(dims, axis, shift))]
    all_gather x2, waiting for transfers between devices: 0.01 us -> 18.2 us  [per_device(): lax.all_gather(s, 'seq', axis=0, tiled=True)]
    pallas_call x5 -> x6, Pallas kernels: 167 us -> 153 us  [call(): pl.pallas_call(kernel, grid=(micros,), in_specs=[spec for _, spec in ins]...]
    dot_general x6 -> x7, matrix products: 90.1 us -> 99.2 us  [mul_t(): lax.dot_general(a, b, (((1,), (1,)), ((), ())), preferred_element_type=f32)]
    ppermute x10 -> x12, starting transfers between devices: 19.9 us -> 28.2 us  [along(): return lax.ppermute(x, 'seq', ring_pairs(dims, axis, shift))]
    unnamed x183 -> x192, local copies, waits for them, and re-layouts: 23.7 us -> 28.6 us
    dot_general x6 -> x7, matrix products: 70.4 us -> 74.4 us  [mul(): lax.dot_general(a, b, (((1,), (0,)), ((), ())), preferred_element_type=f32)]
    dot_general x6 -> x7, matrix products: 77.6 us -> 77.4 us  [t_mul(): lax.dot_general(a, b, (((0,), (0,)), ((), ())), preferred_element_type=f32)]
  transfers between devices with their start and end apart: 27 -> 29, of which waited for: 9 -> 11; matrix products, arithmetic and copies ran while one was open for 25% -> 27% of each run, Pallas kernels for 32% -> 12%
where the time goes in v3:
time: 1240 us; the launch traced here: 1230 us
  Pallas kernels  670 us (54%)
  matrix products  251 us (20%)
  waiting for transfers between devices  132 us (11%)
  other arithmetic  75.8 us (6%)
  local copies, waits for them, and re-layouts  47.9 us (4%)
  starting transfers between devices  42.2 us (3%)
  between operations  15.8 us (1%)
    pallas_call x1, Pallas kernels, gather_all(): pl.pallas_call(functools.partial(gather_kernel, dims, plan, depth, count,...  259 us
    pallas_call x1, Pallas kernels, scatter_all(): pl.pallas_call(functools.partial(scatter_kernel, dims, plan, depth, cuts)...  258 us
    pallas_call x6, Pallas kernels, call(): pl.pallas_call(kernel, grid=(micros,), in_specs=[spec for _, spec in ins]...  153 us
    dot_general x7, matrix products, mul_t(): lax.dot_general(a, b, (((1,), (1,)), ((), ())), preferred_element_type=f32)  99.2 us
    ppermute x12, waiting for transfers between devices, along(): return lax.ppermute(x, 'seq', ring_pairs(dims, axis, shift))  91.9 us
    dot_general x7, matrix products, t_mul(): lax.dot_general(a, b, (((0,), (0,)), ((), ())), preferred_element_type=f32)  77.4 us
    dot_general x7, matrix products, mul(): lax.dot_general(a, b, (((1,), (0,)), ((), ())), preferred_element_type=f32)  74.4 us
    unnamed x192, local copies, waits for them, and re-layouts  28.6 us
  transfers between devices with their start and end apart: 29, of which 11 were waited for; matrix products, arithmetic and copies ran while one was open for 27% of the time, Pallas kernels for 12%

profile of v3, /device:TPU:0, one launch (start us, length us, event | category | flops | bytes accessed | tf_op | source)
XLA Modules:
  0.0 1234.5 jit_solution(3046488480538592324)
XLA Ops:
  12.5 258.7 %shard_map.307 = (bf16[4,2,2,112,128]{4,3,2,1,0:T(8,128)(2,1)}, bf16[4,2,2,112,1152]{4,3,2,1,0:T(8,128)(2,1)}, bf16[4,2,2,112,2688]{4,3,2,1,0:T(8,128)(2,1)}, bf...) custom-call(bf16[112,128]{1,0:T(8,128)(2,1)} %pad.64.refs_0_, ...), custom_call_target="tpu_custom_call" | custom-call | bytes 293601280 | tf_op jit(solution)/shard_map/pallas_call | solution.py:603
  292.4 8.6 shard_map.308
  311.5 21.3 %collective-permute-done.4 = bf16[2,8,160,128]{3,2,1,0:T(8,128)(2,1)S(1)} collective-permute-done((bf16[2,8,160,128]{3,2,1,0:T(8,128)(2,1)}, bf16[2,8,160,128]{3,2,1,0:T(8,128)(2,1)S(1)}, u32[]{:S(2)}, u32[]{:S(2)}) %collective-permute-start.4) | collective-permute-done | bytes 655392 | tf_op jit(solution)/shard_map/ppermute | solution.py:769
  333.2 14.0 %convolution_convert_fusion.5 = bf16[1024,2688]{1,0:T(8,128)(2,1)S(1)} fusion(bf16[1792,2688]{1,0:T(8,128)(2,1)} %bitcast.223, f32[1792]{0:T(1024)S(1)} %get-tuple-element.146, f32[1024]{0:T(1024)S(1)} %bitcast.199, bf16[1024,896]{1,0:T(8,128)(2,1)S(1)} %bitcast.160, bf16[1024,896]{1,0:T(8,128)(2,1)S(1)} %bitcast.154), kind=kOutput, calls=%fused_computation.56 | convolution fusion | flops 9880600576 | bytes 18820096 | tf_op jit(solution)/shard_map/dot_general | solution.py:31
  351.8 8.0 collective-permute-start.8
  367.9 24.5 %collective-permute-done.7 = bf16[2,2,160,128]{3,2,1,0:T(8,128)(2,1)S(1)} collective-permute-done((bf16[2,2,160,128]{3,2,1,0:T(8,128)(2,1)S(1)}, bf16[2,2,160,128]{3,2,1,0:T(8,128)(2,1)S(1)}, u32[]{:S(2)}, u32[]{:S(2)}) %collective-permute-start.7) | collective-permute-done | bytes 163872 | tf_op jit(solution)/shard_map/ppermute | solution.py:769
  400.8 28.1 %shard_map.309.part = f32[2,512,896]{2,1,0:T(8,128)} custom-call(s32[2,512,8]{2,1,0:T(8,128)} %copy.79.ic, s32[2,8,640]{2,1,0:T(8,128)} %pad_add_fusion.ir, bf16[2,512,1152]{2,1,0:T(8,128)(2,1)} %bitcast.167, bf16[2,512,2688]{2,1,0:T(8,128)(2,1)} %bitcast.214, bf16[2,512,2688]{2,1,0:T(8,128)(2,1)} %bitcast.215, bf16[2,512,2688]{2,1,0:T(8,128)(2,1)} %bitcast.216, ...), custom_call_target="tpu_custom_call" | custom-call | flops 30000001024 | bytes 11010048 | tf_op jit(solution)/shard_map/pallas_call | solution.py:336
  431.2 16.1 %shard_map.310 = (bf16[2,512,896]{2,1,0:T(8,128)(2,1)}, bf16[2,512,896]{2,1,0:T(8,128)(2,1)}, f32[2,512,128]{2,1,0:T(8,128)}) custom-call(s32[2,512,8]{2,1,0:T(8,128)} %copy.79.ic, s32[2,8,640]{2,1,0:T(8,128)} %pad_add_fusion.ir, bf16[2,512,1152]{2,1,0:T(8,128)(2,1)} %bitcast.168, f32[2,512,896]{2,1,0:T(8,128)} %shard_map.309.part, ...), custom_call_target="tpu_custom_call" | custom-call | flops 20000000000 | bytes 12582912 | tf_op jit(solution)/shard_map/pallas_call | solution.py:336
  454.4 8.5 collective-permute-done.13
  473.3 11.8 convolution_convert_fusion.4
  485.1 14.3 %convolution_convert_fusion.3 = bf16[1024,2432]{1,0:T(8,128)(2,1)S(1)} fusion(bf16[1024,1792]{1,0:T(8,128)(2,1)} %copy-done.18, bf16[1792,2432]{1,0:T(8,128)(2,1)} %all-gather.3.cloned.1.call-done), kind=kOutput, calls=%fused_computation.54 | convolution fusion | flops 8927969280 | bytes 17367040 | tf_op jit(solution)/shard_map/dot_general | solution.py:31
  501.6 12.9 %convolution_convert_fusion = bf16[1792,2432]{1,0:T(8,128)(2,1)} fusion(bf16[1024,1792]{1,0:T(8,128)(2,1)S(1)} %bitcast.172, bf16[1024,2432]{1,0:T(8,128)(2,1)S(1)} %convolution_convert_fusion.3, bf16[1024,2432]{1,0:T(8,128)(2,1)S(1)} %copy-done.74), kind=kOutput, calls=%fused_computation.6 | convolution fusion | flops 8949760000 | bytes 22347776 | tf_op jit(solution)/shard_map/dot_general | solution.py:39
  520.3 18.2 %all-gather.5.cloned.1.call-done = bf16[1792,2432]{1,0:T(8,128)(2,1)} async-done(((bf16[112,2432]{1,0:T(8,128)(2,1)}), bf16[1792,2432]{1,0:T(8,128)(2,1)}) %all-gather.5.cloned.1.call-update) | async-done | bytes 8716304 | tf_op jit(solution)/shard_map/all_gather | solution.py:924
  538.5 16.8 %convolution_convert_fusion.6 = bf16[1024,1792]{1,0:T(8,128)(2,1)S(1)} fusion(bf16[1792,2432]{1,0:T(8,128)(2,1)} %all-gather.5.cloned.1.call-done, bf16[1024,2432]{1,0:T(8,128)(2,1)} %copy-done.75, bf16[1024,2432]{1,0:T(8,128)(2,1)} %convolution_convert_fusion.4), kind=kOutput, calls=%fused_computation.59 | convolution fusion | flops 8947236864 | bytes 22347776 | tf_op jit(solution)/shard_map/dot_general | solution.py:35
  556.9 18.9 %multiply_convert_fusion = (bf16[1024,2432]{1,0:T(8,128)(2,1)}, bf16[1024,2432]{1,0:T(8,128)(2,1)}) fusion(bf16[1024,2432]{1,0:T(8,128)(2,1)} %convolution_convert_fusion.4, bf16[1024,2432]{1,0:T(8,128)(2,1)} %copy-done.75, bf16[1024,1792]{1,0:T(8,128)(2,1)S(1)} %bitcast.173, bf16[1792,2432]{1,0:T(8,128)(2,1)} %all-gather.5.cloned.1.call-done), kind=kOutput, calls=%fused_computation.17 | convolution fusion | flops 8962834432 | bytes 32309248 | tf_op jit(solution)/shard_map/dot_general | solution.py:31
  575.8 16.1 %fusion.63 = f32[1024,1792]{1,0:T(8,128)} fusion(bf16[1024,2432]{1,0:T(8,128)(2,1)} %get-tuple-element.185, bf16[1792,2432]{1,0:T(8,128)(2,1)} %bitcast.225), kind=kOutput, calls=%fused_computation.297 | convolution fusion | flops 8925478912 | bytes 21037056 | tf_op jit(solution)/shard_map/dot_general | solution.py:35
  591.9 15.7 %add_convert_fusion = bf16[1024,1792]{1,0:T(8,128)(2,1)} fusion(f32[1024,1792]{1,0:T(8,128)} %fusion.63, bf16[1024,2432]{1,0:T(8,128)(2,1)S(1)} %copy-done.76, bf16[1792,2432]{1,0:T(8,128)(2,1)} %all-gather.3.cloned.1.call-done), kind=kOutput, calls=%fused_computation.46 | convolution fusion | flops 8929148928 | bytes 24707072 | tf_op jit(solution)/shard_map/dot_general | solution.py:35
  607.8 14.6 %convolution_convert_fusion.1 = bf16[1792,2432]{1,0:T(8,128)(2,1)} fusion(bf16[1024,1792]{1,0:T(8,128)(2,1)S(1)} %copy-done.19, bf16[1024,2432]{1,0:T(8,128)(2,1)} %get-tuple-element.185), kind=kOutput, calls=%fused_computation.7 | convolution fusion | flops 8929837056 | bytes 17367040 | tf_op jit(solution)/shard_map/dot_general | solution.py:39
  622.5 15.2 %convolution_convert_fusion.2 = bf16[1792,2432]{1,0:T(8,128)(2,1)} fusion(bf16[1024,1792]{1,0:T(8,128)(2,1)} %copy-done.18, bf16[1024,2432]{1,0:T(8,128)(2,1)} %get-tuple-element.184), kind=kOutput, calls=%fused_computation.8 | convolution fusion | flops 8929837056 | bytes 17367040 | tf_op jit(solution)/shard_map/dot_general | solution.py:39
  660.6 13.2 %multiply_reduce_fusion.1 = (f32[1792]{0:T(1024)S(1)}, f32[1792]{0:T(1024)S(1)}, f32[1792]{0:T(1024)S(1)}, f32[2,512,1792]{2,1,0:T(8,128)}, f32[2,512,1792]{2,1,0:T(8,128)}, /*index=5*/f32[2,512,1792]{2,1,0:T(8,128)}) fusion(f32[2,512]{1,0:T(2,128)S(1)} %bitcast.210, bf16[2,512,1792]{2,1,0:T(8,128)(2,1)S(1)} %copy-done.9, ...), kind=kOutput, calls=%fused_computation.35 | convolution fusion | flops 3330534144 | bytes 32629760 | tf_op jit(solution)/shard_map/dot_general | solution.py:35
  681.2 14.6 %shard_map.311 = bf16[2,8,160,128]{3,2,1,0:T(8,128)(2,1)} custom-call(s32[2,512,8]{2,1,0:T(8,128)} %copy.79.ic, bf16[2,512,1152]{2,1,0:T(8,128)(2,1)} %bitcast.169, bf16[2,512,896]{2,1,0:T(8,128)(2,1)} %bitcast.179, bf16[2,512,896]{2,1,0:T(8,128)(2,1)} %get-tuple-element.54.linear, f32[2,512,128]{2,1,0:T(8,128)} %get-tuple-element.55.rden, ...), custom_call_target="tpu_custom_call" | custom-call | flops 1000000000 | bytes 1966080 | tf_op jit(solution)/shard_map/pallas_call | solution.py:336
  704.0 9.1 bitcast_convert_fusion.1.rest_2_
  713.1 22.6 %collective-permute-done.16 = bf16[2,8,160,128]{3,2,1,0:T(8,128)(2,1)S(1)} collective-permute-done((bf16[2,8,160,128]{3,2,1,0:T(8,128)(2,1)}, bf16[2,8,160,128]{3,2,1,0:T(8,128)(2,1)S(1)}, u32[]{:S(2)}, u32[]{:S(2)}) %collective-permute-start.16) | collective-permute-done | bytes 655392 | tf_op jit(solution)/shard_map/ppermute | solution.py:769
  743.1 13.4 %collective-permute-done.17 = bf16[2,8,160,128]{3,2,1,0:T(8,128)(2,1)S(1)} collective-permute-done((bf16[2,8,160,128]{3,2,1,0:T(8,128)(2,1)S(1)}, bf16[2,8,160,128]{3,2,1,0:T(8,128)(2,1)S(1)}, u32[]{:S(2)}, u32[]{:S(2)}) %collective-permute-start.17) | collective-permute-done | bytes 655392 | tf_op jit(solution)/shard_map/ppermute | solution.py:769
  757.0 8.2 collective-permute-start.19
  767.1 70.9 %shard_map.312 = (bf16[2,512,128]{2,1,0:T(8,128)(2,1)}, f32[2,512,128]{2,1,0:T(8,128)}, f32[2,512,896]{2,1,0:T(8,128)}, bf16[2,512,896]{2,1,0:T(8,128)(2,1)}, f3...) custom-call(s32[2,512,8]{2,1,0:T(8,128)} %copy.79.ic, ...), custom_call_target="tpu_custom_call" | custom-call | flops 80000000000 | bytes 31260672 | tf_op jit(solution)/shard_map/pallas_call | solution.py:336
  853.7 8.5 collective-permute-done.22.back_v
  862.9 14.5 %shard_map.313 = (bf16[2,512,1152]{2,1,0:T(8,128)(2,1)}, bf16[2,512,2688]{2,1,0:T(8,128)(2,1)}) custom-call(s32[2,512,8]{2,1,0:T(8,128)} %copy.79.ic, bf16[2,512,1152]{2,1,0:T(8,128)(2,1)} %bitcast.171, bf16[2,8,160,128]{3,2,1,0:T(8,128)(2,1)} %fusion.40.d_own, bf16[8,128,160]{2,1,0:T(8,128)(2,1)} %constant.312.clone.left, ...), custom_call_target="tpu_custom_call" | custom-call | flops 2000000000 | bytes 23592960 | tf_op jit(solution)/shard_map/pallas_call | solution.py:336
  877.4 10.8 fusion.64
  888.2 20.0 %fusion.17 = bf16[1024,1792]{1,0:T(8,128)(2,1)} fusion(f32[1024,1792]{1,0:T(8,128)} %fusion.64, f32[2,512,1792]{2,1,0:T(8,128)} %convert_add_fusion.1, bf16[1024,2688]{1,0:T(8,128)(2,1)} %bitcast.229, bf16[1792,2688]{1,0:T(8,128)(2,1)} %bitcast.224), kind=kOutput, calls=%fused_computation.33 | convolution fusion | flops 9870508032 | bytes 33488896 | tf_op jit(solution)/shard_map/dot_general | solution.py:35
  921.2 13.3 %bitcast_convert_fusion = bf16[1792,2688]{1,0:T(8,128)(2,1)} fusion(bf16[2,512,1792]{2,1,0:T(8,128)(2,1)S(1)} %copy-done.10, bf16[2,512,2688]{2,1,0:T(8,128)(2,1)S(1)} %bitcast.231), kind=kOutput, calls=%fused_computation | convolution fusion | flops 9869819904 | bytes 18808832 | tf_op jit(solution)/shard_map/dot_general | solution.py:39
  951.6 258.5 %shard_map.314 = (f32[112,2432]{1,0:T(8,128)}, f32[112,896]{1,0:T(8,128)}, f32[112,896]{1,0:T(8,128)}, f32[112,896]{1,0:T(8,128)}, f32[112,896]{1,0:T(8,128)}, /...) custom-call(bf16[4,2,2,112,2432]{4,3,2,1,0:T(8,128)(2,1)} %bitcast.1, ...), custom_call_target="tpu_custom_call" | custom-call | bytes 293601280 | tf_op jit(solution)/shard_map/pallas_call | solution.py:740
  (391 shorter events, 198.9 us)
Async XLA Ops:
  7.2 264.1 %copy-start.23 = (bf16[2,512,896]{2,1,0:T(8,128)(2,1)S(1)}, bf16[2,512,896]{2,1,0:T(8,128)(2,1)}, u32[]{:S(2)}) copy-start(bf16[2,512,896]{2,1,0:T(8,128)(2,1)} %param.20) | copy-start | bytes 5505028
  7.2 265.1 %copy-start.65 = (s32[2,4]{1,0:T(2,128)S(1)}, s32[2,4]{1,0:T(2,128)}, u32[]{:S(2)}) copy-start(s32[2,4]{1,0:T(2,128)} %param.22) | copy-start | bytes 100
  7.2 265.1 %copy-start.66 = (s32[2,4]{1,0:T(2,128)S(1)}, s32[2,4]{1,0:T(2,128)}, u32[]{:S(2)}) copy-start(s32[2,4]{1,0:T(2,128)} %param.23) | copy-start | bytes 100
  7.2 477.9 %all-gather.3.cloned.1.call-start = ((), (), s32[]{:S(2)}) async-start(), calls=%async_computation.2 | async-start | bytes 9261056 | tf_op jit(solution)/shard_map/all_gather | solution.py:924
  271.2 267.3 %all-gather.5.cloned.1.call-start = ((), (), s32[]{:S(2)}) async-start(), calls=%async_computation.3 | async-start | bytes 9261056 | tf_op jit(solution)/shard_map/all_gather | solution.py:924
  271.3 10.9 collective-permute-start
  272.0 675.0 %reduce-scatter.5.cloned.1.call-start = ((), (), s32[]{:S(2)}) async-start(), calls=%async_computation.5 | async-start | bytes 9261056 | tf_op jit(solution)/shard_map/reduce_scatter | solution.py:1000
  301.0 31.8 %collective-permute-start.4 = (bf16[2,8,160,128]{3,2,1,0:T(8,128)(2,1)}, bf16[2,8,160,128]{3,2,1,0:T(8,128)(2,1)S(1)}, u32[]{:S(2)}, u32[]{:S(2)}) collective-permute-start(bf16[2,8,160,128]{3,2,1,0:T(8,128)(2,1)} %shard_map.308), channel_id=1, source_target_pairs={{0,2},{2,0},{4,6},{6,4},{8,10},{10,8},{12,14},{14,12},{16,18},{18,... | collective-permute-start | bytes 1966088 | tf_op jit(solution)/shard_map/ppermute | solution.py:769
  305.1 94.3 %collective-permute-start.3 = (bf16[2,64,896]{2,1,0:T(8,128)(2,1)S(1)}, bf16[2,64,896]{2,1,0:T(8,128)(2,1)S(1)}, u32[]{:S(2)}, u32[]{:S(2)}) collective-permute-start(bf16[2,64,896]{2,1,0:T(8,128)(2,1)S(1)} %slice.152), channel_id=1, source_target_pairs={{0,2},{2,4},{4,6},{6,8},{8,10},{10,12},{12,14},{14,16},{16,18},{18... | collective-permute-start | bytes 688136 | tf_op jit(solution)/shard_map/ppermute | solution.py:789
  309.4 50.4 %collective-permute-start.1 = (bf16[2,2,1792]{2,1,0:T(2,128)(2,1)S(1)}, bf16[2,2,1792]{2,1,0:T(2,128)(2,1)S(1)}, u32[]{:S(2)}, u32[]{:S(2)}) collective-permute-start(bf16[2,2,1792]{2,1,0:T(2,128)(2,1)S(1)} %slice.145), channel_id=1, source_target_pairs={{0,2},{2,4},{4,6},{6,8},{8,10},{10,12},{12,14},{14,16},{16,18},{18... | collective-permute-start | bytes 43016 | tf_op jit(solution)/shard_map/ppermute | solution.py:789
  333.1 18.3 %collective-permute-start.5 = (bf16[2,8,160,128]{3,2,1,0:T(8,128)(2,1)S(1)}, bf16[2,8,160,128]{3,2,1,0:T(8,128)(2,1)S(1)}, u32[]{:S(2)}, u32[]{:S(2)}) collective-permute-start(bf16[2,8,160,128]{3,2,1,0:T(8,128)(2,1)S(1)} %fusion.30), channel_id=1, source_target_pairs={{0,4},{2,6},{4,0},{6,2},{8,12},{10,14},{12,8},{14,10},{16,20},{18,... | collective-permute-start | bytes 1966088 | tf_op jit(solution)/shard_map/ppermute | solution.py:769
  347.2 52.2 %collective-permute-start.2 = (bf16[2,64,896]{2,1,0:T(8,128)(2,1)S(1)}, bf16[2,64,896]{2,1,0:T(8,128)(2,1)S(1)}, u32[]{:S(2)}, u32[]{:S(2)}) collective-permute-start(bf16[2,64,896]{2,1,0:T(8,128)(2,1)S(1)} %slice.151), channel_id=1, source_target_pairs={{0,2},{2,4},{4,6},{6,8},{8,10},{10,12},{12,14},{14,16},{16,18},{18... | collective-permute-start | bytes 688136 | tf_op jit(solution)/shard_map/ppermute | solution.py:789
  351.8 16.1 %collective-permute-start.8 = (bf16[2,2,160,128]{3,2,1,0:T(8,128)(2,1)S(1)}, bf16[2,2,160,128]{3,2,1,0:T(8,128)(2,1)S(1)}, u32[]{:S(2)}, u32[]{:S(2)}) collective-permute-start(bf16[2,2,160,128]{3,2,1,0:T(8,128)(2,1)S(1)} %constant_dynamic-slice_fusion.8), channel_id=1, source_target_pairs={{0,24},{2,26},{4,28},{6,30},{8,0},{10,2},{12,4},{14,6},{16,8},{18,... | collective-permute-start | bytes 491528 | tf_op jit(solution)/shard_map/ppermute | solution.py:769
  359.8 32.6 %collective-permute-start.7 = (bf16[2,2,160,128]{3,2,1,0:T(8,128)(2,1)S(1)}, bf16[2,2,160,128]{3,2,1,0:T(8,128)(2,1)S(1)}, u32[]{:S(2)}, u32[]{:S(2)}) collective-permute-start(bf16[2,2,160,128]{3,2,1,0:T(8,128)(2,1)S(1)} %constant_dynamic-slice_fusion.8), channel_id=1, source_target_pairs={{0,16},{2,18},{4,20},{6,22},{8,24},{10,26},{12,28},{14,30},{16,0},... | collective-permute-start | bytes 491528 | tf_op jit(solution)/shard_map/ppermute | solution.py:769
  359.8 32.6 %collective-permute-start.6 = (bf16[2,2,160,128]{3,2,1,0:T(8,128)(2,1)S(1)}, bf16[2,2,160,128]{3,2,1,0:T(8,128)(2,1)S(1)}, u32[]{:S(2)}, u32[]{:S(2)}) collective-permute-start(bf16[2,2,160,128]{3,2,1,0:T(8,128)(2,1)S(1)} %constant_dynamic-slice_fusion.8), channel_id=1, source_target_pairs={{0,8},{2,10},{4,12},{6,14},{8,16},{10,18},{12,20},{14,22},{16,24},... | collective-permute-start | bytes 491528 | tf_op jit(solution)/shard_map/ppermute | solution.py:769
  392.6 6.7 collective-permute-start.9
  399.3 29.6 %collective-permute-start.10 = (bf16[2,4,160,128]{3,2,1,0:T(8,128)(2,1)S(1)}, bf16[2,4,160,128]{3,2,1,0:T(8,128)(2,1)}, u32[]{:S(2)}, u32[]{:S(2)}) collective-permute-start(bf16[2,4,160,128]{3,2,1,0:T(8,128)(2,1)S(1)} %pad_maximum_fusion.5), channel_id=1, source_target_pairs={{0,4},{2,6},{4,0},{6,2},{8,12},{10,14},{12,8},{14,10},{16,20},{18,... | collective-permute-start | bytes 983048 | tf_op jit(solution)/shard_map/ppermute | solution.py:769
  453.8 11.6 collective-permute-start.11
  453.9 9.0 collective-permute-start.13
  514.6 434.9 %reduce-scatter.3.cloned.1.call-start = ((), (), s32[]{:S(2)}) async-start(), calls=%async_computation.4 | async-start | bytes 9261056 | tf_op jit(solution)/shard_map/reduce_scatter | solution.py:1015
  556.9 351.9 %collective-permute-start.12 = (bf16[1024,896]{1,0:T(8,128)(2,1)}, bf16[1024,896]{1,0:T(8,128)(2,1)}, u32[]{:S(2)}, u32[]{:S(2)}) collective-permute-start(bf16[1024,896]{1,0:T(8,128)(2,1)} %constant_dynamic-slice_fusion.7), channel_id=1, source_target_pairs={{0,1},{1,0},{2,3},{3,2},{4,5},{5,4},{6,7},{7,6},{8,9},{9,8},{10,11... | collective-permute-start | bytes 5505032 | tf_op jit(solution)/shard_map/ppermute | solution.py:773
  607.7 30.0 %collective-permute-start.14 = (bf16[1024,1792]{1,0:T(8,128)(2,1)}, bf16[1024,1792]{1,0:T(8,128)(2,1)}, u32[]{:S(2)}, u32[]{:S(2)}) collective-permute-start(bf16[1024,1792]{1,0:T(8,128)(2,1)} %add_convert_fusion), channel_id=1, source_target_pairs={{0,1},{1,0},{2,3},{3,2},{4,5},{5,4},{6,7},{7,6},{8,9},{9,8},{10,11... | collective-permute-start | bytes 11010056 | tf_op jit(solution)/shard_map/ppermute | solution.py:773
  695.7 39.9 %collective-permute-start.16 = (bf16[2,8,160,128]{3,2,1,0:T(8,128)(2,1)}, bf16[2,8,160,128]{3,2,1,0:T(8,128)(2,1)S(1)}, u32[]{:S(2)}, u32[]{:S(2)}) collective-permute-start(bf16[2,8,160,128]{3,2,1,0:T(8,128)(2,1)} %shard_map.311), channel_id=1, source_target_pairs={{0,2},{2,0},{4,6},{6,4},{8,10},{10,8},{12,14},{14,12},{16,18},{18,... | collective-permute-start | bytes 1966088 | tf_op jit(solution)/shard_map/ppermute | solution.py:769
  702.4 36.9 %collective-permute-start.15 = (bf16[2,2,1792]{2,1,0:T(2,128)(2,1)S(1)}, bf16[2,2,1792]{2,1,0:T(2,128)(2,1)S(1)}, u32[]{:S(2)}, u32[]{:S(2)}) collective-permute-start(bf16[2,2,1792]{2,1,0:T(2,128)(2,1)S(1)} %fusion.48), channel_id=1, source_target_pairs={{2,0},{4,2},{6,4},{8,6},{10,8},{12,10},{14,12},{16,14},{18,16},{20... | collective-permute-start | bytes 43016 | tf_op jit(solution)/shard_map/ppermute | solution.py:789
  736.0 20.5 %collective-permute-start.17 = (bf16[2,8,160,128]{3,2,1,0:T(8,128)(2,1)S(1)}, bf16[2,8,160,128]{3,2,1,0:T(8,128)(2,1)S(1)}, u32[]{:S(2)}, u32[]{:S(2)}) collective-permute-start(bf16[2,8,160,128]{3,2,1,0:T(8,128)(2,1)S(1)} %fusion.42), channel_id=1, source_target_pairs={{0,4},{2,6},{4,0},{6,2},{8,12},{10,14},{12,8},{14,10},{16,20},{18,... | collective-permute-start | bytes 1966088 | tf_op jit(solution)/shard_map/ppermute | solution.py:769
  756.9 82.4 %collective-permute-start.20 = (bf16[2,8,160,128]{3,2,1,0:T(8,128)(2,1)S(1)}, bf16[2,8,160,128]{3,2,1,0:T(8,128)(2,1)S(1)}, u32[]{:S(2)}, u32[]{:S(2)}) collective-permute-start(bf16[2,8,160,128]{3,2,1,0:T(8,128)(2,1)S(1)} %fusion.44.rest_0_), channel_id=1, source_target_pairs={{0,24},{2,26},{4,28},{6,30},{8,0},{10,2},{12,4},{14,6},{16,8},{18,... | collective-permute-start | bytes 1966088 | tf_op jit(solution)/shard_map/ppermute | solution.py:769
  757.0 90.3 %collective-permute-start.19 = (bf16[2,8,160,128]{3,2,1,0:T(8,128)(2,1)S(1)}, bf16[2,8,160,128]{3,2,1,0:T(8,128)(2,1)S(1)}, u32[]{:S(2)}, u32[]{:S(2)}) collective-permute-start(bf16[2,8,160,128]{3,2,1,0:T(8,128)(2,1)S(1)} %fusion.44.rest_0_), channel_id=1, source_target_pairs={{0,16},{2,18},{4,20},{6,22},{8,24},{10,26},{12,28},{14,30},{16,0},... | collective-permute-start | bytes 1966088 | tf_op jit(solution)/shard_map/ppermute | solution.py:769
  765.2 82.0 %collective-permute-start.18 = (bf16[2,8,160,128]{3,2,1,0:T(8,128)(2,1)S(1)}, bf16[2,8,160,128]{3,2,1,0:T(8,128)(2,1)}, u32[]{:S(2)}, u32[]{:S(2)}) collective-permute-start(bf16[2,8,160,128]{3,2,1,0:T(8,128)(2,1)S(1)} %fusion.44.rest_0_), channel_id=1, source_target_pairs={{0,8},{2,10},{4,12},{6,14},{8,16},{10,18},{12,20},{14,22},{16,24},... | collective-permute-start | bytes 1966088 | tf_op jit(solution)/shard_map/ppermute | solution.py:769
  838.0 15.7 %collective-permute-start.21 = (bf16[2,64,896]{2,1,0:T(8,128)(2,1)}, bf16[2,64,896]{2,1,0:T(8,128)(2,1)S(1)}, u32[]{:S(2)}, u32[]{:S(2)}) collective-permute-start(bf16[2,64,896]{2,1,0:T(8,128)(2,1)} %get-tuple-element.61), channel_id=1, source_target_pairs={{2,0},{4,2},{6,4},{8,6},{10,8},{12,10},{14,12},{16,14},{18,16},{20... | collective-permute-start | bytes 688136 | tf_op jit(solution)/shard_map/ppermute | solution.py:789
  839.3 22.9 %collective-permute-start.22 = (bf16[2,64,896]{2,1,0:T(8,128)(2,1)}, bf16[2,64,896]{2,1,0:T(8,128)(2,1)S(1)}, u32[]{:S(2)}, u32[]{:S(2)}) collective-permute-start(bf16[2,64,896]{2,1,0:T(8,128)(2,1)} %get-tuple-element.62), channel_id=1, source_target_pairs={{2,0},{4,2},{6,4},{8,6},{10,8},{12,10},{14,12},{16,14},{18,16},{20... | collective-permute-start | bytes 688136 | tf_op jit(solution)/shard_map/ppermute | solution.py:789
  908.2 26.4 %collective-permute-start.23 = (bf16[1024,1792]{1,0:T(8,128)(2,1)}, bf16[1024,1792]{1,0:T(8,128)(2,1)S(1)}, u32[]{:S(2)}, u32[]{:S(2)}) collective-permute-start(bf16[1024,1792]{1,0:T(8,128)(2,1)} %fusion.17), channel_id=1, source_target_pairs={{0,1},{1,0},{2,3},{3,2},{4,5},{5,4},{6,7},{7,6},{8,9},{9,8},{10,11... | collective-permute-start | bytes 11010056 | tf_op jit(solution)/shard_map/ppermute | solution.py:773
  908.3 6.0 collective-permute-start.24
  (85 other events, 2598.7 us)
Sparse Core Ops, SparseCore 0:
  271.4 147.2 all-gather.2
  421.3 117.1 all-gather.4
  540.9 197.9 reduce-scatter.4
  741.0 198.1 reduce-scatter.2

commit v4 on v3

--- a/solution.py
+++ b/solution.py
@@ -620,15 +620,10 @@
 
 
 def scatter_kernel(dims, plan, depth, cuts, *refs):
-    count, made = len(cuts), sum(len(c) for c in cuts)
-    grads, rest = refs[:count], refs[-(made + 4 * len(plan) + 3) :]
-    outs, rest = list(rest[:made]), rest[made:]
-    pieces = []
-    for w, widths in enumerate(cuts):
-        at = 0
-        for width in widths:
-            pieces.append((w, at, at + width, outs[len(pieces)]))
-            at += width
+    count = len(cuts)
+    grads, rest = refs[:count], refs[-(1 + 4 * len(plan) + 3) :]
+    out, rest = rest[0], rest[1:]
+    starts = [sum(cuts[:w]) for w in range(count)]
     n = len(plan)
     landed, sums = rest[: 3 * n], rest[3 * n : 4 * n]
     own_sem, send, recv = rest[4 * n :]
@@ -708,10 +703,7 @@
             if phase < 2:
                 sums[k][at] = total.astype(bf16)
             else:
-                for owner, first, last, out in pieces:
-                    low, high = max(first, c0), min(last, c1)
-                    if owner == w and low < high:
-                        out[:, low - first : high - first] = total[:, low - c0 : high - c0]
+                out[:, starts[w] + c0 : starts[w] + c1] = total
             return carry
 
         if size == 1:
@@ -726,7 +718,8 @@
             copy.wait_send()
 
 
-def scatter_all(grads, cuts, after, plan, dims, depth, collective_id):
+def scatter_all(grads, after, plan, dims, depth, collective_id):
+    cuts = [g.shape[4] for g in grads]
     sems = len(plan) * sum(d - 1 for d in dims)
     rows = grads[0].shape[3]
     landed, sums = [], []
@@ -740,8 +733,8 @@
     return pl.pallas_call(
         functools.partial(scatter_kernel, dims, plan, depth, cuts),
         in_specs=[pl.BlockSpec(memory_space=pl.ANY)] * (len(grads) + len(after)),
-        out_specs=[pl.BlockSpec(memory_space=pltpu.VMEM)] * sum(len(c) for c in cuts),
-        out_shape=[jax.ShapeDtypeStruct((rows, width), f32) for c in cuts for width in c],
+        out_specs=pl.BlockSpec(memory_space=pltpu.VMEM),
+        out_shape=jax.ShapeDtypeStruct((rows, sum(cuts)), f32),
         scratch_shapes=landed
         + sums
         + [
@@ -1069,15 +1062,17 @@
         g.astype(bf16).reshape(dims + (-1, g.shape[1]))
         for g in (grad_up, grad_out, grad_conv, grad_rest, grad_kv, d_small)
     ]
-    cuts = [[g.shape[4]] for g in grads]
-    cuts[3], cuts[4] = [half] * 3, [half, qk, qk]
     plan = [
         (w, first, last, order[::-1])
         for w, first, last, order in chunk_plan([g.shape[4] for g in grads], LAST)
     ]
-    sum_up, sum_out, sum_conv, s_wq, s_wk, s_cg, s_v, s_q, s_k, sum_small = scatter_all(
-        grads, cuts, (sum_gate, sum_down), plan, dims, 2, 2
-    )
+    sums = scatter_all(grads, (sum_gate, sum_down), plan, dims, 2, 2)
+    ff = w_up.shape[1]
+    widths = (ff, half, half, half, half, half, half, qk, qk, LANES)
+    ends = [sum(widths[: i + 1]) for i in range(len(widths))]
+    sum_up, sum_out, sum_conv, s_wq, s_wk, s_cg, s_v, s_q, s_k, sum_small = [
+        sums[:, end - size : end] for end, size in zip(ends, widths)
+    ]
     sum_small = sum_small.T
     gains_count = norm_gains.shape[0]
     return (

time: 1240 us -> 1230 us (level)
    unnamed x192 -> x181, local copies, waits for them, and re-layouts: 28.6 us -> 13.2 us
  transfers between devices with their start and end apart: 29 -> 29, of which waited for: 11 -> 11; matrix products, arithmetic and copies ran while one was open for 27% -> 28% of each run, Pallas kernels for 12% -> 12%
where the time goes in v4:
time: 1230 us; the launch traced here: 1220 us
  Pallas kernels  670 us (54%)
  matrix products  251 us (20%)
  waiting for transfers between devices  132 us (11%)
  other arithmetic  75.9 us (6%)
  starting transfers between devices  42.3 us (3%)
  local copies, waits for them, and re-layouts  38.6 us (3%)
  between operations  15.8 us (1%)
    pallas_call x1, Pallas kernels, gather_all(): pl.pallas_call(functools.partial(gather_kernel, dims, plan, depth, count,...  259 us
    pallas_call x1, Pallas kernels, scatter_all(): pl.pallas_call(functools.partial(scatter_kernel, dims, plan, depth, cuts)...  259 us
    pallas_call x6, Pallas kernels, call(): pl.pallas_call(kernel, grid=(micros,), in_specs=[spec for _, spec in ins]...  153 us
    dot_general x7, matrix products, mul_t(): lax.dot_general(a, b, (((1,), (1,)), ((), ())), preferred_element_type=f32)  99.2 us
    ppermute x12, waiting for transfers between devices, along(): return lax.ppermute(x, 'seq', ring_pairs(dims, axis, shift))  91.8 us
    dot_general x7, matrix products, t_mul(): lax.dot_general(a, b, (((0,), (0,)), ((), ())), preferred_element_type=f32)  77.4 us
    dot_general x7, matrix products, mul(): lax.dot_general(a, b, (((1,), (0,)), ((), ())), preferred_element_type=f32)  74.3 us
    ppermute x12, starting transfers between devices, along(): return lax.ppermute(x, 'seq', ring_pairs(dims, axis, shift))  28.3 us
  transfers between devices with their start and end apart: 29, of which 11 were waited for; matrix products, arithmetic and copies ran while one was open for 28% of the time, Pallas kernels for 12%

profile of v4, /device:TPU:0, one launch (start us, length us, event | category | flops | bytes accessed | tf_op | source)
XLA Modules:
  0.0 1224.9 jit_solution(9499664995125889220)
XLA Ops:
  12.5 258.7 %shard_map.307 = (bf16[4,2,2,112,128]{4,3,2,1,0:T(8,128)(2,1)}, bf16[4,2,2,112,1152]{4,3,2,1,0:T(8,128)(2,1)}, bf16[4,2,2,112,2688]{4,3,2,1,0:T(8,128)(2,1)}, bf...) custom-call(bf16[112,128]{1,0:T(8,128)(2,1)} %pad.64.refs_0_, ...), custom_call_target="tpu_custom_call" | custom-call | bytes 293601280 | tf_op jit(solution)/shard_map/pallas_call | solution.py:603
  292.3 8.6 shard_map.308
  311.3 21.4 %collective-permute-done.4 = bf16[2,8,160,128]{3,2,1,0:T(8,128)(2,1)S(1)} collective-permute-done((bf16[2,8,160,128]{3,2,1,0:T(8,128)(2,1)}, bf16[2,8,160,128]{3,2,1,0:T(8,128)(2,1)S(1)}, u32[]{:S(2)}, u32[]{:S(2)}) %collective-permute-start.4) | collective-permute-done | bytes 655392 | tf_op jit(solution)/shard_map/ppermute | solution.py:762
  333.1 14.0 %convolution_convert_fusion.5 = bf16[1024,2688]{1,0:T(8,128)(2,1)S(1)} fusion(bf16[1792,2688]{1,0:T(8,128)(2,1)} %bitcast.223, f32[1792]{0:T(1024)S(1)} %get-tuple-element.126, f32[1024]{0:T(1024)S(1)} %bitcast.199, bf16[1024,896]{1,0:T(8,128)(2,1)S(1)} %bitcast.162, bf16[1024,896]{1,0:T(8,128)(2,1)S(1)} %bitcast.156), kind=kOutput, calls=%fused_computation.56 | convolution fusion | flops 9880600576 | bytes 18820096 | tf_op jit(solution)/shard_map/dot_general | solution.py:31
  351.7 8.3 collective-permute-start.8
  368.1 24.4 %collective-permute-done.7 = bf16[2,2,160,128]{3,2,1,0:T(8,128)(2,1)S(1)} collective-permute-done((bf16[2,2,160,128]{3,2,1,0:T(8,128)(2,1)S(1)}, bf16[2,2,160,128]{3,2,1,0:T(8,128)(2,1)S(1)}, u32[]{:S(2)}, u32[]{:S(2)}) %collective-permute-start.7) | collective-permute-done | bytes 163872 | tf_op jit(solution)/shard_map/ppermute | solution.py:762
  400.7 28.1 %shard_map.309.part = f32[2,512,896]{2,1,0:T(8,128)} custom-call(s32[2,512,8]{2,1,0:T(8,128)} %copy.79.ic, s32[2,8,640]{2,1,0:T(8,128)} %pad_add_fusion.ir, bf16[2,512,1152]{2,1,0:T(8,128)(2,1)} %bitcast.169, bf16[2,512,2688]{2,1,0:T(8,128)(2,1)} %bitcast.214, bf16[2,512,2688]{2,1,0:T(8,128)(2,1)} %bitcast.215, bf16[2,512,2688]{2,1,0:T(8,128)(2,1)} %bitcast.216, ...), custom_call_target="tpu_custom_call" | custom-call | flops 30000001024 | bytes 11010048 | tf_op jit(solution)/shard_map/pallas_call | solution.py:336
  431.1 16.0 %shard_map.310 = (bf16[2,512,896]{2,1,0:T(8,128)(2,1)}, bf16[2,512,896]{2,1,0:T(8,128)(2,1)}, f32[2,512,128]{2,1,0:T(8,128)}) custom-call(s32[2,512,8]{2,1,0:T(8,128)} %copy.79.ic, s32[2,8,640]{2,1,0:T(8,128)} %pad_add_fusion.ir, bf16[2,512,1152]{2,1,0:T(8,128)(2,1)} %bitcast.170, f32[2,512,896]{2,1,0:T(8,128)} %shard_map.309.part, ...), custom_call_target="tpu_custom_call" | custom-call | flops 20000000000 | bytes 12582912 | tf_op jit(solution)/shard_map/pallas_call | solution.py:336
  454.3 8.5 collective-permute-done.13
  473.1 11.8 convolution_convert_fusion.4
  485.0 14.2 %convolution_convert_fusion.3 = bf16[1024,2432]{1,0:T(8,128)(2,1)S(1)} fusion(bf16[1024,1792]{1,0:T(8,128)(2,1)} %copy-done.18, bf16[1792,2432]{1,0:T(8,128)(2,1)} %all-gather.3.cloned.1.call-done), kind=kOutput, calls=%fused_computation.54 | convolution fusion | flops 8927969280 | bytes 17367040 | tf_op jit(solution)/shard_map/dot_general | solution.py:31
  501.4 12.9 %convolution_convert_fusion = bf16[1792,2432]{1,0:T(8,128)(2,1)} fusion(bf16[1024,1792]{1,0:T(8,128)(2,1)S(1)} %bitcast.174, bf16[1024,2432]{1,0:T(8,128)(2,1)S(1)} %convolution_convert_fusion.3, bf16[1024,2432]{1,0:T(8,128)(2,1)S(1)} %copy-done.73), kind=kOutput, calls=%fused_computation.6 | convolution fusion | flops 8949760000 | bytes 22347776 | tf_op jit(solution)/shard_map/dot_general | solution.py:39
  520.1 18.2 %all-gather.5.cloned.1.call-done = bf16[1792,2432]{1,0:T(8,128)(2,1)} async-done(((bf16[112,2432]{1,0:T(8,128)(2,1)}), bf16[1792,2432]{1,0:T(8,128)(2,1)}) %all-gather.5.cloned.1.call-update) | async-done | bytes 8716304 | tf_op jit(solution)/shard_map/all_gather | solution.py:917
  538.3 16.8 %convolution_convert_fusion.6 = bf16[1024,1792]{1,0:T(8,128)(2,1)S(1)} fusion(bf16[1792,2432]{1,0:T(8,128)(2,1)} %all-gather.5.cloned.1.call-done, bf16[1024,2432]{1,0:T(8,128)(2,1)} %copy-done.74, bf16[1024,2432]{1,0:T(8,128)(2,1)} %convolution_convert_fusion.4), kind=kOutput, calls=%fused_computation.59 | convolution fusion | flops 8947236864 | bytes 22347776 | tf_op jit(solution)/shard_map/dot_general | solution.py:35
  556.7 18.8 %multiply_convert_fusion = (bf16[1024,2432]{1,0:T(8,128)(2,1)}, bf16[1024,2432]{1,0:T(8,128)(2,1)}) fusion(bf16[1024,2432]{1,0:T(8,128)(2,1)} %convolution_convert_fusion.4, bf16[1024,2432]{1,0:T(8,128)(2,1)} %copy-done.74, bf16[1024,1792]{1,0:T(8,128)(2,1)S(1)} %bitcast.175, bf16[1792,2432]{1,0:T(8,128)(2,1)} %all-gather.5.cloned.1.call-done), kind=kOutput, calls=%fused_computation.17 | convolution fusion | flops 8962834432 | bytes 32309248 | tf_op jit(solution)/shard_map/dot_general | solution.py:31
  575.6 16.1 %fusion.64 = f32[1024,1792]{1,0:T(8,128)} fusion(bf16[1024,2432]{1,0:T(8,128)(2,1)} %get-tuple-element.165, bf16[1792,2432]{1,0:T(8,128)(2,1)} %bitcast.225), kind=kOutput, calls=%fused_computation.300 | convolution fusion | flops 8925478912 | bytes 21037056 | tf_op jit(solution)/shard_map/dot_general | solution.py:35
  591.7 15.7 %add_convert_fusion = bf16[1024,1792]{1,0:T(8,128)(2,1)} fusion(f32[1024,1792]{1,0:T(8,128)} %fusion.64, bf16[1024,2432]{1,0:T(8,128)(2,1)S(1)} %copy-done.75, bf16[1792,2432]{1,0:T(8,128)(2,1)} %all-gather.3.cloned.1.call-done), kind=kOutput, calls=%fused_computation.46 | convolution fusion | flops 8929148928 | bytes 24707072 | tf_op jit(solution)/shard_map/dot_general | solution.py:35
  607.6 14.6 %convolution_convert_fusion.1 = bf16[1792,2432]{1,0:T(8,128)(2,1)} fusion(bf16[1024,1792]{1,0:T(8,128)(2,1)S(1)} %copy-done.19, bf16[1024,2432]{1,0:T(8,128)(2,1)} %get-tuple-element.165), kind=kOutput, calls=%fused_computation.7 | convolution fusion | flops 8929837056 | bytes 17367040 | tf_op jit(solution)/shard_map/dot_general | solution.py:39
  622.3 15.2 %convolution_convert_fusion.2 = bf16[1792,2432]{1,0:T(8,128)(2,1)} fusion(bf16[1024,1792]{1,0:T(8,128)(2,1)} %copy-done.18, bf16[1024,2432]{1,0:T(8,128)(2,1)} %get-tuple-element.164), kind=kOutput, calls=%fused_computation.8 | convolution fusion | flops 8929837056 | bytes 17367040 | tf_op jit(solution)/shard_map/dot_general | solution.py:39
  660.3 13.2 %multiply_reduce_fusion.1 = (f32[1792]{0:T(1024)S(1)}, f32[1792]{0:T(1024)S(1)}, f32[1792]{0:T(1024)S(1)}, f32[2,512,1792]{2,1,0:T(8,128)}, f32[2,512,1792]{2,1,0:T(8,128)}, /*index=5*/f32[2,512,1792]{2,1,0:T(8,128)}) fusion(f32[2,512]{1,0:T(2,128)S(1)} %bitcast.210, bf16[2,512,1792]{2,1,0:T(8,128)(2,1)S(1)} %copy-done.9, ...), kind=kOutput, calls=%fused_computation.35 | convolution fusion | flops 3330534144 | bytes 32629760 | tf_op jit(solution)/shard_map/dot_general | solution.py:35
  680.9 14.5 %shard_map.311 = bf16[2,8,160,128]{3,2,1,0:T(8,128)(2,1)} custom-call(s32[2,512,8]{2,1,0:T(8,128)} %copy.79.ic, bf16[2,512,1152]{2,1,0:T(8,128)(2,1)} %bitcast.171, bf16[2,512,896]{2,1,0:T(8,128)(2,1)} %bitcast.181, bf16[2,512,896]{2,1,0:T(8,128)(2,1)} %get-tuple-element.44.linear, f32[2,512,128]{2,1,0:T(8,128)} %get-tuple-element.45.rden, ...), custom_call_target="tpu_custom_call" | custom-call | flops 1000000000 | bytes 1966080 | tf_op jit(solution)/shard_map/pallas_call | solution.py:336
  703.8 9.1 bitcast_convert_fusion.1.rest_2_
  712.9 22.5 %collective-permute-done.16 = bf16[2,8,160,128]{3,2,1,0:T(8,128)(2,1)S(1)} collective-permute-done((bf16[2,8,160,128]{3,2,1,0:T(8,128)(2,1)}, bf16[2,8,160,128]{3,2,1,0:T(8,128)(2,1)S(1)}, u32[]{:S(2)}, u32[]{:S(2)}) %collective-permute-start.16) | collective-permute-done | bytes 655392 | tf_op jit(solution)/shard_map/ppermute | solution.py:762
  742.9 13.4 %collective-permute-done.17 = bf16[2,8,160,128]{3,2,1,0:T(8,128)(2,1)S(1)} collective-permute-done((bf16[2,8,160,128]{3,2,1,0:T(8,128)(2,1)S(1)}, bf16[2,8,160,128]{3,2,1,0:T(8,128)(2,1)S(1)}, u32[]{:S(2)}, u32[]{:S(2)}) %collective-permute-start.17) | collective-permute-done | bytes 655392 | tf_op jit(solution)/shard_map/ppermute | solution.py:762
  756.7 8.2 collective-permute-start.19
  766.8 70.9 %shard_map.312 = (bf16[2,512,128]{2,1,0:T(8,128)(2,1)}, f32[2,512,128]{2,1,0:T(8,128)}, f32[2,512,896]{2,1,0:T(8,128)}, bf16[2,512,896]{2,1,0:T(8,128)(2,1)}, f3...) custom-call(s32[2,512,8]{2,1,0:T(8,128)} %copy.79.ic, ...), custom_call_target="tpu_custom_call" | custom-call | flops 80000000000 | bytes 31260672 | tf_op jit(solution)/shard_map/pallas_call | solution.py:336
  853.4 8.5 collective-permute-done.22.back_v
  862.6 14.5 %shard_map.313 = (bf16[2,512,1152]{2,1,0:T(8,128)(2,1)}, bf16[2,512,2688]{2,1,0:T(8,128)(2,1)}) custom-call(s32[2,512,8]{2,1,0:T(8,128)} %copy.79.ic, bf16[2,512,1152]{2,1,0:T(8,128)(2,1)} %bitcast.173, bf16[2,8,160,128]{3,2,1,0:T(8,128)(2,1)} %fusion.40.d_own, bf16[8,128,160]{2,1,0:T(8,128)(2,1)} %constant.312.clone.left, ...), custom_call_target="tpu_custom_call" | custom-call | flops 2000000000 | bytes 23592960 | tf_op jit(solution)/shard_map/pallas_call | solution.py:336
  877.1 10.8 fusion.65
  887.9 19.9 %fusion.17 = bf16[1024,1792]{1,0:T(8,128)(2,1)} fusion(f32[1024,1792]{1,0:T(8,128)} %fusion.65, f32[2,512,1792]{2,1,0:T(8,128)} %convert_add_fusion.1, bf16[1024,2688]{1,0:T(8,128)(2,1)} %bitcast.229, bf16[1792,2688]{1,0:T(8,128)(2,1)} %bitcast.224), kind=kOutput, calls=%fused_computation.33 | convolution fusion | flops 9870508032 | bytes 33488896 | tf_op jit(solution)/shard_map/dot_general | solution.py:35
  920.9 13.3 %bitcast_convert_fusion = bf16[1792,2688]{1,0:T(8,128)(2,1)} fusion(bf16[2,512,1792]{2,1,0:T(8,128)(2,1)S(1)} %copy-done.10, bf16[2,512,2688]{2,1,0:T(8,128)(2,1)S(1)} %bitcast.231), kind=kOutput, calls=%fused_computation | convolution fusion | flops 9869819904 | bytes 18808832 | tf_op jit(solution)/shard_map/dot_general | solution.py:39
  951.3 258.5 %shard_map.314 = f32[112,8192]{1,0:T(8,128)} custom-call(bf16[4,2,2,112,2432]{4,3,2,1,0:T(8,128)(2,1)} %bitcast.177, bf16[4,2,2,112,896]{4,3,2,1,0:T(8,128)(2,1)} %bitcast.186, bf16[4,2,2,112,896]{4,3,2,1,0:T(8,128)(2,1)} %bitcast.187, bf16[4,2,2,112,2688]{4,3,2,1,0:T(8,128)(2,1)} %bitcast.176, bf16[4,2,2,112,1152]{4,3,2,1,0:T(8,128)(2,1)} %bitcast.184, ...), custom_call_target="tpu_custom_call" | custom-call | bytes 293601280 | tf_op jit(solution)/shard_map/pallas_call | solution.py:733
  (383 shorter events, 189.2 us)
Async XLA Ops:
  7.2 264.1 %copy-start.23 = (bf16[2,512,896]{2,1,0:T(8,128)(2,1)S(1)}, bf16[2,512,896]{2,1,0:T(8,128)(2,1)}, u32[]{:S(2)}) copy-start(bf16[2,512,896]{2,1,0:T(8,128)(2,1)} %param.20) | copy-start | bytes 5505028
  7.2 265.1 %copy-start.64 = (s32[2,4]{1,0:T(2,128)S(1)}, s32[2,4]{1,0:T(2,128)}, u32[]{:S(2)}) copy-start(s32[2,4]{1,0:T(2,128)} %param.22) | copy-start | bytes 100
  7.2 265.1 %copy-start.65 = (s32[2,4]{1,0:T(2,128)S(1)}, s32[2,4]{1,0:T(2,128)}, u32[]{:S(2)}) copy-start(s32[2,4]{1,0:T(2,128)} %param.23) | copy-start | bytes 100
  7.2 477.7 %all-gather.3.cloned.1.call-start = ((), (), s32[]{:S(2)}) async-start(), calls=%async_computation.2 | async-start | bytes 9261056 | tf_op jit(solution)/shard_map/all_gather | solution.py:917
  271.2 267.1 %all-gather.5.cloned.1.call-start = ((), (), s32[]{:S(2)}) async-start(), calls=%async_computation.3 | async-start | bytes 9261056 | tf_op jit(solution)/shard_map/all_gather | solution.py:917
  271.3 10.9 collective-permute-start
  272.0 674.7 %reduce-scatter.5.cloned.1.call-start = ((), (), s32[]{:S(2)}) async-start(), calls=%async_computation.5 | async-start | bytes 9261056 | tf_op jit(solution)/shard_map/reduce_scatter | solution.py:993
  300.9 31.9 %collective-permute-start.4 = (bf16[2,8,160,128]{3,2,1,0:T(8,128)(2,1)}, bf16[2,8,160,128]{3,2,1,0:T(8,128)(2,1)S(1)}, u32[]{:S(2)}, u32[]{:S(2)}) collective-permute-start(bf16[2,8,160,128]{3,2,1,0:T(8,128)(2,1)} %shard_map.308), channel_id=1, source_target_pairs={{0,2},{2,0},{4,6},{6,4},{8,10},{10,8},{12,14},{14,12},{16,18},{18,... | collective-permute-start | bytes 1966088 | tf_op jit(solution)/shard_map/ppermute | solution.py:762
  305.0 94.3 %collective-permute-start.3 = (bf16[2,64,896]{2,1,0:T(8,128)(2,1)S(1)}, bf16[2,64,896]{2,1,0:T(8,128)(2,1)S(1)}, u32[]{:S(2)}, u32[]{:S(2)}) collective-permute-start(bf16[2,64,896]{2,1,0:T(8,128)(2,1)S(1)} %slice.192), channel_id=1, source_target_pairs={{0,2},{2,4},{4,6},{6,8},{8,10},{10,12},{12,14},{14,16},{16,18},{18... | collective-permute-start | bytes 688136 | tf_op jit(solution)/shard_map/ppermute | solution.py:782
  309.3 50.8 %collective-permute-start.1 = (bf16[2,2,1792]{2,1,0:T(2,128)(2,1)S(1)}, bf16[2,2,1792]{2,1,0:T(2,128)(2,1)S(1)}, u32[]{:S(2)}, u32[]{:S(2)}) collective-permute-start(bf16[2,2,1792]{2,1,0:T(2,128)(2,1)S(1)} %slice.185), channel_id=1, source_target_pairs={{0,2},{2,4},{4,6},{6,8},{8,10},{10,12},{12,14},{14,16},{16,18},{18... | collective-permute-start | bytes 43016 | tf_op jit(solution)/shard_map/ppermute | solution.py:782
  333.0 18.3 %collective-permute-start.5 = (bf16[2,8,160,128]{3,2,1,0:T(8,128)(2,1)S(1)}, bf16[2,8,160,128]{3,2,1,0:T(8,128)(2,1)S(1)}, u32[]{:S(2)}, u32[]{:S(2)}) collective-permute-start(bf16[2,8,160,128]{3,2,1,0:T(8,128)(2,1)S(1)} %fusion.30), channel_id=1, source_target_pairs={{0,4},{2,6},{4,0},{6,2},{8,12},{10,14},{12,8},{14,10},{16,20},{18,... | collective-permute-start | bytes 1966088 | tf_op jit(solution)/shard_map/ppermute | solution.py:762
  347.2 52.1 %collective-permute-start.2 = (bf16[2,64,896]{2,1,0:T(8,128)(2,1)S(1)}, bf16[2,64,896]{2,1,0:T(8,128)(2,1)S(1)}, u32[]{:S(2)}, u32[]{:S(2)}) collective-permute-start(bf16[2,64,896]{2,1,0:T(8,128)(2,1)S(1)} %slice.191), channel_id=1, source_target_pairs={{0,2},{2,4},{4,6},{6,8},{8,10},{10,12},{12,14},{14,16},{16,18},{18... | collective-permute-start | bytes 688136 | tf_op jit(solution)/shard_map/ppermute | solution.py:782
  351.7 16.4 %collective-permute-start.8 = (bf16[2,2,160,128]{3,2,1,0:T(8,128)(2,1)S(1)}, bf16[2,2,160,128]{3,2,1,0:T(8,128)(2,1)S(1)}, u32[]{:S(2)}, u32[]{:S(2)}) collective-permute-start(bf16[2,2,160,128]{3,2,1,0:T(8,128)(2,1)S(1)} %constant_dynamic-slice_fusion.8), channel_id=1, source_target_pairs={{0,24},{2,26},{4,28},{6,30},{8,0},{10,2},{12,4},{14,6},{16,8},{18,... | collective-permute-start | bytes 491528 | tf_op jit(solution)/shard_map/ppermute | solution.py:762
  360.0 32.5 %collective-permute-start.7 = (bf16[2,2,160,128]{3,2,1,0:T(8,128)(2,1)S(1)}, bf16[2,2,160,128]{3,2,1,0:T(8,128)(2,1)S(1)}, u32[]{:S(2)}, u32[]{:S(2)}) collective-permute-start(bf16[2,2,160,128]{3,2,1,0:T(8,128)(2,1)S(1)} %constant_dynamic-slice_fusion.8), channel_id=1, source_target_pairs={{0,16},{2,18},{4,20},{6,22},{8,24},{10,26},{12,28},{14,30},{16,0},... | collective-permute-start | bytes 491528 | tf_op jit(solution)/shard_map/ppermute | solution.py:762
  360.0 32.5 %collective-permute-start.6 = (bf16[2,2,160,128]{3,2,1,0:T(8,128)(2,1)S(1)}, bf16[2,2,160,128]{3,2,1,0:T(8,128)(2,1)S(1)}, u32[]{:S(2)}, u32[]{:S(2)}) collective-permute-start(bf16[2,2,160,128]{3,2,1,0:T(8,128)(2,1)S(1)} %constant_dynamic-slice_fusion.8), channel_id=1, source_target_pairs={{0,8},{2,10},{4,12},{6,14},{8,16},{10,18},{12,20},{14,22},{16,24},... | collective-permute-start | bytes 491528 | tf_op jit(solution)/shard_map/ppermute | solution.py:762
  392.7 6.4 collective-permute-start.9
  399.2 29.6 %collective-permute-start.10 = (bf16[2,4,160,128]{3,2,1,0:T(8,128)(2,1)S(1)}, bf16[2,4,160,128]{3,2,1,0:T(8,128)(2,1)}, u32[]{:S(2)}, u32[]{:S(2)}) collective-permute-start(bf16[2,4,160,128]{3,2,1,0:T(8,128)(2,1)S(1)} %pad_maximum_fusion.5), channel_id=1, source_target_pairs={{0,4},{2,6},{4,0},{6,2},{8,12},{10,14},{12,8},{14,10},{16,20},{18,... | collective-permute-start | bytes 983048 | tf_op jit(solution)/shard_map/ppermute | solution.py:762
  453.7 11.6 collective-permute-start.11
  453.8 9.0 collective-permute-start.13
  514.4 434.9 %reduce-scatter.3.cloned.1.call-start = ((), (), s32[]{:S(2)}) async-start(), calls=%async_computation.4 | async-start | bytes 9261056 | tf_op jit(solution)/shard_map/reduce_scatter | solution.py:1008
  556.7 351.8 %collective-permute-start.12 = (bf16[1024,896]{1,0:T(8,128)(2,1)}, bf16[1024,896]{1,0:T(8,128)(2,1)}, u32[]{:S(2)}, u32[]{:S(2)}) collective-permute-start(bf16[1024,896]{1,0:T(8,128)(2,1)} %constant_dynamic-slice_fusion.7), channel_id=1, source_target_pairs={{0,1},{1,0},{2,3},{3,2},{4,5},{5,4},{6,7},{7,6},{8,9},{9,8},{10,11... | collective-permute-start | bytes 5505032 | tf_op jit(solution)/shard_map/ppermute | solution.py:766
  607.4 30.1 %collective-permute-start.14 = (bf16[1024,1792]{1,0:T(8,128)(2,1)}, bf16[1024,1792]{1,0:T(8,128)(2,1)}, u32[]{:S(2)}, u32[]{:S(2)}) collective-permute-start(bf16[1024,1792]{1,0:T(8,128)(2,1)} %add_convert_fusion), channel_id=1, source_target_pairs={{0,1},{1,0},{2,3},{3,2},{4,5},{5,4},{6,7},{7,6},{8,9},{9,8},{10,11... | collective-permute-start | bytes 11010056 | tf_op jit(solution)/shard_map/ppermute | solution.py:766
  695.5 39.9 %collective-permute-start.16 = (bf16[2,8,160,128]{3,2,1,0:T(8,128)(2,1)}, bf16[2,8,160,128]{3,2,1,0:T(8,128)(2,1)S(1)}, u32[]{:S(2)}, u32[]{:S(2)}) collective-permute-start(bf16[2,8,160,128]{3,2,1,0:T(8,128)(2,1)} %shard_map.311), channel_id=1, source_target_pairs={{0,2},{2,0},{4,6},{6,4},{8,10},{10,8},{12,14},{14,12},{16,18},{18,... | collective-permute-start | bytes 1966088 | tf_op jit(solution)/shard_map/ppermute | solution.py:762
  702.2 36.8 %collective-permute-start.15 = (bf16[2,2,1792]{2,1,0:T(2,128)(2,1)S(1)}, bf16[2,2,1792]{2,1,0:T(2,128)(2,1)S(1)}, u32[]{:S(2)}, u32[]{:S(2)}) collective-permute-start(bf16[2,2,1792]{2,1,0:T(2,128)(2,1)S(1)} %fusion.48), channel_id=1, source_target_pairs={{2,0},{4,2},{6,4},{8,6},{10,8},{12,10},{14,12},{16,14},{18,16},{20... | collective-permute-start | bytes 43016 | tf_op jit(solution)/shard_map/ppermute | solution.py:782
  735.8 20.5 %collective-permute-start.17 = (bf16[2,8,160,128]{3,2,1,0:T(8,128)(2,1)S(1)}, bf16[2,8,160,128]{3,2,1,0:T(8,128)(2,1)S(1)}, u32[]{:S(2)}, u32[]{:S(2)}) collective-permute-start(bf16[2,8,160,128]{3,2,1,0:T(8,128)(2,1)S(1)} %fusion.42), channel_id=1, source_target_pairs={{0,4},{2,6},{4,0},{6,2},{8,12},{10,14},{12,8},{14,10},{16,20},{18,... | collective-permute-start | bytes 1966088 | tf_op jit(solution)/shard_map/ppermute | solution.py:762
  756.6 82.4 %collective-permute-start.20 = (bf16[2,8,160,128]{3,2,1,0:T(8,128)(2,1)S(1)}, bf16[2,8,160,128]{3,2,1,0:T(8,128)(2,1)S(1)}, u32[]{:S(2)}, u32[]{:S(2)}) collective-permute-start(bf16[2,8,160,128]{3,2,1,0:T(8,128)(2,1)S(1)} %fusion.44.rest_0_), channel_id=1, source_target_pairs={{0,24},{2,26},{4,28},{6,30},{8,0},{10,2},{12,4},{14,6},{16,8},{18,... | collective-permute-start | bytes 1966088 | tf_op jit(solution)/shard_map/ppermute | solution.py:762
  756.7 90.2 %collective-permute-start.19 = (bf16[2,8,160,128]{3,2,1,0:T(8,128)(2,1)S(1)}, bf16[2,8,160,128]{3,2,1,0:T(8,128)(2,1)S(1)}, u32[]{:S(2)}, u32[]{:S(2)}) collective-permute-start(bf16[2,8,160,128]{3,2,1,0:T(8,128)(2,1)S(1)} %fusion.44.rest_0_), channel_id=1, source_target_pairs={{0,16},{2,18},{4,20},{6,22},{8,24},{10,26},{12,28},{14,30},{16,0},... | collective-permute-start | bytes 1966088 | tf_op jit(solution)/shard_map/ppermute | solution.py:762
  764.9 82.0 %collective-permute-start.18 = (bf16[2,8,160,128]{3,2,1,0:T(8,128)(2,1)S(1)}, bf16[2,8,160,128]{3,2,1,0:T(8,128)(2,1)}, u32[]{:S(2)}, u32[]{:S(2)}) collective-permute-start(bf16[2,8,160,128]{3,2,1,0:T(8,128)(2,1)S(1)} %fusion.44.rest_0_), channel_id=1, source_target_pairs={{0,8},{2,10},{4,12},{6,14},{8,16},{10,18},{12,20},{14,22},{16,24},... | collective-permute-start | bytes 1966088 | tf_op jit(solution)/shard_map/ppermute | solution.py:762
  837.8 15.7 %collective-permute-start.21 = (bf16[2,64,896]{2,1,0:T(8,128)(2,1)}, bf16[2,64,896]{2,1,0:T(8,128)(2,1)S(1)}, u32[]{:S(2)}, u32[]{:S(2)}) collective-permute-start(bf16[2,64,896]{2,1,0:T(8,128)(2,1)} %get-tuple-element.51), channel_id=1, source_target_pairs={{2,0},{4,2},{6,4},{8,6},{10,8},{12,10},{14,12},{16,14},{18,16},{20... | collective-permute-start | bytes 688136 | tf_op jit(solution)/shard_map/ppermute | solution.py:782
  839.1 22.8 %collective-permute-start.22 = (bf16[2,64,896]{2,1,0:T(8,128)(2,1)}, bf16[2,64,896]{2,1,0:T(8,128)(2,1)S(1)}, u32[]{:S(2)}, u32[]{:S(2)}) collective-permute-start(bf16[2,64,896]{2,1,0:T(8,128)(2,1)} %get-tuple-element.52), channel_id=1, source_target_pairs={{2,0},{4,2},{6,4},{8,6},{10,8},{12,10},{14,12},{16,14},{18,16},{20... | collective-permute-start | bytes 688136 | tf_op jit(solution)/shard_map/ppermute | solution.py:782
  907.9 26.3 %collective-permute-start.23 = (bf16[1024,1792]{1,0:T(8,128)(2,1)}, bf16[1024,1792]{1,0:T(8,128)(2,1)S(1)}, u32[]{:S(2)}, u32[]{:S(2)}) collective-permute-start(bf16[1024,1792]{1,0:T(8,128)(2,1)} %fusion.17), channel_id=1, source_target_pairs={{0,1},{1,0},{2,3},{3,2},{4,5},{5,4},{6,7},{7,6},{8,9},{9,8},{10,11... | collective-permute-start | bytes 11010056 | tf_op jit(solution)/shard_map/ppermute | solution.py:766
  908.0 6.0 collective-permute-start.24
  (84 other events, 2582.0 us)
Sparse Core Ops, SparseCore 0:
  271.4 147.2 all-gather.2
  421.3 116.9 all-gather.4
  540.6 197.9 reduce-scatter.4
  740.8 198.1 reduce-scatter.2
